TPU v7x, 32 devices: a whole 2x2x4 slice. The times are simulated.
32 devices in a mesh: replica: 8 (over y, x, core), fsdp: 4 (over z).
Axes of the slice: x: 2, y: 2, z: 4, core: 2. Of those that a mesh axis runs over, the one named last changes fastest.
Arguments:
- tokens: bfloat16 [16384, 4096], P(('replica', 'fsdp')), may hold values from -6 to 6
- key_cotangent: bfloat16 [16384, 512], P(('replica', 'fsdp')), may hold values from -0.25 to 0.25
- key_weight: bfloat16 [32768, 512], P(('replica', 'fsdp')), may hold values from -0.09375 to 0.09375
- first_moment: float32 [32768, 512], P(('replica', 'fsdp')), may hold values from -6 to 6
- second_moment: float32 [32768, 512], P(('replica', 'fsdp')), may hold values from 0.1 to 3
- local_slab: bfloat16 [6144, 4096], P(('replica', 'fsdp')), as said below
- outer_params: float32 [768, 4096], P('fsdp', 'replica')
- outer_momentum: float32 [768, 4096], P('fsdp', 'replica'), may hold values from -3 to 3
Outputs:
- projected: bfloat16 [16384, 512], P(('replica', 'fsdp'))
- new_weight: bfloat16 [32768, 512], P(('replica', 'fsdp'))
- new_first: float32 [32768, 512], P(('replica', 'fsdp'))
- new_second: float32 [32768, 512], P(('replica', 'fsdp'))
- new_outer: float32 [768, 4096], P('fsdp', 'replica')
- new_momentum: float32 [768, 4096], P('fsdp', 'replica')
- new_local: bfloat16 [6144, 4096], P(('replica', 'fsdp'))
Inputs may be any that keep to these rules, and one draw needn't show every extreme that they name: `local_slab`: each replica's fragment equals outer_params plus a drift that the replicas partly share.
All inputs are finite; a program needn't handle non-finite values.
Results may differ from a plain program's by a relative error of at most 0.00045.
Values may be sent and summed in bfloat16 or wider, within the bound.
No kernel may reach another device: no remote copies, remote signals or barrier semaphores. Data moves between devices by JAX's collectives and lax.ppermute only.
A program may use at most 128 MiB of HBM per device.

v0:
```python
import jax
import jax.numpy as jnp
from jax import lax
from jax.sharding import PartitionSpec as P

BETA_ONE = 0.9
BETA_TWO = 0.95
INNER_RATE = 0.001
DECAY_RATE = 0.1
EPSILON = 1e-08
FIRST_FIX = 1.0 - (0.9**50) ** 2
SECOND_FIX = 1.0 - (0.95**50) ** 2
OUTER_RATE = 0.7
OUTER_MOMENTUM = 0.9
MERGE_WEIGHT = 0.5


def outer_update(outer_params, outer_momentum, summed, replicas):
    average = summed / replicas
    pseudo_grad = outer_params - average
    new_momentum = OUTER_MOMENTUM * outer_momentum + pseudo_grad
    new_outer = outer_params - OUTER_RATE * (pseudo_grad + OUTER_MOMENTUM * new_momentum)
    return (new_outer, new_momentum)


def shards(
    tokens,
    key_cotangent,
    key_weight,
    first_moment,
    second_moment,
    local_slab,
    outer_params,
    outer_momentum,
):
    columns = tokens
    projected = jnp.dot(
        columns,
        lax.all_gather(key_weight, "fsdp", axis=0, tiled=True),
        preferred_element_type=jnp.float32,
    ).astype(jnp.bfloat16)
    columns = tokens
    gradient = lax.psum_scatter(
        lax.dot_general(
            columns, key_cotangent, (((0,), (0,)), ((), ())), preferred_element_type=jnp.float32
        ),
        "fsdp",
        scatter_dimension=0,
        tiled=True,
    )
    new_first = BETA_ONE * first_moment + (1.0 - BETA_ONE) * gradient
    new_second = BETA_TWO * second_moment + (1.0 - BETA_TWO) * gradient * gradient
    weight_f = key_weight.astype(jnp.float32)
    update = (
        new_first / FIRST_FIX / (jnp.sqrt(new_second / SECOND_FIX) + EPSILON)
        + DECAY_RATE * weight_f
    )
    new_weight = (weight_f - INNER_RATE * update).astype(jnp.bfloat16)
    replicas = lax.axis_size("replica")
    column_count = outer_params.shape[1]
    slab_f = local_slab.astype(jnp.float32)
    whole_params, whole_momentum = (
        lax.all_gather(outer_params, "replica", axis=1, tiled=True),
        lax.all_gather(outer_momentum, "replica", axis=1, tiled=True),
    )
    summed = lax.psum(slab_f, "replica")
    whole_outer, whole_new_momentum = outer_update(whole_params, whole_momentum, summed, replicas)
    first_column = lax.axis_index("replica") * column_count
    new_outer = lax.dynamic_slice_in_dim(whole_outer, first_column, column_count, 1)
    new_momentum = lax.dynamic_slice_in_dim(whole_new_momentum, first_column, column_count, 1)
    new_local = (MERGE_WEIGHT * slab_f + (1.0 - MERGE_WEIGHT) * whole_outer).astype(jnp.bfloat16)
    return (projected, new_weight, new_first, new_second, new_outer, new_momentum, new_local)


def solution(mesh):
    return jax.shard_map(
        shards,
        mesh=mesh,
        in_specs=(
            P(("replica", "fsdp"), None),
            P(("replica", "fsdp"), None),
            P(("replica", "fsdp"), None),
            P(("replica", "fsdp"), None),
            P(("replica", "fsdp"), None),
            P(("replica", "fsdp"), None),
            P("fsdp", "replica"),
            P("fsdp", "replica"),
        ),
        out_specs=(
            P(("replica", "fsdp"), None),
            P(("replica", "fsdp"), None),
            P(("replica", "fsdp"), None),
            P(("replica", "fsdp"), None),
            P("fsdp", "replica"),
            P("fsdp", "replica"),
            P(("replica", "fsdp"), None),
        ),
        check_vma=False,
    )
```

profile of v0, /device:TPU:0, one launch (start us, length us, event | category | flops | bytes accessed | tf_op | source)
XLA Modules:
  0.0 342.1 jit_solution(11278539419430202498)
XLA Ops:
  7.2 0.0 copy-start
  7.2 0.0 all-gather.6.cloned.1.call-start
  7.2 0.7 all-gather.6.cloned.1.call-update
  7.9 0.0 all-gather.8.cloned.1.call-start
  8.0 0.7 all-gather.8.cloned.1.call-update
  8.7 0.0 all-gather.4.cloned.1.call-start
  8.7 0.7 all-gather.4.cloned.1.call-update
  9.4 0.0 reduce-scatter.2.cloned.1.call-start
  9.4 0.0 copy-done
  9.5 7.8 %fusion.5 = f32[4096,512]{1,0:T(8,128)} fusion(bf16[512,4096]{1,0:T(8,128)(2,1)} %param.8, bf16[512,512]{1,0:T(8,128)(2,1)S(1)} %copy-done), kind=kOutput, calls=%fused_computation.15 | convolution fusion | flops 2147483648 | bytes 13107200 | tf_op jit(solution)/shard_map/dot_general | solution.py:44
  17.2 0.0 copy-start.1
  17.2 0.0 reduce-scatter.2.cloned.1.call-update
  17.3 1.4 copy-done.1
  18.7 91.8 %all-reduce.1 = f32[192,4096]{1,0:T(8,128)} all-reduce(bf16[192,4096]{1,0:T(8,128)(2,1)S(1)} %copy-done.1), channel_id=1, replica_groups=mesh['replica'=8,'fsdp'=4] {'replica'}, use_global_device_ids=true, to_apply=%region_1.0 | all-reduce | flops 786432 | bytes 4718592 | tf_op jit(solution)/shard_map/psum | solution.py:66
  110.4 0.0 all-gather.6.cloned.1.call-done
  110.4 0.0 all-gather.8.cloned.1.call-done
  110.4 6.7 %multiply_convert_fusion = (bf16[192,4096]{1,0:T(8,128)(2,1)}, f32[192,4096]{1,0:T(8,128)S(1)}, f32[192,4096]{1,0:T(8,128)S(1)}) fusion(bf16[192,4096]{1,0:T(8,128)(2,1)S(1)} %copy-done.1, f32[192,4096]{1,0:T(8,128)} %all-gather.6.cloned.1.call-done, f32[192,4096]{1,0:T(8,128)} %all-gather.8.cloned.1.call-done, f32[192,4096]{1,0:T(8,128)} %all-reduce.1), kind=kLoop, calls=%fused_computation | loop fusion | flops 9437184 | bytes 18874368 | tf_op jit(solution)/shard_map/convert_element_type | solution.py:71
  117.1 0.9 constant_dynamic-slice_fusion
  118.1 0.0 copy-start.2
  118.1 65.6 %all-gather.4.cloned.1.call-done = bf16[4096,512]{1,0:T(8,128)(2,1)} async-done(((bf16[1024,512]{1,0:T(8,128)(2,1)}), bf16[4096,512]{1,0:T(8,128)(2,1)}) %all-gather.4.cloned.1.call-update) | async-done | bytes 4194320 | tf_op jit(solution)/shard_map/all_gather | solution.py:39
  183.7 6.6 %convolution_convert_fusion = bf16[512,512]{1,0:T(8,128)(2,1)} fusion(bf16[512,4096]{1,0:T(8,128)(2,1)} %param.8, bf16[4096,512]{1,0:T(8,128)(2,1)} %all-gather.4.cloned.1.call-done), kind=kOutput, calls=%fused_computation.12 | convolution fusion | flops 2147745792 | bytes 8912896 | tf_op jit(solution)/shard_map/dot_general | solution.py:37
  190.3 138.6 %reduce-scatter.2.cloned.1.call-done = f32[1024,512]{1,0:T(8,128)} async-done(((f32[4096,512]{1,0:T(8,128)}), f32[1024,512]{1,0:T(8,128)}) %reduce-scatter.2.cloned.1.call-update) | async-done | bytes 2097168 | tf_op jit(solution)/shard_map/reduce_scatter | solution.py:43
  328.9 0.0 copy-done.2
  328.9 6.6 %fusion.2 = (bf16[1024,512]{1,0:T(8,128)(2,1)}, f32[1024,512]{1,0:T(8,128)}, f32[1024,512]{1,0:T(8,128)}) fusion(bf16[1024,512]{1,0:T(8,128)(2,1)S(1)} %copy-done.2, f32[1024,512]{1,0:T(8,128)} %reduce-scatter.2.cloned.1.call-done, f32[1024,512]{1,0:T(8,128)} %param.11, f32[1024,512]{1,0:T(8,128)} %param.12), kind=kLoop, calls=%fused_computation.9 | loop fusion | flops 8912896 | bytes 12582912 | tf_op jit(solution)/shard_map/convert_element_type | solution.py:58
Async XLA Ops:
  7.2 2.3 copy-start
  7.2 103.2 %all-gather.6.cloned.1.call-start = ((), (), s32[]{:S(2)}) async-start(), calls=%async_computation.3 | async-start | bytes 3538944 | tf_op jit(solution)/shard_map/all_gather | solution.py:63
  7.9 102.5 %all-gather.8.cloned.1.call-start = ((), (), s32[]{:S(2)}) async-start(), calls=%async_computation.4 | async-start | bytes 3538944 | tf_op jit(solution)/shard_map/all_gather | solution.py:64
  8.7 175.0 %all-gather.4.cloned.1.call-start = ((), (), s32[]{:S(2)}) async-start(), calls=%async_computation.1 | async-start | bytes 5242880 | tf_op jit(solution)/shard_map/all_gather | solution.py:39
  9.4 319.5 %reduce-scatter.2.cloned.1.call-start = ((), (), s32[]{:S(2)}) async-start(), calls=%async_computation.2 | async-start | bytes 10485760 | tf_op jit(solution)/shard_map/reduce_scatter | solution.py:43
  17.2 1.4 copy-start.1
  118.1 210.9 %copy-start.2 = (bf16[1024,512]{1,0:T(8,128)(2,1)S(1)}, bf16[1024,512]{1,0:T(8,128)(2,1)}, u32[]{:S(2)}) copy-start(bf16[1024,512]{1,0:T(8,128)(2,1)} %param.10) | copy-start | bytes 3145732
Sparse Core Ops, SparseCore 0:
  9.9 44.5 all-gather.5
  56.4 44.8 all-gather.7
  102.9 80.7 all-gather.3
  185.9 142.9 reduce-scatter.1
where the time goes:
time: 342 us
  waiting for transfers between devices  206 us (60%)
  blocking collectives  91.8 us (27%)
  matrix products  14.4 us (4%)
  between operations  13.8 us (4%)
  other arithmetic  13.3 us (4%)
    reduce_scatter x1, waiting for transfers between devices, shards(): lax.psum_scatter(lax.dot_general(columns, key_cotangent, (((0,), (0,)), (...  139 us
    psum x1, blocking collectives, shards(): summed = lax.psum(slab_f, 'replica')  91.8 us
    all_gather x1, waiting for transfers between devices, shards(): lax.all_gather(key_weight, 'fsdp', axis=0, tiled=True)  65.6 us
    dot_general x1, matrix products, shards(): lax.dot_general(columns, key_cotangent, (((0,), (0,)), ((), ())), preferr...  7.79 us
  transfers between devices with their start and end apart: 4, of which 2 were waited for; matrix products, arithmetic and copies ran while one was open for 6% of the time, Pallas kernels for 0%

commit v1 on v0

v1 whole, which is shorter than its diff:
```python
import jax
import jax.numpy as jnp
from jax import lax
from jax.sharding import PartitionSpec as P

BETA_ONE = 0.9
BETA_TWO = 0.95
INNER_RATE = 0.001
DECAY_RATE = 0.1
EPSILON = 1e-08
FIRST_FIX = 1.0 - (0.9**50) ** 2
SECOND_FIX = 1.0 - (0.95**50) ** 2
OUTER_RATE = 0.7
OUTER_MOMENTUM = 0.9
MERGE_WEIGHT = 0.5


def term_scale(replica_tokens):
    scale = 1.0
    while replica_tokens * 6 * 0.25 * scale * 2 < 60000:
        scale *= 2
    return scale


def outer_update(outer_params, outer_momentum, summed, replicas):
    average = summed / replicas
    pseudo_grad = outer_params - average
    new_momentum = OUTER_MOMENTUM * outer_momentum + pseudo_grad
    new_outer = outer_params - OUTER_RATE * (pseudo_grad + OUTER_MOMENTUM * new_momentum)
    return (new_outer, new_momentum)


def shards(
    tokens,
    key_cotangent,
    key_weight,
    first_moment,
    second_moment,
    local_slab,
    outer_params,
    outer_momentum,
):
    n = lax.axis_size("fsdp")
    me = lax.axis_index("fsdp")
    rows = key_weight.shape[0]
    scale = term_scale(n * tokens.shape[0])

    def columns_of(owner):
        return lax.dynamic_slice_in_dim(tokens, jnp.clip(owner, 0, n - 1) * rows, rows, 1)

    def term(owner):
        return lax.dot_general(
            columns_of(owner),
            key_cotangent,
            (((0,), (0,)), ((), ())),
            preferred_element_type=jnp.float32,
        )

    def keyed(owner, weight):
        return jnp.dot(columns_of(owner), weight, preferred_element_type=jnp.float32)

    held_up, held_down = key_weight, key_weight
    total = keyed(me, key_weight)
    come_up, come_down = None, None
    for t in range(n - 1):
        up = [(i, i + 1) for i in range(t, n - 1)]
        down = [(n - 1 - a, n - 1 - b) for a, b in up]
        held_up = lax.ppermute(held_up, "fsdp", up)
        held_down = lax.ppermute(held_down, "fsdp", down)
        total = total + keyed(me - t - 1, held_up) + keyed(me + t + 1, held_down)
        send_up = term(n - 1 - t + me) * scale
        send_down = term(t - (n - 1 - me)) * scale
        if come_up is not None:
            send_up = send_up + come_up.astype(jnp.float32)
            send_down = send_down + come_down.astype(jnp.float32)
        up = [(i, i + 1) for i in range(t + 1)]
        down = [(n - 1 - a, n - 1 - b) for a, b in up]
        come_up = lax.ppermute(send_up.astype(jnp.float16), "fsdp", up)
        come_down = lax.ppermute(send_down.astype(jnp.float16), "fsdp", down)
    projected = total.astype(jnp.bfloat16)
    gradient = term(me)
    if come_up is not None:
        gradient = gradient + (come_up.astype(jnp.float32) + come_down.astype(jnp.float32)) / scale

    new_first = BETA_ONE * first_moment + (1.0 - BETA_ONE) * gradient
    new_second = BETA_TWO * second_moment + (1.0 - BETA_TWO) * gradient * gradient
    weight_f = key_weight.astype(jnp.float32)
    update = (
        new_first / FIRST_FIX / (jnp.sqrt(new_second / SECOND_FIX) + EPSILON)
        + DECAY_RATE * weight_f
    )
    new_weight = (weight_f - INNER_RATE * update).astype(jnp.bfloat16)

    replicas = lax.axis_size("replica")
    slab_rows, column_count = outer_params.shape
    parts = lax.all_to_all(
        local_slab.reshape(slab_rows, replicas, column_count), "replica", 1, 0, tiled=False
    )
    summed = jnp.sum(parts.astype(jnp.float32), axis=0)
    new_outer, new_momentum = outer_update(outer_params, outer_momentum, summed, replicas)
    whole_outer = lax.all_gather(new_outer, "replica", axis=1, tiled=True)
    slab_f = local_slab.astype(jnp.float32)
    new_local = (MERGE_WEIGHT * slab_f + (1.0 - MERGE_WEIGHT) * whole_outer).astype(jnp.bfloat16)
    return (projected, new_weight, new_first, new_second, new_outer, new_momentum, new_local)


def solution(mesh):
    split = P(("replica", "fsdp"), None)
    outer = P("fsdp", "replica")
    return jax.shard_map(
        shards,
        mesh=mesh,
        in_specs=(split, split, split, split, split, split, outer, outer),
        out_specs=(split, split, split, split, outer, outer, split),
        check_vma=False,
    )
```

time: 342 us -> 170 us (0.50)
  the two profiles are of different devices: /device:TPU:0 before, /device:TPU:26 now
where the time goes in v1:
time: 170 us
  waiting for transfers between devices  58.9 us (35%)
  starting transfers between devices  45.4 us (27%)
  matrix products  33.2 us (20%)
  between operations  14.3 us (8%)
  other arithmetic  13.7 us (8%)
  local copies, waits for them, and re-layouts  4.21 us (2%)
    ppermute x3, waiting for transfers between devices, shards(): held_up = lax.ppermute(held_up, 'fsdp', up)  38 us
    ppermute x3, starting transfers between devices, shards(): come_down = lax.ppermute(send_down.astype(jnp.float16), 'fsdp', down)  24.4 us
    dot_general x7, matrix products, term(): lax.dot_general(columns_of(owner), key_cotangent, (((0,), (0,)), ((), ())...  19.4 us
    dot_general x7, matrix products, keyed(): jnp.dot(columns_of(owner), weight, preferred_element_type=jnp.float32)  13.8 us
    all_to_all x1, waiting for transfers between devices, shards(): lax.all_to_all(local_slab.reshape(slab_rows, replicas, column_count), 're...  12.7 us
    ppermute x3, waiting for transfers between devices, shards(): come_down = lax.ppermute(send_down.astype(jnp.float16), 'fsdp', down)  8.11 us
    ppermute x3, starting transfers between devices, shards(): held_down = lax.ppermute(held_down, 'fsdp', down)  8.08 us
    convert_element_type x1, other arithmetic, shards(): new_weight = (weight_f - INNER_RATE * update).astype(jnp.bfloat16)  5.2 us
  transfers between devices with their start and end apart: 14, of which 4 were waited for; matrix products, arithmetic and copies ran while one was open for 25% of the time, Pallas kernels for 0%

profile of v1, /device:TPU:26, one launch (start us, length us, event | category | flops | bytes accessed | tf_op | source)
XLA Modules:
  0.0 169.5 jit_solution(13115176191968862027)
XLA Ops:
  7.2 0.0 copy-start
  7.2 2.1 %copy.16 = bf16[24,8,8,512]{3,2,1,0:T(8,128)(2,1)S(1)} copy(bf16[24,8,8,512]{3,1,2,0:T(8,128)(2,1)} %bitcast.18) | data formatting | bytes 3145728
  9.3 1.6 copy.15
  10.9 4.4 %all-to-all-start = ((bf16[1,192,8,512]{3,1,0,2:T(8,128)(2,1)}), bf16[1,192,8,512]{3,1,0,2:T(8,128)(2,1)S(1)}, u32[]{:S(2)}, u32[]{:S(2)}) async-start(bf16[1,192,8,512]{3,1,0,2:T(8,128)(2,1)} %copy.15), calls=%async_computation | async-start | bytes 3145728 | tf_op jit(solution)/shard_map/all_to_all | solution.py:96
  15.3 1.3 collective-permute-start
  16.6 5.6 %collective-permute-start.1 = (bf16[1024,512]{1,0:T(8,128)(2,1)}, bf16[1024,512]{1,0:T(8,128)(2,1)}, u32[]{:S(2)}, u32[]{:S(2)}) collective-permute-start(bf16[1024,512]{1,0:T(8,128)(2,1)} %param.10), channel_id=1, source_target_pairs={{3,2},{2,1},{1,0},{7,6},{6,5},{5,4},{11,10},{10,9},{9,8},{15,14},{... | collective-permute-start | bytes 3145736 | tf_op jit(solution)/shard_map/ppermute | solution.py:69
  22.2 12.7 %all-to-all-done = bf16[1,192,8,512]{3,1,0,2:T(8,128)(2,1)S(1)} async-done(((bf16[1,192,8,512]{3,1,0,2:T(8,128)(2,1)}), bf16[1,192,8,512]{3,1,0,2:T(8,128)(2,1)S(1)}, u32[]{:S(2)}, u32[]{:S(2)}) %all-to-all-start) | async-done | bytes 1572896 | tf_op jit(solution)/shard_map/all_to_all | solution.py:96
  34.9 0.2 convert_reduce_fusion
  35.1 1.0 multiply_subtract_fusion
  36.1 0.0 all-gather.2.cloned.1.call-update
  36.1 2.9 %multiply_convert_fusion.2 = f16[1024,512]{1,0:T(8,128)(2,1)} fusion(bf16[512,512]{1,0:T(8,128)(2,1)S(1)} %copy-done, bf16[512,4096]{1,0:T(8,128)(2,1)} %param.8, s32[]{:T(128)S(6)} %select_n.40), kind=kOutput, calls=%fused_computation.16 | convolution fusion | flops 537919488 | bytes 2621444 | tf_op jit(solution)/shard_map/dot_general | solution.py:52
  39.1 1.6 collective-permute-start.6
  40.7 2.9 %multiply_convert_fusion.1 = f16[1024,512]{1,0:T(8,128)(2,1)} fusion(bf16[512,512]{1,0:T(8,128)(2,1)S(1)} %copy-done, bf16[512,4096]{1,0:T(8,128)(2,1)} %param.8, s32[]{:T(128)S(6)} %select_n.43), kind=kOutput, calls=%fused_computation.13 | convolution fusion | flops 537919488 | bytes 2621444 | tf_op jit(solution)/shard_map/dot_general | solution.py:52
  43.7 3.4 %collective-permute-start.9 = (f16[1024,512]{1,0:T(8,128)(2,1)}, f16[1024,512]{1,0:T(8,128)(2,1)}, u32[]{:S(2)}, u32[]{:S(2)}) collective-permute-start(f16[1024,512]{1,0:T(8,128)(2,1)} %multiply_convert_fusion.1), channel_id=1, source_target_pairs={{3,2},{7,6},{11,10},{15,14},{19,18},{23,22},{27,26},{31,30}} | collective-permute-start | bytes 3145736 | tf_op jit(solution)/shard_map/ppermute | solution.py:79
  47.1 3.4 %fusion.20 = f32[1024,512]{1,0:T(8,128)} fusion(bf16[512,512]{1,0:T(8,128)(2,1)S(1)} %copy-done, bf16[512,4096]{1,0:T(8,128)(2,1)} %param.8, s32[]{:T(128)S(6)} %select_n.36), kind=kOutput, calls=%fused_computation.37 | convolution fusion | flops 536870912 | bytes 3670020 | tf_op jit(solution)/shard_map/dot_general | solution.py:52
  50.5 2.0 %fusion.23 = f32[1024,512]{1,0:T(8,128)S(1)} fusion(bf16[512,512]{1,0:T(8,128)(2,1)S(1)} %copy-done, bf16[512,4096]{1,0:T(8,128)(2,1)} %param.8, s32[]{:T(128)S(6)} %select_n.34), kind=kOutput, calls=%fused_computation.40 | convolution fusion | flops 536870912 | bytes 3670020 | tf_op jit(solution)/shard_map/dot_general | solution.py:52
  52.5 2.1 %fusion.9 = f32[1024,512]{1,0:T(8,128)} fusion(bf16[512,512]{1,0:T(8,128)(2,1)S(1)} %copy-done, bf16[512,4096]{1,0:T(8,128)(2,1)S(1)} %copy-done.1, s32[]{:T(128)S(6)} %select_n.41), kind=kOutput, calls=%fused_computation.26 | convolution fusion | flops 536870912 | bytes 3670020 | tf_op jit(solution)/shard_map/dot_general | solution.py:52
  54.6 3.0 %add_convert_fusion.3 = f16[1024,512]{1,0:T(8,128)(2,1)} fusion(f16[1024,512]{1,0:T(8,128)(2,1)} %collective-permute-done.6, bf16[512,512]{1,0:T(8,128)(2,1)S(1)} %copy-done, bf16[512,4096]{1,0:T(8,128)(2,1)S(1)} %copy-done.1, s32[]{:T(128)S(6)} %select_n.38), kind=kOutput, calls=%fused_computation.15 | convolution fusion | flops 538968064 | bytes 3670020 | tf_op jit(solution)/shard_map/dot_general | solution.py:52
  57.6 1.7 %collective-permute-start.7 = (f16[1024,512]{1,0:T(8,128)(2,1)}, f16[1024,512]{1,0:T(8,128)(2,1)}, u32[]{:S(2)}, u32[]{:S(2)}) collective-permute-start(f16[1024,512]{1,0:T(8,128)(2,1)} %add_convert_fusion.3), channel_id=1, source_target_pairs={{0,1},{1,2},{4,5},{5,6},{8,9},{9,10},{12,13},{13,14},{16,17},{17,1... | collective-permute-start | bytes 3145736 | tf_op jit(solution)/shard_map/ppermute | solution.py:78
  59.3 0.0 collective-permute-done.1
  59.3 1.6 collective-permute-start.3
  61.0 8.1 %collective-permute-done.9 = f16[1024,512]{1,0:T(8,128)(2,1)} collective-permute-done((f16[1024,512]{1,0:T(8,128)(2,1)}, f16[1024,512]{1,0:T(8,128)(2,1)}, u32[]{:S(2)}, u32[]{:S(2)}) %collective-permute-start.9) | collective-permute-done | bytes 1048608 | tf_op jit(solution)/shard_map/ppermute | solution.py:79
  69.1 3.0 %add_convert_fusion.1 = f16[1024,512]{1,0:T(8,128)(2,1)} fusion(f16[1024,512]{1,0:T(8,128)(2,1)} %collective-permute-done.9, bf16[512,512]{1,0:T(8,128)(2,1)S(1)} %copy-done, bf16[512,4096]{1,0:T(8,128)(2,1)S(1)} %copy-done.1, s32[]{:T(128)S(6)} %select_n.42), kind=kOutput, calls=%fused_computation.12 | convolution fusion | flops 538968064 | bytes 3670020 | tf_op jit(solution)/shard_map/dot_general | solution.py:52
  72.1 9.1 %collective-permute-start.10 = (f16[1024,512]{1,0:T(8,128)(2,1)}, f16[1024,512]{1,0:T(8,128)(2,1)}, u32[]{:S(2)}, u32[]{:S(2)}) collective-permute-start(f16[1024,512]{1,0:T(8,128)(2,1)} %add_convert_fusion.1), channel_id=1, source_target_pairs={{3,2},{2,1},{7,6},{6,5},{11,10},{10,9},{15,14},{14,13},{19,18},{18... | collective-permute-start | bytes 3145736 | tf_op jit(solution)/shard_map/ppermute | solution.py:79
  81.2 0.0 collective-permute-done
  81.2 1.3 collective-permute-start.2
  82.5 2.9 %fusion.25 = f32[512,512]{1,0:T(8,128)} fusion(bf16[1024,512]{1,0:T(8,128)(2,1)} %param.10, bf16[512,4096]{1,0:T(8,128)(2,1)S(1)} %copy-done.1, s32[]{:T(128)S(6)} %select_n.34), kind=kOutput, calls=%fused_computation.42 | convolution fusion | flops 536870912 | bytes 3145732 | tf_op jit(solution)/shard_map/dot_general | solution.py:60
  85.4 2.7 %convolution_add_fusion.3 = f32[512,512]{1,0:T(8,128)S(1)} fusion(f32[512,512]{1,0:T(8,128)} %fusion.25, bf16[1024,512]{1,0:T(8,128)(2,1)} %collective-permute-done, bf16[512,4096]{1,0:T(8,128)(2,1)} %param.8, s32[]{:T(128)S(6)} %select_n.35), kind=kOutput, calls=%fused_computation.22 | convolution fusion | flops 537133056 | bytes 4194308 | tf_op jit(solution)/shard_map/dot_general | solution.py:60
  88.1 0.4 copy-done.2
  88.5 2.1 %convolution_add_fusion.2 = f32[512,512]{1,0:T(8,128)S(1)} fusion(f32[512,512]{1,0:T(8,128)S(1)} %convolution_add_fusion.3, bf16[1024,512]{1,0:T(8,128)(2,1)} %collective-permute-done.1, bf16[512,4096]{1,0:T(8,128)(2,1)S(1)} %copy-done.2, s32[]{:T(128)S(6)} %select_n.36), kind=kOutput, calls=%fused_computation.21 | convolution fusion | flops 537133056 | bytes 4194308 | tf_op jit(solution)/shard_map/dot_general | solution.py:60
  90.6 0.0 copy-start.3
  90.6 0.0 collective-permute-done.3
  90.6 0.9 collective-permute-start.5
  91.5 1.6 add_convert_fusion.2
  93.2 1.3 collective-permute-start.8
  94.5 15.0 %collective-permute-done.2 = bf16[1024,512]{1,0:T(8,128)(2,1)} collective-permute-done((bf16[1024,512]{1,0:T(8,128)(2,1)}, bf16[1024,512]{1,0:T(8,128)(2,1)}, u32[]{:S(2)}, u32[]{:S(2)}) %collective-permute-start.2) | collective-permute-done | bytes 1048608 | tf_op jit(solution)/shard_map/ppermute | solution.py:68
  109.5 1.3 collective-permute-start.4
  110.8 1.6 add_convert_fusion
  112.4 11.9 %collective-permute-start.11 = (f16[1024,512]{1,0:T(8,128)(2,1)S(1)}, f16[1024,512]{1,0:T(8,128)(2,1)S(1)}, u32[]{:S(2)}, u32[]{:S(2)}) collective-permute-start(f16[1024,512]{1,0:T(8,128)(2,1)S(1)} %add_convert_fusion), channel_id=1, source_target_pairs={{3,2},{2,1},{1,0},{7,6},{6,5},{5,4},{11,10},{10,9},{9,8},{15,14},{... | collective-permute-start | bytes 3145736 | tf_op jit(solution)/shard_map/ppermute | solution.py:79
  124.4 1.9 %fusion.18 = f32[512,512]{1,0:T(8,128)S(1)} fusion(bf16[1024,512]{1,0:T(8,128)(2,1)} %collective-permute-done.3, bf16[512,4096]{1,0:T(8,128)(2,1)S(1)} %copy-done.2, s32[]{:T(128)S(6)} %select_n.38), kind=kOutput, calls=%fused_computation.35 | convolution fusion | flops 536870912 | bytes 3145732 | tf_op jit(solution)/shard_map/dot_general | solution.py:60
  126.3 1.9 %fusion.5 = f32[512,512]{1,0:T(8,128)S(1)} fusion(f32[512,512]{1,0:T(8,128)S(1)} %fusion.18, f32[512,512]{1,0:T(8,128)S(1)} %convolution_add_fusion.2, bf16[1024,512]{1,0:T(8,128)(2,1)} %collective-permute-done.2, bf16[512,4096]{1,0:T(8,128)(2,1)S(1)} %copy-done.2, s32[]{:T(128)S(6)} %select_n.37), kind=kOutput, calls=%fused_computation.20 | convolution fusion | flops 537395200 | bytes 5242884 | tf_op jit(solution)/shard_map/dot_general | solution.py:60
  128.3 0.7 fusion.15
  129.0 0.0 copy-start.5
  129.0 0.0 copy-start.6
  129.0 23.0 %collective-permute-done.4 = bf16[1024,512]{1,0:T(8,128)(2,1)S(1)} collective-permute-done((bf16[1024,512]{1,0:T(8,128)(2,1)}, bf16[1024,512]{1,0:T(8,128)(2,1)S(1)}, u32[]{:S(2)}, u32[]{:S(2)}) %collective-permute-start.4) | collective-permute-done | bytes 1048608 | tf_op jit(solution)/shard_map/ppermute | solution.py:68
  152.0 1.5 fusion.6
  153.6 5.2 %fusion.2 = (bf16[1024,512]{1,0:T(8,128)(2,1)}, f32[1024,512]{1,0:T(8,128)}, f32[1024,512]{1,0:T(8,128)}) fusion(bf16[1024,512]{1,0:T(8,128)(2,1)} %param.10, f32[1024,512]{1,0:T(8,128)S(1)} %fusion.23, f16[1024,512]{1,0:T(8,128)(2,1)S(1)} %collective-permute-done.11, f16[1024,512]{1,0:T(8,128)(2,1)S(1)} %collective-permute-done.8, ...), kind=kLoop, calls=%fused_computation.7 | loop fusion | flops 11534336 | bytes 14680064 | tf_op jit(solution)/shard_map/convert_element_type | solution.py:92
  158.8 3.9 %multiply_convert_fusion = bf16[192,4096]{1,0:T(8,128)(2,1)} fusion(f32[192,4096]{1,0:T(8,128)} %all-gather.2.cloned.1.call-done, bf16[192,4096]{1,0:T(8,128)(2,1)} %param.13), kind=kLoop, calls=%fused_computation | loop fusion | flops 3145728 | bytes 6291456 | tf_op jit(solution)/shard_map/convert_element_type | solution.py:103
  (21 shorter events, 0.0 us)
Async XLA Ops:
  7.2 29.0 %copy-start = (bf16[512,512]{1,0:T(8,128)(2,1)S(1)}, bf16[512,512]{1,0:T(8,128)(2,1)}, u32[]{:S(2)}) copy-start(bf16[512,512]{1,0:T(8,128)(2,1)} %param.9) | copy-start | bytes 1572868
  10.9 24.1 %copy-start.7 = (f32[192,512]{1,0:T(8,128)S(1)}, f32[192,512]{1,0:T(8,128)}, u32[]{:S(2)}) copy-start(f32[192,512]{1,0:T(8,128)} %param.14) | copy-start | bytes 1179652
  10.9 24.1 %copy-start.8 = (f32[192,512]{1,0:T(8,128)S(1)}, f32[192,512]{1,0:T(8,128)}, u32[]{:S(2)}) copy-start(f32[192,512]{1,0:T(8,128)} %param.15) | copy-start | bytes 1179652
  10.9 23.9 %all-to-all-start = ((bf16[1,192,8,512]{3,1,0,2:T(8,128)(2,1)}), bf16[1,192,8,512]{3,1,0,2:T(8,128)(2,1)S(1)}, u32[]{:S(2)}, u32[]{:S(2)}) async-start(bf16[1,192,8,512]{3,1,0,2:T(8,128)(2,1)} %copy.15), calls=%async_computation | async-start | bytes 3145728 | tf_op jit(solution)/shard_map/all_to_all | solution.py:96
  15.3 143.4 %all-gather.2.cloned.1.call-start = ((), (), s32[]{:S(2)}) async-start(), calls=%async_computation.1 | async-start | bytes 3538944 | tf_op jit(solution)/shard_map/all_gather | solution.py:101
  15.3 65.8 %collective-permute-start = (bf16[1024,512]{1,0:T(8,128)(2,1)}, bf16[1024,512]{1,0:T(8,128)(2,1)}, u32[]{:S(2)}, u32[]{:S(2)}) collective-permute-start(bf16[1024,512]{1,0:T(8,128)(2,1)} %param.10), channel_id=1, source_target_pairs={{0,1},{1,2},{2,3},{4,5},{5,6},{6,7},{8,9},{9,10},{10,11},{12,13},{... | collective-permute-start | bytes 3145736 | tf_op jit(solution)/shard_map/ppermute | solution.py:68
  16.6 42.7 %collective-permute-start.1 = (bf16[1024,512]{1,0:T(8,128)(2,1)}, bf16[1024,512]{1,0:T(8,128)(2,1)}, u32[]{:S(2)}, u32[]{:S(2)}) collective-permute-start(bf16[1024,512]{1,0:T(8,128)(2,1)} %param.10), channel_id=1, source_target_pairs={{3,2},{2,1},{1,0},{7,6},{6,5},{5,4},{11,10},{10,9},{9,8},{15,14},{... | collective-permute-start | bytes 3145736 | tf_op jit(solution)/shard_map/ppermute | solution.py:69
  39.1 15.5 %collective-permute-start.6 = (f16[1024,512]{1,0:T(8,128)(2,1)}, f16[1024,512]{1,0:T(8,128)(2,1)}, u32[]{:S(2)}, u32[]{:S(2)}) collective-permute-start(f16[1024,512]{1,0:T(8,128)(2,1)} %multiply_convert_fusion.2), channel_id=1, source_target_pairs={{0,1},{4,5},{8,9},{12,13},{16,17},{20,21},{24,25},{28,29}} | collective-permute-start | bytes 3145736 | tf_op jit(solution)/shard_map/ppermute | solution.py:78
  43.7 25.4 %collective-permute-start.9 = (f16[1024,512]{1,0:T(8,128)(2,1)}, f16[1024,512]{1,0:T(8,128)(2,1)}, u32[]{:S(2)}, u32[]{:S(2)}) collective-permute-start(f16[1024,512]{1,0:T(8,128)(2,1)} %multiply_convert_fusion.1), channel_id=1, source_target_pairs={{3,2},{7,6},{11,10},{15,14},{19,18},{23,22},{27,26},{31,30}} | collective-permute-start | bytes 3145736 | tf_op jit(solution)/shard_map/ppermute | solution.py:79
  47.1 5.4 %copy-start.1 = (bf16[512,4096]{1,0:T(8,128)(2,1)S(1)}, bf16[512,4096]{1,0:T(8,128)(2,1)}, u32[]{:S(2)}) copy-start(bf16[512,4096]{1,0:T(8,128)(2,1)} %param.8) | copy-start | bytes 12582916
  57.6 33.9 %collective-permute-start.7 = (f16[1024,512]{1,0:T(8,128)(2,1)}, f16[1024,512]{1,0:T(8,128)(2,1)}, u32[]{:S(2)}, u32[]{:S(2)}) collective-permute-start(f16[1024,512]{1,0:T(8,128)(2,1)} %add_convert_fusion.3), channel_id=1, source_target_pairs={{0,1},{1,2},{4,5},{5,6},{8,9},{9,10},{12,13},{13,14},{16,17},{17,1... | collective-permute-start | bytes 3145736 | tf_op jit(solution)/shard_map/ppermute | solution.py:78
  59.3 31.3 %collective-permute-start.3 = (bf16[1024,512]{1,0:T(8,128)(2,1)}, bf16[1024,512]{1,0:T(8,128)(2,1)}, u32[]{:S(2)}, u32[]{:S(2)}) collective-permute-start(bf16[1024,512]{1,0:T(8,128)(2,1)} %collective-permute-done.1), channel_id=1, source_target_pairs={{2,1},{1,0},{6,5},{5,4},{10,9},{9,8},{14,13},{13,12},{18,17},{17,1... | collective-permute-start | bytes 3145736 | tf_op jit(solution)/shard_map/ppermute | solution.py:69
  72.1 38.7 %collective-permute-start.10 = (f16[1024,512]{1,0:T(8,128)(2,1)}, f16[1024,512]{1,0:T(8,128)(2,1)}, u32[]{:S(2)}, u32[]{:S(2)}) collective-permute-start(f16[1024,512]{1,0:T(8,128)(2,1)} %add_convert_fusion.1), channel_id=1, source_target_pairs={{3,2},{2,1},{7,6},{6,5},{11,10},{10,9},{15,14},{14,13},{19,18},{18... | collective-permute-start | bytes 3145736 | tf_op jit(solution)/shard_map/ppermute | solution.py:79
  81.2 28.3 %collective-permute-start.2 = (bf16[1024,512]{1,0:T(8,128)(2,1)}, bf16[1024,512]{1,0:T(8,128)(2,1)}, u32[]{:S(2)}, u32[]{:S(2)}) collective-permute-start(bf16[1024,512]{1,0:T(8,128)(2,1)} %collective-permute-done), channel_id=1, source_target_pairs={{1,2},{2,3},{5,6},{6,7},{9,10},{10,11},{13,14},{14,15},{17,18},{18... | collective-permute-start | bytes 3145736 | tf_op jit(solution)/shard_map/ppermute | solution.py:68
  85.4 3.1 %copy-start.2 = (bf16[512,4096]{1,0:T(8,128)(2,1)S(1)}, bf16[512,4096]{1,0:T(8,128)(2,1)}, u32[]{:S(2)}) copy-start(bf16[512,4096]{1,0:T(8,128)(2,1)} %param.8) | copy-start | bytes 12582916
  88.5 3.0 %copy-start.4 = (f32[1024,512]{1,0:T(8,128)S(1)}, f32[1024,512]{1,0:T(8,128)}, u32[]{:S(2)}) copy-start(f32[1024,512]{1,0:T(8,128)} %fusion.20) | copy-start | bytes 6291460
  90.6 20.2 %copy-start.3 = (f32[1024,512]{1,0:T(8,128)S(1)}, f32[1024,512]{1,0:T(8,128)}, u32[]{:S(2)}) copy-start(f32[1024,512]{1,0:T(8,128)} %fusion.9) | copy-start | bytes 6291460
  90.6 37.6 %collective-permute-start.5 = (bf16[1024,512]{1,0:T(8,128)(2,1)}, bf16[1024,512]{1,0:T(8,128)(2,1)S(1)}, u32[]{:S(2)}, u32[]{:S(2)}) collective-permute-start(bf16[1024,512]{1,0:T(8,128)(2,1)} %collective-permute-done.3), channel_id=1, source_target_pairs={{1,0},{5,4},{9,8},{13,12},{17,16},{21,20},{25,24},{29,28}} | collective-permute-start | bytes 3145736 | tf_op jit(solution)/shard_map/ppermute | solution.py:69
  93.2 60.4 %collective-permute-start.8 = (f16[1024,512]{1,0:T(8,128)(2,1)S(1)}, f16[1024,512]{1,0:T(8,128)(2,1)S(1)}, u32[]{:S(2)}, u32[]{:S(2)}) collective-permute-start(f16[1024,512]{1,0:T(8,128)(2,1)S(1)} %add_convert_fusion.2), channel_id=1, source_target_pairs={{0,1},{1,2},{2,3},{4,5},{5,6},{6,7},{8,9},{9,10},{10,11},{12,13},{... | collective-permute-start | bytes 3145736 | tf_op jit(solution)/shard_map/ppermute | solution.py:78
  109.5 42.6 %collective-permute-start.4 = (bf16[1024,512]{1,0:T(8,128)(2,1)}, bf16[1024,512]{1,0:T(8,128)(2,1)S(1)}, u32[]{:S(2)}, u32[]{:S(2)}) collective-permute-start(bf16[1024,512]{1,0:T(8,128)(2,1)} %collective-permute-done.2), channel_id=1, source_target_pairs={{2,3},{6,7},{10,11},{14,15},{18,19},{22,23},{26,27},{30,31}} | collective-permute-start | bytes 3145736 | tf_op jit(solution)/shard_map/ppermute | solution.py:68
  112.4 41.1 %collective-permute-start.11 = (f16[1024,512]{1,0:T(8,128)(2,1)S(1)}, f16[1024,512]{1,0:T(8,128)(2,1)S(1)}, u32[]{:S(2)}, u32[]{:S(2)}) collective-permute-start(f16[1024,512]{1,0:T(8,128)(2,1)S(1)} %add_convert_fusion), channel_id=1, source_target_pairs={{3,2},{2,1},{1,0},{7,6},{6,5},{5,4},{11,10},{10,9},{9,8},{15,14},{... | collective-permute-start | bytes 3145736 | tf_op jit(solution)/shard_map/ppermute | solution.py:79
  129.0 24.6 %copy-start.5 = (f32[1024,512]{1,0:T(8,128)S(1)}, f32[1024,512]{1,0:T(8,128)}, u32[]{:S(2)}) copy-start(f32[1024,512]{1,0:T(8,128)} %param.11) | copy-start | bytes 6291460
  129.0 24.6 %copy-start.6 = (f32[1024,512]{1,0:T(8,128)S(1)}, f32[1024,512]{1,0:T(8,128)}, u32[]{:S(2)}) copy-start(f32[1024,512]{1,0:T(8,128)} %param.12) | copy-start | bytes 6291460
Sparse Core Ops, SparseCore 0:
  36.3 32.3 all-gather.1

commit v2 on v1

v2 whole, which is shorter than its diff:
```python
import functools

import jax
import jax.numpy as jnp
from jax import lax
from jax.experimental import pallas as pl
from jax.experimental.pallas import tpu as pltpu
from jax.sharding import PartitionSpec as P

BETA_ONE = 0.9
BETA_TWO = 0.95
INNER_RATE = 0.001
DECAY_RATE = 0.1
EPSILON = 1e-08
FIRST_FIX = 1.0 - (0.9**50) ** 2
SECOND_FIX = 1.0 - (0.95**50) ** 2
OUTER_RATE = 0.7
OUTER_MOMENTUM = 0.9
MERGE_WEIGHT = 0.5
PIECES = 2
WEIGHT_PIECES = 1
TUNE = {'vmem': 60, 'columns': 40000000000, 'outer_after': (3, 0), ('x', 2, 0): 10, ('x', 2, 1): 10, ('x', 3, 0): 10, ('x', 3, 1): 10}
VM = TUNE.get('vmem', 60)
ANY = pl.BlockSpec(memory_space=pl.ANY)
MIB = 1 << 20


def term_scale(replica_tokens):
    scale = 1.0
    while replica_tokens * 6 * 0.25 * scale * 2 < 60000:
        scale *= 2
    return scale


def shape_of(array, dtype=None):
    return jax.ShapeDtypeStruct(array.shape, dtype or array.dtype)


def call(kernel, vmem=VM, flops=0, moved=0, **settings):
    return pl.pallas_call(
        kernel,
        compiler_params=pltpu.CompilerParams(vmem_limit_bytes=vmem * MIB),
        cost_estimate=pl.CostEstimate(flops=flops, bytes_accessed=moved, transcendentals=0),
        **settings,
    )


def after(value, *others, flops=0):
    def kernel(*refs):
        pass

    return call(
        kernel,
        vmem=1,
        flops=flops,
        out_shape=shape_of(value),
        in_specs=[ANY] * (1 + len(others)),
        out_specs=ANY,
        input_output_aliases={0: 0},
    )(value, *others)


def gradient_terms(owners, tokens, key_cotangent, scale, rows, strips, *others):
    units = owners.shape[0]
    strip, width = rows // strips, key_cotangent.shape[1]

    def kernel(owners_ref, tokens_ref, cotangent_ref, *refs):
        outs = refs[len(others) : len(others) + units * strips]
        made, sems = refs[-2:]
        unit = pl.program_id(0)
        slot = lax.rem(unit, 2)

        def copy(slot, s, k):
            return pltpu.make_async_copy(made.at[slot, s], outs[k * strips + s], sems.at[slot, s])

        @pl.when(unit >= 2)
        def _():
            for s in range(strips):
                copy(slot, s, 0).wait()

        for s in range(strips):
            made[slot, s] = scale * lax.dot_general(
                tokens_ref[:, s * strip : (s + 1) * strip],
                cotangent_ref[...],
                (((0,), (0,)), ((), ())),
                preferred_element_type=jnp.float32,
            )
        for k in range(units):

            @pl.when(unit == k)
            def _(k=k):
                for s in range(strips):
                    copy(slot, s, k).start()

        @pl.when(unit == units - 1)
        def _():
            for s in range(strips):
                if units > 1:
                    copy(1 - slot, s, 0).wait()
                copy(slot, s, 0).wait()

    outs = call(
        kernel,
        flops=TUNE.get("terms", 5) * 10**9,
        out_shape=[jax.ShapeDtypeStruct((strip, width), jnp.float32)] * (units * strips),
        grid_spec=pltpu.PrefetchScalarGridSpec(
            num_scalar_prefetch=1,
            grid=(units,),
            in_specs=[
                pl.BlockSpec((tokens.shape[0], rows), lambda i, owners: (0, owners[i])),
                pl.BlockSpec(key_cotangent.shape, lambda i, owners: (0, 0)),
            ]
            + [ANY] * len(others),
            out_specs=[ANY] * (units * strips),
            scratch_shapes=[
                pltpu.VMEM((2, strips, strip, width), jnp.float32),
                pltpu.SemaphoreType.DMA((2, strips)),
            ],
        ),
    )(owners, tokens, key_cotangent, *others)
    return [outs[k * strips : (k + 1) * strips] for k in range(units)]


def project(owners, valid, tokens, weights, rows, *others):
    strip, width = weights[0][0].shape
    strips = rows // strip
    steps = len(weights)
    flat = [piece for step in weights for piece in step]
    count = len(flat)

    def kernel(owners_ref, valid_ref, tokens_ref, *refs):
        out, total, held, sems = refs[-4:]
        step = pl.program_id(0)

        def copy(k, s):
            return pltpu.make_async_copy(refs[k * strips + s], held.at[k, s], sems.at[k, s])

        @pl.when(step == 0)
        def _():
            for k in range(steps):

                @pl.when(valid_ref[k] == 1)
                def _(k=k):
                    for s in range(strips):
                        copy(k, s).start()

            total[...] = jnp.zeros_like(total)

        @pl.when(valid_ref[step] == 1)
        def _():
            for s in range(strips):
                pltpu.make_async_copy(refs[s], held.at[step, s], sems.at[step, s]).wait()
                total[...] += jnp.dot(
                    tokens_ref[:, s * strip : (s + 1) * strip],
                    held[step, s],
                    preferred_element_type=jnp.float32,
                )

        @pl.when(step == steps - 1)
        def _():
            out[...] = total[...].astype(out.dtype)

    return call(
        kernel,
        flops=TUNE.get("project", 6) * 10**9,
        out_shape=jax.ShapeDtypeStruct((tokens.shape[0], width), jnp.bfloat16),
        grid_spec=pltpu.PrefetchScalarGridSpec(
            num_scalar_prefetch=2,
            grid=(steps,),
            in_specs=[pl.BlockSpec((tokens.shape[0], rows), lambda i, o, v: (0, o[i]))]
            + [ANY] * (count + len(others)),
            out_specs=pl.BlockSpec((tokens.shape[0], width), lambda i, o, v: (0, 0)),
            scratch_shapes=[
                pltpu.VMEM((tokens.shape[0], width), jnp.float32),
                pltpu.VMEM((steps, strips, strip, width), jnp.bfloat16),
                pltpu.SemaphoreType.DMA((steps, strips)),
            ],
        ),
    )(owners, valid, tokens, *flat, *others)


def row_blocks(slab_rows):
    return next(k for k in (4, 3, 2, 1) if slab_rows % (16 * k) == 0 or k == 1)


def outer_terms(slab, outer_params, outer_momentum, place, replicas, *others):
    slab_rows, column_count = outer_params.shape
    blocks = row_blocks(slab_rows)
    step = slab_rows // blocks
    both_ways = OUTER_RATE * (1.0 + OUTER_MOMENTUM)

    def kernel(place_ref, slab_ref, params_ref, momentum_ref, *refs):
        out_ref = refs[-1]
        for r in range(replicas):
            part = slab_ref[:, r * column_count : (r + 1) * column_count]
            out_ref[r] = (both_ways / replicas) * part.astype(jnp.float32)
        own = (1.0 - both_ways) * params_ref[...]
        own = own - (OUTER_RATE * OUTER_MOMENTUM * OUTER_MOMENTUM) * momentum_ref[...]
        out_ref[place_ref[0]] += own

    rows_of = pl.BlockSpec((step, column_count), lambda i, place: (i, 0))
    return call(
        kernel,
        flops=TUNE.get("columns", 0),
        out_shape=jax.ShapeDtypeStruct((replicas, slab_rows, column_count), jnp.float32),
        grid_spec=pltpu.PrefetchScalarGridSpec(
            num_scalar_prefetch=1,
            grid=(blocks,),
            in_specs=[pl.BlockSpec((step, slab.shape[1]), lambda i, place: (i, 0)), rows_of, rows_of]
            + [ANY] * len(others),
            out_specs=pl.BlockSpec((replicas, step, column_count), lambda i, place: (0, i, 0)),
        ),
    )(jnp.reshape(place, (1,)).astype(jnp.int32), slab, outer_params, outer_momentum, *others)


def merge(slab, whole_outer, *others):
    replicas, slab_rows, column_count = whole_outer.shape
    blocks = row_blocks(slab_rows)
    step = slab_rows // blocks

    def kernel(slab_ref, outer_ref, *refs):
        out_ref = refs[-1]
        for r in range(replicas):
            part = slice(r * column_count, (r + 1) * column_count)
            slab_f = slab_ref[:, part].astype(jnp.float32)
            merged = MERGE_WEIGHT * slab_f + (1.0 - MERGE_WEIGHT) * outer_ref[r]
            out_ref[:, part] = merged.astype(out_ref.dtype)

    block = pl.BlockSpec((step, slab.shape[1]), lambda i: (i, 0))
    return call(
        kernel,
        flops=TUNE.get("merge", 3) * 10**9,
        out_shape=shape_of(slab),
        grid=(blocks,),
        in_specs=[block, pl.BlockSpec((replicas, step, column_count), lambda i: (0, i, 0))]
        + [ANY] * len(others),
        out_specs=block,
    )(slab, whole_outer, *others)


def shards(
    tokens,
    key_cotangent,
    key_weight,
    first_moment,
    second_moment,
    local_slab,
    outer_params,
    outer_momentum,
):
    n = lax.axis_size("fsdp")
    me = lax.axis_index("fsdp")
    replicas = lax.axis_size("replica")
    rows = key_weight.shape[0]
    strip = rows // PIECES
    scale = term_scale(n * tokens.shape[0])
    every = range(PIECES)

    def mirrored(links):
        return [(n - 1 - a, n - 1 - b) for a, b in links]

    def among(devices):
        return functools.reduce(jnp.logical_or, [me == d for d in devices], jnp.bool_(False))

    def distinct(devices):
        return len(set(devices)) == len(devices)

    def exchange(up_load, down_load, up):
        down = mirrored(up)
        if distinct([a for a, _ in up + down]) and distinct([b for _, b in up + down]):
            load = up_load
            if up_load is not down_load:
                load = jnp.where(among([a for a, _ in up]), up_load, down_load)
            come = lax.ppermute(load, "fsdp", up + down)
            return come, come
        return lax.ppermute(up_load, "fsdp", up), lax.ppermute(down_load, "fsdp", down)

    def one_of(come):
        return come[0].astype(jnp.float32) if come[0] is come[1] else both(come)

    def both(come):
        return come[0].astype(jnp.float32) + come[1].astype(jnp.float32)

    weight_strip = rows // WEIGHT_PIECES
    each = range(WEIGHT_PIECES)
    weights = [key_weight[p * weight_strip : (p + 1) * weight_strip] for p in each]
    held = [[None] * WEIGHT_PIECES for _ in range(n)]
    sums = [None] * PIECES

    for p in each:
        held[0][p] = exchange(weights[p], weights[p], [(i, i + 1) for i in range(n - 1)])
    place = lax.axis_index("replica")

    owners, loads_of = [], [None]
    for t in range(1, n):
        up, down = n + me - t, t - 1 - (n - 1 - me)
        if 2 * t <= n:
            loads_of.append([len(owners)])
            owners.append(jnp.where(me < t, up, down))
        else:
            loads_of.append([len(owners), len(owners) + 1])
            owners += [up, down]
    owners = jnp.clip(jnp.stack(owners), 0, n - 1).astype(jnp.int32)
    terms = gradient_terms(owners, tokens, key_cotangent, scale, rows, PIECES)
    others = (terms[0][0],) if TUNE.get("terms_first", 1) else ()
    columns = outer_terms(local_slab, outer_params, outer_momentum, place, replicas, *others)
    new_outer = lax.psum_scatter(columns, "replica", scatter_dimension=0, tiled=False)


    for t in range(1, n):
        links = [(i, i + 1) for i in range(t)]
        for p in every:
            w = p * WEIGHT_PIECES // PIECES
            came = held[t - 1][w]
            if t < n - 1 and held[t][w] is None:
                held[t][w] = exchange(*came, [(i, i + 1) for i in range(t, n - 1)])
            if (t, p) == TUNE.get("outer_after"):
                new_outer = after(new_outer, *came)
            lag = TUNE.get("lag", 2)
            others = tuple(held[t - lag][w]) if t >= TUNE.get("tied_from", 3) and t >= lag else ()
            if (t, p) == TUNE.get("outer_before"):
                others = (*others, new_outer)
            loads = [terms[k][p] if t == 1 else after(terms[k][p], *others, flops=TUNE.get(("x", t, p), 0) * 10**9) for k in loads_of[t]]
            if len(loads) == 1:
                load = loads[0] if t == 1 else loads[0] + one_of(sums[p])
                up_load = down_load = load.astype(jnp.float16)
            else:
                up_load = (loads[0] + sums[p][0].astype(jnp.float32)).astype(jnp.float16)
                down_load = (loads[1] + sums[p][1].astype(jnp.float32)).astype(jnp.float16)
            sums[p] = exchange(up_load, down_load, links)
    whole_outer = lax.all_gather(new_outer, "replica", axis=0)
    new_momentum = (outer_params - new_outer) / OUTER_RATE + OUTER_MOMENTUM * outer_momentum
    new_momentum = new_momentum / (1.0 + OUTER_MOMENTUM)
    new_local = merge(local_slab, whole_outer, *((held[n - 2][WEIGHT_PIECES - 1][0],) if TUNE.get("merge_late", 0) else ()))

    owners, valid, steps = [me], [me >= 0], [weights]
    for t in range(n - 1):
        if held[t][0][0] is held[t][0][1]:
            owners.append(jnp.where(me - t - 1 >= 0, me - t - 1, me + t + 1))
            valid.append((me - t - 1 >= 0) | (me + t + 1 <= n - 1))
            steps.append([held[t][p][0] for p in each])
        else:
            owners += [me - t - 1, me + t + 1]
            valid += [me - t - 1 >= 0, me + t + 1 <= n - 1]
            steps += [[held[t][p][0] for p in each], [held[t][p][1] for p in each]]
    owners = jnp.clip(jnp.stack(owners), 0, n - 1).astype(jnp.int32)
    others = (new_local,) if TUNE.get("merge_first", 1) else ()
    projected = project(owners, jnp.stack(valid).astype(jnp.int32), tokens, steps, rows, *others)

    [own] = gradient_terms(jnp.reshape(me, (1,)), tokens, key_cotangent, scale, rows, PIECES, *others)
    own = [after(o, projected) for o in own]
    gradient = jnp.concatenate([own[p] + one_of(sums[p]) for p in every], 0) / scale
    new_first = BETA_ONE * first_moment + (1.0 - BETA_ONE) * gradient
    new_second = BETA_TWO * second_moment + (1.0 - BETA_TWO) * gradient * gradient
    weight_f = key_weight.astype(jnp.float32)
    update = (
        new_first / FIRST_FIX / (jnp.sqrt(new_second / SECOND_FIX) + EPSILON)
        + DECAY_RATE * weight_f
    )
    new_weight = (weight_f - INNER_RATE * update).astype(jnp.bfloat16)
    return (projected, new_weight, new_first, new_second, new_outer, new_momentum, new_local)


def solution(mesh):
    split = P(("replica", "fsdp"), None)
    outer = P("fsdp", "replica")
    return jax.shard_map(
        shards,
        mesh=mesh,
        in_specs=(split, split, split, split, split, split, outer, outer),
        out_specs=(split, split, split, split, outer, outer, split),
        check_vma=False,
    )
```

time: 170 us -> 179 us (1.053)
  the two profiles are of different devices: /device:TPU:26 before, /device:TPU:0 now
where the time goes in v2:
time: 179 us; the launch traced here: 178 us
  starting transfers between devices  53.4 us (30%)
  waiting for transfers between devices  52.4 us (29%)
  Pallas kernels  29.4 us (16%)
  other arithmetic  21.1 us (12%)
  between operations  14.5 us (8%)
  local copies, waits for them, and re-layouts  7.47 us (4%)
    ppermute x6, starting transfers between devices, exchange(): lax.ppermute(up_load, 'fsdp', up)  35.1 us
    ppermute x6, waiting for transfers between devices, exchange(): lax.ppermute(down_load, 'fsdp', down)  29 us
    ppermute x3, waiting for transfers between devices, exchange(): come = lax.ppermute(load, 'fsdp', up + down)  22 us
    ppermute x3, starting transfers between devices, exchange(): come = lax.ppermute(load, 'fsdp', up + down)  11.8 us
    pallas_call x2, Pallas kernels, gradient_terms(): call(kernel, flops=TUNE.get('terms', 5) * 10 ** 9, out_shape=[jax.ShapeDt...  11.5 us
    pallas_call x1, Pallas kernels, project(): call(kernel, flops=TUNE.get('project', 6) * 10 ** 9, out_shape=jax.ShapeD...  9.44 us
    convert_element_type x4, other arithmetic, shards(): up_load = down_load = load.astype(jnp.float16)  7.4 us
    unnamed x48, local copies, waits for them, and re-layouts  7.28 us
  transfers between devices with their start and end apart: 17, of which 5 were waited for; matrix products, arithmetic and copies ran while one was open for 9% of the time, Pallas kernels for 10%

profile of v2, /device:TPU:0, one launch (start us, length us, event | category | flops | bytes accessed | tf_op | source)
XLA Modules:
  0.0 178.2 jit_solution(12320806576456938875)
XLA Ops:
  7.2 0.7 add_clamp_fusion.owners_ref
  7.9 8.0 %shard_map.135 = (f32[512,512]{1,0:T(8,128)}, f32[512,512]{1,0:T(8,128)}, f32[512,512]{1,0:T(8,128)}, f32[512,512]{1,0:T(8,128)}, f32[512,512]{1,0:T(8,128)}, /*...) custom-call(s32[4]{0:T(128)} %add_clamp_fusion.owners_ref, bf16[512,4096]{1,0:T(8,128)(2,1)} %tokens_ref.5, ...), custom_call_target="tpu_custom_call" | custom-call | flops 5000000000 | tf_op jit(solution)/shard_map/pallas_call | solution.py:102
  15.9 4.1 %shard_map.136 = f32[8,192,512]{2,1,0:T(8,128)} custom-call(s32[1]{0:T(128)} %bitcast.12.place_ref, bf16[192,4096]{1,0:T(8,128)(2,1)} %slab_ref.3, f32[192,512]{1,0:T(8,128)} %params_ref.1, f32[192,512]{1,0:T(8,128)} %momentum_ref.1, f32[512,512]{1,0:T(8,128)} %get-tuple-element.17.refs_0_), custom_call_target="tpu_custom_call" | custom-call | flops 40000000000 | tf_op jit(solution)/shard_map/pallas_call | solution.py:202
  20.1 1.1 copy-done.20
  21.2 1.3 collective-permute-start.1
  22.5 6.5 %collective-permute-start = (bf16[1024,512]{1,0:T(8,128)(2,1)S(1)}, bf16[1024,512]{1,0:T(8,128)(2,1)}, u32[]{:S(2)}, u32[]{:S(2)}) collective-permute-start(bf16[1024,512]{1,0:T(8,128)(2,1)S(1)} %copy-done.20), channel_id=1, source_target_pairs={{0,1},{1,2},{2,3},{4,5},{5,6},{6,7},{8,9},{9,10},{10,11},{12,13},{... | collective-permute-start | bytes 3145736 | tf_op jit(solution)/shard_map/ppermute | solution.py:276
  29.0 20.3 %collective-permute-done.1.refs_2_ = bf16[1024,512]{1,0:T(8,128)(2,1)} collective-permute-done((bf16[1024,512]{1,0:T(8,128)(2,1)S(1)}, bf16[1024,512]{1,0:T(8,128)(2,1)}, u32[]{:S(2)}, u32[]{:S(2)}) %collective-permute-start.1) | collective-permute-done | bytes 1048608 | tf_op jit(solution)/shard_map/ppermute | solution.py:276
  49.4 1.3 collective-permute-start.3
  50.7 0.7 collective-permute-start.2
  51.4 2.2 %convert_element_type.65 = f16[512,512]{1,0:T(8,128)(2,1)} convert(f32[512,512]{1,0:T(8,128)} %get-tuple-element.17.refs_0_) | non-fusion elementwise | flops 262144 | bytes 1572864 | tf_op jit(solution)/shard_map/convert_element_type | solution.py:326
  53.6 8.4 %collective-permute-start.5 = (f16[512,512]{1,0:T(8,128)(2,1)}, f16[512,512]{1,0:T(8,128)(2,1)}, u32[]{:S(2)}, u32[]{:S(2)}) collective-permute-start(f16[512,512]{1,0:T(8,128)(2,1)} %convert_element_type.65), channel_id=1, source_target_pairs={{0,1},{3,2},{4,5},{7,6},{8,9},{11,10},{12,13},{15,14},{16,17},{19,... | collective-permute-start | bytes 1572872 | tf_op jit(solution)/shard_map/ppermute | solution.py:274
  62.0 2.1 %convert_element_type.74 = f16[512,512]{1,0:T(8,128)(2,1)} convert(f32[512,512]{1,0:T(8,128)} %get-tuple-element.25) | non-fusion elementwise | flops 262144 | bytes 1572864 | tf_op jit(solution)/shard_map/convert_element_type | solution.py:326
  64.1 2.1 %collective-permute-start.10 = (f16[512,512]{1,0:T(8,128)(2,1)}, f16[512,512]{1,0:T(8,128)(2,1)}, u32[]{:S(2)}, u32[]{:S(2)}) collective-permute-start(f16[512,512]{1,0:T(8,128)(2,1)} %convert_element_type.74), channel_id=1, source_target_pairs={{0,1},{3,2},{4,5},{7,6},{8,9},{11,10},{12,13},{15,14},{16,17},{19,... | collective-permute-start | bytes 1572872 | tf_op jit(solution)/shard_map/ppermute | solution.py:274
  66.2 1.0 copy-done.16
  67.2 8.7 %collective-permute-done.3.refs_4_.refs_2_ = bf16[1024,512]{1,0:T(8,128)(2,1)S(1)} collective-permute-done((bf16[1024,512]{1,0:T(8,128)(2,1)}, bf16[1024,512]{1,0:T(8,128)(2,1)S(1)}, u32[]{:S(2)}, u32[]{:S(2)}) %collective-permute-start.3) | collective-permute-done | bytes 1048608 | tf_op jit(solution)/shard_map/ppermute | solution.py:276
  75.8 1.2 broadcast_select_fusion
  77.0 1.3 collective-permute-start.4
  78.4 1.0 copy-done.13
  79.4 0.5 convert_element_type.63.valid_ref
  80.0 0.6 broadcast_clamp_fusion.owners_ref
  80.6 22.0 %collective-permute-done.4.refs_1_.refs_2_.refs_5_ = bf16[1024,512]{1,0:T(8,128)(2,1)S(1)} collective-permute-done((bf16[1024,512]{1,0:T(8,128)(2,1)}, bf16[1024,512]{1,0:T(8,128)(2,1)S(1)}, u32[]{:S(2)}, u32[]{:S(2)}) %collective-permute-start.4) | collective-permute-done | bytes 1048608 | tf_op jit(solution)/shard_map/ppermute | solution.py:274
  102.6 1.9 %add_convert_fusion.5 = f16[512,512]{1,0:T(8,128)(2,1)S(1)} fusion(f32[512,512]{1,0:T(8,128)} %copy-done.16, f16[512,512]{1,0:T(8,128)(2,1)} %collective-permute-done.5), kind=kLoop, calls=%fused_computation.15 | loop fusion | flops 786432 | bytes 2097152 | tf_op jit(solution)/shard_map/convert_element_type | solution.py:326
  104.5 0.7 collective-permute-start.8
  105.2 2.2 %collective-permute-start.6 = (f16[512,512]{1,0:T(8,128)(2,1)S(1)}, f16[512,512]{1,0:T(8,128)(2,1)S(1)}, u32[]{:S(2)}, u32[]{:S(2)}) collective-permute-start(f16[512,512]{1,0:T(8,128)(2,1)S(1)} %add_convert_fusion.5), channel_id=1, source_target_pairs={{0,1},{1,2},{4,5},{5,6},{8,9},{9,10},{12,13},{13,14},{16,17},{17,1... | collective-permute-start | bytes 1572872 | tf_op jit(solution)/shard_map/ppermute | solution.py:276
  107.5 1.2 add_convert_fusion.2
  108.7 0.7 collective-permute-start.13
  109.4 7.8 %collective-permute-start.11 = (f16[512,512]{1,0:T(8,128)(2,1)S(1)}, f16[512,512]{1,0:T(8,128)(2,1)S(1)}, u32[]{:S(2)}, u32[]{:S(2)}) collective-permute-start(f16[512,512]{1,0:T(8,128)(2,1)S(1)} %add_convert_fusion.2), channel_id=1, source_target_pairs={{0,1},{1,2},{4,5},{5,6},{8,9},{9,10},{12,13},{13,14},{16,17},{17,1... | collective-permute-start | bytes 1572872 | tf_op jit(solution)/shard_map/ppermute | solution.py:276
  117.2 1.2 collective-permute-done.6
  118.4 0.2 add_convert_fusion.4
  118.6 8.6 %collective-permute-start.7 = (f16[512,512]{1,0:T(8,128)(2,1)S(1)}, f16[512,512]{1,0:T(8,128)(2,1)S(1)}, u32[]{:S(2)}, u32[]{:S(2)}) collective-permute-start(f16[512,512]{1,0:T(8,128)(2,1)S(1)} %add_convert_fusion.4), channel_id=1, source_target_pairs={{0,1},{1,2},{2,3},{4,5},{5,6},{6,7},{8,9},{9,10},{10,11},{12,13},{... | collective-permute-start | bytes 1572872 | tf_op jit(solution)/shard_map/ppermute | solution.py:276
  127.2 1.0 add_convert_fusion.3
  128.2 1.3 collective-permute-start.9
  129.6 1.0 add_convert_fusion.1
  130.6 9.3 %collective-permute-start.12 = (f16[512,512]{1,0:T(8,128)(2,1)}, f16[512,512]{1,0:T(8,128)(2,1)}, u32[]{:S(2)}, u32[]{:S(2)}) collective-permute-start(f16[512,512]{1,0:T(8,128)(2,1)} %add_convert_fusion.1), channel_id=1, source_target_pairs={{0,1},{1,2},{2,3},{4,5},{5,6},{6,7},{8,9},{9,10},{10,11},{12,13},{... | collective-permute-start | bytes 1572872 | tf_op jit(solution)/shard_map/ppermute | solution.py:276
  140.0 1.0 add_convert_fusion
  140.9 1.3 collective-permute-start.14
  142.2 0.9 add_multiply_fusion
  143.1 4.3 %shard_map.138.refs_6_.refs_0_ = bf16[192,4096]{1,0:T(8,128)(2,1)} custom-call(bf16[192,4096]{1,0:T(8,128)(2,1)} %slab_ref.3, f32[8,192,512]{2,1,0:T(8,128)} %bitcast.19), custom_call_target="tpu_custom_call" | custom-call | flops 3000000000 | tf_op jit(solution)/shard_map/pallas_call | solution.py:230
  147.4 9.4 %shard_map.139.refs_1_ = bf16[512,512]{1,0:T(8,128)(2,1)} custom-call(s32[6]{0:T(128)} %broadcast_clamp_fusion.owners_ref, s32[6]{0:T(128)} %convert_element_type.63.valid_ref, bf16[512,4096]{1,0:T(8,128)(2,1)} %tokens_ref.5, bf16[1024,512]{1,0:T(8,128)(2,1)} %refs_0_.1, bf16[1024,512]{1,0:T(8,128)(2,1)} %collective-permute-done.refs_1_, ...), custom_call_target="tpu_custom_call" | custom-call | flops 6000000000 | tf_op jit(solution)/shard_map/pallas_call | solution.py:163
  156.9 3.5 %shard_map.140 = (f32[512,512]{1,0:T(8,128)}, f32[512,512]{1,0:T(8,128)}) custom-call(s32[1]{0:T(128)} %bitcast.owners_ref, bf16[512,4096]{1,0:T(8,128)(2,1)} %tokens_ref.5, bf16[512,512]{1,0:T(8,128)(2,1)} %cotangent_ref.3, bf16[192,4096]{1,0:T(8,128)(2,1)} %shard_map.138.refs_6_.refs_0_), custom_call_target="tpu_custom_call" | custom-call | flops 5000000000 | tf_op jit(solution)/shard_map/pallas_call | solution.py:102
  160.5 1.3 copy-done.1
  161.8 1.0 copy-done.2
  162.8 1.2 copy-done.3
  164.0 1.4 add_add_fusion.1
  165.4 1.6 add_add_fusion
  167.0 0.4 copy-done.18
  167.4 0.3 copy-done.21
  167.6 3.8 %fusion.2 = (bf16[1024,512]{1,0:T(8,128)(2,1)}, f32[1024,512]{1,0:T(8,128)}, f32[1024,512]{1,0:T(8,128)}) fusion(bf16[1024,512]{1,0:T(8,128)(2,1)S(1)} %copy-done.21, f32[512,512]{1,0:T(8,128)S(1)} %add_add_fusion, f32[512,512]{1,0:T(8,128)S(1)} %add_add_fusion.1, f32[1024,512]{1,0:T(8,128)S(1)} %copy-done.18, f32[1024,512]{1,0:T(8,128)S(1)} %copy-done.19), kind=kLoop, calls=%fused_computation.4 | loop fusion | flops 9961472 | bytes 12582912 | tf_op jit(solution)/shard_map/convert_element_type | solution.py:360
  (68 shorter events, 0.6 us)
Async XLA Ops:
  7.2 95.4 %reduce-scatter.2.cloned.1.call-start = ((), (), s32[]{:S(2)}) async-start(), calls=%async_computation.1 | async-start | bytes 3538944 | tf_op jit(solution)/shard_map/reduce_scatter | solution.py:307
  20.0 1.2 copy-start.20
  20.0 46.2 %copy-start.15 = (f32[512,512]{1,0:T(8,128)S(1)}, f32[512,512]{1,0:T(8,128)}, u32[]{:S(2)}) copy-start(f32[512,512]{1,0:T(8,128)} %get-tuple-element.20.refs_0_) | copy-start | bytes 3145732
  20.0 123.1 %all-gather.3.cloned.1.call-start = ((), (), s32[]{:S(2)}) async-start(), calls=%async_computation.2 | async-start | bytes 3538944 | tf_op jit(solution)/shard_map/all_gather | solution.py:331
  21.2 28.2 %collective-permute-start.1 = (bf16[1024,512]{1,0:T(8,128)(2,1)S(1)}, bf16[1024,512]{1,0:T(8,128)(2,1)}, u32[]{:S(2)}, u32[]{:S(2)}) collective-permute-start(bf16[1024,512]{1,0:T(8,128)(2,1)S(1)} %copy-done.20), channel_id=1, source_target_pairs={{3,2},{2,1},{1,0},{7,6},{6,5},{5,4},{11,10},{10,9},{9,8},{15,14},{... | collective-permute-start | bytes 3145736 | tf_op jit(solution)/shard_map/ppermute | solution.py:276
  22.5 28.2 %collective-permute-start = (bf16[1024,512]{1,0:T(8,128)(2,1)S(1)}, bf16[1024,512]{1,0:T(8,128)(2,1)}, u32[]{:S(2)}, u32[]{:S(2)}) collective-permute-start(bf16[1024,512]{1,0:T(8,128)(2,1)S(1)} %copy-done.20), channel_id=1, source_target_pairs={{0,1},{1,2},{2,3},{4,5},{5,6},{6,7},{8,9},{9,10},{10,11},{12,13},{... | collective-permute-start | bytes 3145736 | tf_op jit(solution)/shard_map/ppermute | solution.py:276
  49.4 26.4 %collective-permute-start.3 = (bf16[1024,512]{1,0:T(8,128)(2,1)}, bf16[1024,512]{1,0:T(8,128)(2,1)S(1)}, u32[]{:S(2)}, u32[]{:S(2)}) collective-permute-start(bf16[1024,512]{1,0:T(8,128)(2,1)} %collective-permute-done.1.refs_2_), channel_id=1, source_target_pairs={{2,1},{1,0},{6,5},{5,4},{10,9},{9,8},{14,13},{13,12},{18,17},{17,1... | collective-permute-start | bytes 3145736 | tf_op jit(solution)/shard_map/ppermute | solution.py:276
  50.7 25.1 %collective-permute-start.2 = (bf16[1024,512]{1,0:T(8,128)(2,1)}, bf16[1024,512]{1,0:T(8,128)(2,1)S(1)}, u32[]{:S(2)}, u32[]{:S(2)}) collective-permute-start(bf16[1024,512]{1,0:T(8,128)(2,1)} %collective-permute-done.refs_1_), channel_id=1, source_target_pairs={{1,2},{2,3},{5,6},{6,7},{9,10},{10,11},{13,14},{14,15},{17,18},{18... | collective-permute-start | bytes 3145736 | tf_op jit(solution)/shard_map/ppermute | solution.py:276
  53.6 49.0 %collective-permute-start.5 = (f16[512,512]{1,0:T(8,128)(2,1)}, f16[512,512]{1,0:T(8,128)(2,1)}, u32[]{:S(2)}, u32[]{:S(2)}) collective-permute-start(f16[512,512]{1,0:T(8,128)(2,1)} %convert_element_type.65), channel_id=1, source_target_pairs={{0,1},{3,2},{4,5},{7,6},{8,9},{11,10},{12,13},{15,14},{16,17},{19,... | collective-permute-start | bytes 1572872 | tf_op jit(solution)/shard_map/ppermute | solution.py:274
  64.1 43.3 %collective-permute-start.10 = (f16[512,512]{1,0:T(8,128)(2,1)}, f16[512,512]{1,0:T(8,128)(2,1)}, u32[]{:S(2)}, u32[]{:S(2)}) collective-permute-start(f16[512,512]{1,0:T(8,128)(2,1)} %convert_element_type.74), channel_id=1, source_target_pairs={{0,1},{3,2},{4,5},{7,6},{8,9},{11,10},{12,13},{15,14},{16,17},{19,... | collective-permute-start | bytes 1572872 | tf_op jit(solution)/shard_map/ppermute | solution.py:274
  66.2 1.0 copy-start.16
  67.2 11.2 %copy-start.12 = (f32[512,512]{1,0:T(8,128)S(1)}, f32[512,512]{1,0:T(8,128)}, u32[]{:S(2)}) copy-start(f32[512,512]{1,0:T(8,128)} %get-tuple-element.24.refs_0_) | copy-start | bytes 3145732
  75.8 64.1 %copy-start.7 = (bf16[1024,512]{1,0:T(8,128)(2,1)}, bf16[1024,512]{1,0:T(8,128)(2,1)S(1)}, u32[]{:S(2)}) copy-start(bf16[1024,512]{1,0:T(8,128)(2,1)S(1)} %collective-permute-done.3.refs_4_.refs_2_) | copy-start | bytes 3145732
  75.8 64.1 %copy-start.9 = (bf16[1024,512]{1,0:T(8,128)(2,1)}, bf16[1024,512]{1,0:T(8,128)(2,1)S(1)}, u32[]{:S(2)}) copy-start(bf16[1024,512]{1,0:T(8,128)(2,1)S(1)} %collective-permute-done.2.refs_3_.refs_1_) | copy-start | bytes 3145732
  77.0 25.5 %collective-permute-start.4 = (bf16[1024,512]{1,0:T(8,128)(2,1)}, bf16[1024,512]{1,0:T(8,128)(2,1)S(1)}, u32[]{:S(2)}, u32[]{:S(2)}) collective-permute-start(bf16[1024,512]{1,0:T(8,128)(2,1)} %broadcast_select_fusion), channel_id=1, source_target_pairs={{2,3},{1,0},{6,7},{5,4},{10,11},{9,8},{14,15},{13,12},{18,19},{17,... | collective-permute-start | bytes 3145736 | tf_op jit(solution)/shard_map/ppermute | solution.py:274
  78.4 1.0 copy-start.13
  102.6 2.0 %copy-start.4 = (bf16[1024,512]{1,0:T(8,128)(2,1)}, bf16[1024,512]{1,0:T(8,128)(2,1)S(1)}, u32[]{:S(2)}) copy-start(bf16[1024,512]{1,0:T(8,128)(2,1)S(1)} %collective-permute-done.4.refs_1_.refs_2_.refs_5_) | copy-start | bytes 3145732
  102.6 4.9 %copy-start.14 = (f32[512,512]{1,0:T(8,128)S(1)}, f32[512,512]{1,0:T(8,128)}, u32[]{:S(2)}) copy-start(f32[512,512]{1,0:T(8,128)} %copy-done.13) | copy-start | bytes 3145732
  102.6 14.5 %copy-start.11 = (f32[512,512]{1,0:T(8,128)S(1)}, f32[512,512]{1,0:T(8,128)}, u32[]{:S(2)}) copy-start(f32[512,512]{1,0:T(8,128)} %get-tuple-element.19.refs_0_) | copy-start | bytes 3145732
  104.5 22.6 %collective-permute-start.8 = (f16[512,512]{1,0:T(8,128)(2,1)S(1)}, f16[512,512]{1,0:T(8,128)(2,1)S(1)}, u32[]{:S(2)}, u32[]{:S(2)}) collective-permute-start(f16[512,512]{1,0:T(8,128)(2,1)S(1)} %add_convert_fusion.5), channel_id=1, source_target_pairs={{3,2},{2,1},{7,6},{6,5},{11,10},{10,9},{15,14},{14,13},{19,18},{18... | collective-permute-start | bytes 1572872 | tf_op jit(solution)/shard_map/ppermute | solution.py:276
  105.2 13.1 %collective-permute-start.6 = (f16[512,512]{1,0:T(8,128)(2,1)S(1)}, f16[512,512]{1,0:T(8,128)(2,1)S(1)}, u32[]{:S(2)}, u32[]{:S(2)}) collective-permute-start(f16[512,512]{1,0:T(8,128)(2,1)S(1)} %add_convert_fusion.5), channel_id=1, source_target_pairs={{0,1},{1,2},{4,5},{5,6},{8,9},{9,10},{12,13},{13,14},{16,17},{17,1... | collective-permute-start | bytes 1572872 | tf_op jit(solution)/shard_map/ppermute | solution.py:276
  108.7 31.3 %collective-permute-start.13 = (f16[512,512]{1,0:T(8,128)(2,1)S(1)}, f16[512,512]{1,0:T(8,128)(2,1)S(1)}, u32[]{:S(2)}, u32[]{:S(2)}) collective-permute-start(f16[512,512]{1,0:T(8,128)(2,1)S(1)} %add_convert_fusion.2), channel_id=1, source_target_pairs={{3,2},{2,1},{7,6},{6,5},{11,10},{10,9},{15,14},{14,13},{19,18},{18... | collective-permute-start | bytes 1572872 | tf_op jit(solution)/shard_map/ppermute | solution.py:276
  109.4 20.2 %collective-permute-start.11 = (f16[512,512]{1,0:T(8,128)(2,1)S(1)}, f16[512,512]{1,0:T(8,128)(2,1)S(1)}, u32[]{:S(2)}, u32[]{:S(2)}) collective-permute-start(f16[512,512]{1,0:T(8,128)(2,1)S(1)} %add_convert_fusion.2), channel_id=1, source_target_pairs={{0,1},{1,2},{4,5},{5,6},{8,9},{9,10},{12,13},{13,14},{16,17},{17,1... | collective-permute-start | bytes 1572872 | tf_op jit(solution)/shard_map/ppermute | solution.py:276
  117.2 10.0 %copy-start.10 = (f32[512,512]{1,0:T(8,128)S(1)}, f32[512,512]{1,0:T(8,128)}, u32[]{:S(2)}) copy-start(f32[512,512]{1,0:T(8,128)} %get-tuple-element.21.refs_0_) | copy-start | bytes 3145732
  118.6 44.2 %collective-permute-start.7 = (f16[512,512]{1,0:T(8,128)(2,1)S(1)}, f16[512,512]{1,0:T(8,128)(2,1)S(1)}, u32[]{:S(2)}, u32[]{:S(2)}) collective-permute-start(f16[512,512]{1,0:T(8,128)(2,1)S(1)} %add_convert_fusion.4), channel_id=1, source_target_pairs={{0,1},{1,2},{2,3},{4,5},{5,6},{6,7},{8,9},{9,10},{10,11},{12,13},{... | collective-permute-start | bytes 1572872 | tf_op jit(solution)/shard_map/ppermute | solution.py:276
  127.2 2.3 %copy-start.8 = (f32[512,512]{1,0:T(8,128)S(1)}, f32[512,512]{1,0:T(8,128)}, u32[]{:S(2)}) copy-start(f32[512,512]{1,0:T(8,128)} %get-tuple-element.23.refs_0_) | copy-start | bytes 3145732
  128.2 34.6 %collective-permute-start.9 = (f16[512,512]{1,0:T(8,128)(2,1)}, f16[512,512]{1,0:T(8,128)(2,1)}, u32[]{:S(2)}, u32[]{:S(2)}) collective-permute-start(f16[512,512]{1,0:T(8,128)(2,1)} %add_convert_fusion.3), channel_id=1, source_target_pairs={{3,2},{2,1},{1,0},{7,6},{6,5},{5,4},{11,10},{10,9},{9,8},{15,14},{... | collective-permute-start | bytes 1572872 | tf_op jit(solution)/shard_map/ppermute | solution.py:276
  129.5 10.4 %copy-start.6 = (f32[512,512]{1,0:T(8,128)S(1)}, f32[512,512]{1,0:T(8,128)}, u32[]{:S(2)}) copy-start(f32[512,512]{1,0:T(8,128)} %get-tuple-element.26.refs_0_) | copy-start | bytes 3145732
  130.6 34.8 %collective-permute-start.12 = (f16[512,512]{1,0:T(8,128)(2,1)}, f16[512,512]{1,0:T(8,128)(2,1)}, u32[]{:S(2)}, u32[]{:S(2)}) collective-permute-start(f16[512,512]{1,0:T(8,128)(2,1)} %add_convert_fusion.1), channel_id=1, source_target_pairs={{0,1},{1,2},{2,3},{4,5},{5,6},{6,7},{8,9},{9,10},{10,11},{12,13},{... | collective-permute-start | bytes 1572872 | tf_op jit(solution)/shard_map/ppermute | solution.py:276
  139.9 2.3 %copy-start.17 = (f32[192,512]{1,0:T(8,128)S(1)}, f32[192,512]{1,0:T(8,128)}, u32[]{:S(2)}) copy-start(f32[192,512]{1,0:T(8,128)} %shard_map.137) | copy-start | bytes 1179652
  139.9 2.3 %copy-start.22 = (f32[192,512]{1,0:T(8,128)S(1)}, f32[192,512]{1,0:T(8,128)}, u32[]{:S(2)}) copy-start(f32[192,512]{1,0:T(8,128)} %params_ref.1) | copy-start | bytes 1179652
  139.9 2.3 %copy-start.23 = (f32[192,512]{1,0:T(8,128)S(1)}, f32[192,512]{1,0:T(8,128)}, u32[]{:S(2)}) copy-start(f32[192,512]{1,0:T(8,128)} %momentum_ref.1) | copy-start | bytes 1179652
  140.9 24.5 %collective-permute-start.14 = (f16[512,512]{1,0:T(8,128)(2,1)}, f16[512,512]{1,0:T(8,128)(2,1)}, u32[]{:S(2)}, u32[]{:S(2)}) collective-permute-start(f16[512,512]{1,0:T(8,128)(2,1)} %add_convert_fusion), channel_id=1, source_target_pairs={{3,2},{2,1},{1,0},{7,6},{6,5},{5,4},{11,10},{10,9},{9,8},{15,14},{... | collective-permute-start | bytes 1572872 | tf_op jit(solution)/shard_map/ppermute | solution.py:276
  156.9 3.6 %copy-start.5 = (bf16[512,512]{1,0:T(8,128)(2,1)S(1)}, bf16[512,512]{1,0:T(8,128)(2,1)}, u32[]{:S(2)}) copy-start(bf16[512,512]{1,0:T(8,128)(2,1)} %shard_map.139.refs_1_) | copy-start | bytes 1572868
  160.4 2.3 %copy-start = (f32[512,512]{1,0:T(8,128)S(1)}, f32[512,512]{1,0:T(8,128)}, u32[]{:S(2)}) copy-start(f32[512,512]{1,0:T(8,128)} %get-tuple-element.22.refs_0_) | copy-start | bytes 3145732
  160.4 1.3 copy-start.1
  161.8 1.0 copy-start.2
  162.7 1.2 copy-start.3
  164.0 3.0 %copy-start.19 = (f32[1024,512]{1,0:T(8,128)S(1)}, f32[1024,512]{1,0:T(8,128)}, u32[]{:S(2)}) copy-start(f32[1024,512]{1,0:T(8,128)} %param.12) | copy-start | bytes 6291460
  165.4 2.0 %copy-start.18 = (f32[1024,512]{1,0:T(8,128)S(1)}, f32[1024,512]{1,0:T(8,128)}, u32[]{:S(2)}) copy-start(f32[1024,512]{1,0:T(8,128)} %param.11) | copy-start | bytes 6291460
  165.4 2.2 %copy-start.21 = (bf16[1024,512]{1,0:T(8,128)(2,1)S(1)}, bf16[1024,512]{1,0:T(8,128)(2,1)}, u32[]{:S(2)}) copy-start(bf16[1024,512]{1,0:T(8,128)(2,1)} %refs_0_.1) | copy-start | bytes 3145732
Sparse Core Ops, SparseCore 0:
  20.1 48.9 reduce-scatter.1
  102.7 35.4 all-gather.2

commit v3 on v2

v3 whole, which is shorter than its diff:
```python
import functools

import jax
import jax.numpy as jnp
from jax import lax
from jax.experimental import pallas as pl
from jax.experimental.pallas import tpu as pltpu
from jax.sharding import PartitionSpec as P

BETA_ONE = 0.9
BETA_TWO = 0.95
INNER_RATE = 0.001
DECAY_RATE = 0.1
EPSILON = 1e-08
FIRST_FIX = 1.0 - (0.9**50) ** 2
SECOND_FIX = 1.0 - (0.95**50) ** 2
OUTER_RATE = 0.7
OUTER_MOMENTUM = 0.9
MERGE_WEIGHT = 0.5
TUNE = {'rp': 2, 'gp': 2, 'vk': 16, 'vm': 12, 'vo': 12, 'columns': 0, 'chain': 1, 'gate': None, ('tie', 1, 0): None, ('tie', 1, 1): None, ('tie', 3, 0): 2, ('tie', 3, 1): 2, ('x', 2, 0): 14, ('x', 2, 1): 14, ('x', 3, 0): 14, ('x', 3, 1): 14}
PIECES = TUNE.get("rp", 2)
WEIGHT_PIECES = TUNE.get('gp', 2)
VM = TUNE.get('vmem', 60)
ANY = pl.BlockSpec(memory_space=pl.ANY)
MIB = 1 << 20


def term_scale(replica_tokens):
    scale = 1.0
    while replica_tokens * 6 * 0.25 * scale * 2 < 60000:
        scale *= 2
    return scale


def shape_of(array, dtype=None):
    return jax.ShapeDtypeStruct(array.shape, dtype or array.dtype)


def call(kernel, vmem=VM, flops=0, moved=0, **settings):
    return pl.pallas_call(
        kernel,
        compiler_params=pltpu.CompilerParams(vmem_limit_bytes=vmem * MIB),
        cost_estimate=pl.CostEstimate(flops=flops, bytes_accessed=moved, transcendentals=0),
        **settings,
    )


def after(value, *others, flops=0):
    def kernel(*refs):
        pass

    return call(
        kernel,
        vmem=1,
        flops=flops,
        out_shape=shape_of(value),
        in_specs=[ANY] * (1 + len(others)),
        out_specs=ANY,
        input_output_aliases={0: 0},
    )(value, *others)


def project(owners, valid, tokens, weights, rows, *others):
    strip, width = weights[0][0].shape
    strips = rows // strip
    steps = len(weights)
    flat = [piece for step in weights for piece in step]
    count = len(flat)

    def kernel(owners_ref, valid_ref, tokens_ref, *refs):
        out, total, held, sems = refs[-4:]
        step = pl.program_id(0)

        def copy(k, s):
            return pltpu.make_async_copy(refs[k * strips + s], held.at[k, s], sems.at[k, s])

        @pl.when(step == 0)
        def _():
            for k in range(steps):

                @pl.when(valid_ref[k] == 1)
                def _(k=k):
                    for s in range(strips):
                        copy(k, s).start()

            total[...] = jnp.zeros_like(total)

        @pl.when(valid_ref[step] == 1)
        def _():
            for s in range(strips):
                pltpu.make_async_copy(refs[s], held.at[step, s], sems.at[step, s]).wait()
                total[...] += jnp.dot(
                    tokens_ref[:, s * strip : (s + 1) * strip],
                    held[step, s],
                    preferred_element_type=jnp.float32,
                )

        @pl.when(step == steps - 1)
        def _():
            out[...] = total[...].astype(out.dtype)

    return call(
        kernel,
        vmem=TUNE.get('vk', 60),
        flops=TUNE.get("project", 6) * 10**9,
        out_shape=jax.ShapeDtypeStruct((tokens.shape[0], width), jnp.bfloat16),
        grid_spec=pltpu.PrefetchScalarGridSpec(
            num_scalar_prefetch=2,
            grid=(steps,),
            in_specs=[pl.BlockSpec((tokens.shape[0], rows), lambda i, o, v: (0, o[i]))]
            + [ANY] * (count + len(others)),
            out_specs=pl.BlockSpec((tokens.shape[0], width), lambda i, o, v: (0, 0)),
            scratch_shapes=[
                pltpu.VMEM((tokens.shape[0], width), jnp.float32),
                pltpu.VMEM((steps, strips, strip, width), jnp.bfloat16),
                pltpu.SemaphoreType.DMA((steps, strips)),
            ],
        ),
    )(owners, valid, tokens, *flat, *others)


def row_blocks(slab_rows):
    return next(k for k in (4, 3, 2, 1) if slab_rows % (16 * k) == 0 or k == 1)


def scalar(value):
    return jnp.reshape(value, (1,)).astype(jnp.int32)


def split_blocks(slab, place, replicas, *others):
    half = replicas // 2
    slab_rows, column_count = slab.shape[0], slab.shape[1] // replicas
    blocks = row_blocks(slab_rows)
    step = slab_rows // blocks

    def kernel(place_ref, slab_ref, *refs):
        keep_ref, send_ref = refs[-2:]
        parity = lax.rem(place_ref[0], 2)
        for j in range(half):
            for out_ref, own in ((keep_ref, parity), (send_ref, 1 - parity)):
                first = pl.multiple_of((2 * j + own) * column_count, column_count)
                out_ref[j] = slab_ref[:, pl.ds(first, column_count)]

    out = jax.ShapeDtypeStruct((half, slab_rows, column_count), slab.dtype)
    return call(
        kernel,
        vmem=TUNE.get("vo", 12),
        flops=int(TUNE.get("columns", 0) * 10**9),
        out_shape=[out, out],
        grid_spec=pltpu.PrefetchScalarGridSpec(
            num_scalar_prefetch=1,
            grid=(blocks,),
            in_specs=[pl.BlockSpec((step, slab.shape[1]), lambda i, place: (i, 0))]
            + [ANY] * len(others),
            out_specs=[pl.BlockSpec((half, step, column_count), lambda i, place: (0, i, 0))] * 2,
        ),
    )(scalar(place), slab, *others)


def pair_sums(keep, came, place, *others):
    half, slab_rows, column_count = keep.shape

    def kernel(place_ref, keep_ref, came_ref, *refs):
        outs = refs[-half:]
        mine = place_ref[0] // 2
        for j in range(half):
            k = mine ^ j
            outs[j][...] = keep_ref[k].astype(jnp.float32) + came_ref[k].astype(jnp.float32)

    out = jax.ShapeDtypeStruct((slab_rows, column_count), jnp.float32)
    whole = pl.BlockSpec(keep.shape, lambda i, place: (0, 0, 0))
    return call(
        kernel,
        vmem=14,
        out_shape=[out] * half,
        grid_spec=pltpu.PrefetchScalarGridSpec(
            num_scalar_prefetch=1,
            grid=(1,),
            in_specs=[whole, whole] + [ANY] * len(others),
            out_specs=[pl.BlockSpec(out.shape, lambda i, place: (0, 0))] * half,
        ),
    )(scalar(place), keep, came, *others)


def outer_update(parts, outer_params, outer_momentum, replicas, *others):
    def kernel(params_ref, momentum_ref, *refs):
        params_out, momentum_out = refs[-2:]
        summed = refs[0][...]
        for part in refs[1 : len(parts)]:
            summed = summed + part[...]
        average = summed / replicas
        params = params_ref[...]
        pseudo_grad = params - average
        new_momentum = OUTER_MOMENTUM * momentum_ref[...] + pseudo_grad
        momentum_out[...] = new_momentum
        params_out[...] = params - OUTER_RATE * (pseudo_grad + OUTER_MOMENTUM * new_momentum)

    whole = pl.BlockSpec(outer_params.shape, lambda: (0, 0))
    return call(
        kernel,
        vmem=12,
        out_shape=[shape_of(outer_params), shape_of(outer_momentum)],
        in_specs=[whole] * (2 + len(parts)) + [ANY] * len(others),
        out_specs=[whole] * 2,
    )(outer_params, outer_momentum, *parts, *others)


def merge(slab, mine, theirs, place):
    half, slab_rows, column_count = mine.shape
    blocks = row_blocks(slab_rows)
    step = slab_rows // blocks

    def kernel(place_ref, slab_ref, mine_ref, theirs_ref, out_ref):
        for j in range(half):
            for ref, owner in ((mine_ref, place_ref[0]), (theirs_ref, place_ref[0] ^ 1)):
                first = pl.multiple_of((owner ^ (2 * j)) * column_count, column_count)
                part = pl.ds(first, column_count)
                slab_f = slab_ref[:, part].astype(jnp.float32)
                merged = MERGE_WEIGHT * slab_f + (1.0 - MERGE_WEIGHT) * ref[j]
                out_ref[:, part] = merged.astype(out_ref.dtype)

    block = pl.BlockSpec((step, slab.shape[1]), lambda i, place: (i, 0))
    outer = pl.BlockSpec((half, step, column_count), lambda i, place: (0, i, 0))
    return call(
        kernel,
        vmem=TUNE.get("vm", 12),
        flops=int(TUNE.get("merge", 3) * 10**9),
        out_shape=shape_of(slab),
        grid_spec=pltpu.PrefetchScalarGridSpec(
            num_scalar_prefetch=1, grid=(blocks,), in_specs=[block, outer, outer], out_specs=block
        ),
    )(scalar(place), slab, mine, theirs)


def shards(
    tokens,
    key_cotangent,
    key_weight,
    first_moment,
    second_moment,
    local_slab,
    outer_params,
    outer_momentum,
):
    n = lax.axis_size("fsdp")
    me = lax.axis_index("fsdp")
    replicas = lax.axis_size("replica")
    rows = key_weight.shape[0]
    strip = rows // PIECES
    scale = term_scale(n * tokens.shape[0])
    every = range(PIECES)

    def mirrored(links):
        return [(n - 1 - a, n - 1 - b) for a, b in links]

    def among(devices):
        return functools.reduce(jnp.logical_or, [me == d for d in devices], jnp.bool_(False))

    def distinct(devices):
        return len(set(devices)) == len(devices)

    def exchange(up_load, down_load, up):
        down = mirrored(up)
        if distinct([a for a, _ in up + down]) and distinct([b for _, b in up + down]):
            load = up_load
            if up_load is not down_load:
                load = jnp.where(among([a for a, _ in up]), up_load, down_load)
            come = lax.ppermute(load, "fsdp", up + down)
            return come, come
        return lax.ppermute(up_load, "fsdp", up), lax.ppermute(down_load, "fsdp", down)

    def one_of(come):
        return come[0].astype(jnp.float32) if come[0] is come[1] else both(come)

    def both(come):
        return come[0].astype(jnp.float32) + come[1].astype(jnp.float32)

    weight_strip = rows // WEIGHT_PIECES
    each = range(WEIGHT_PIECES)
    weights = [key_weight[p * weight_strip : (p + 1) * weight_strip] for p in each]
    held = [[None] * WEIGHT_PIECES for _ in range(n)]
    sums = [None] * PIECES

    for p in each:
        held[0][p] = exchange(weights[p], weights[p], [(i, i + 1) for i in range(n - 1)])
    place = lax.axis_index("replica")

    def columns_of(owner, p):
        first = jnp.clip(owner, 0, n - 1) * rows + p * strip
        return lax.dynamic_slice_in_dim(tokens, first, strip, 1)

    def term(columns, cotangent):
        return scale * lax.dot_general(
            columns, cotangent, (((0,), (0,)), ((), ())), preferred_element_type=jnp.float32
        )

    if TUNE.get("gate") is not None:
        first_owner = jnp.where(me < 1, n + me - 1, 0 - (n - 1 - me))
        firsts = [after(term(columns_of(first_owner, q), key_cotangent)) for q in every]

    def swap(array, k):
        return lax.ppermute(array, "replica", [(i, i ^ k) for i in range(replicas)])

    late = tuple(firsts) if TUNE.get("late", 0) else ()
    keep, send = split_blocks(local_slab, place, replicas, *late)
    pairs = pair_sums(keep, swap(send, 1), place)
    parts = [pairs[0]] + [swap(pairs[j], 2 * j) for j in range(1, replicas // 2)]
    if TUNE.get("outer_tie") is not None:
        parts[0] = after(parts[0], *held[TUNE["outer_tie"]][0])
    new_outer, new_momentum = outer_update(parts, outer_params, outer_momentum, replicas)
    mine = [new_outer] + [swap(new_outer, 2 * j) for j in range(1, replicas // 2)]

    cotangent = key_cotangent
    for t in range(1, n):
        links = [(i, i + 1) for i in range(t)]
        up, down = n + me - t, t - 1 - (n - 1 - me)
        owners = [jnp.where(me < t, up, down)] if 2 * t <= n else [up, down]
        for p in every:
            w = p * WEIGHT_PIECES // PIECES
            if t == 1 and p == 0 and TUNE.get("gate") is not None:
                for v in each:
                    first = after(held[0][v][0], *firsts, flops=TUNE["gate"] * 10**9)
                    second = first if held[0][v][1] is held[0][v][0] else after(held[0][v][1], *firsts)
                    held[0][v] = (first, second)
            came = held[t - 1][w]
            if t < n - 1 and held[t][w] is None:
                held[t][w] = exchange(*came, [(i, i + 1) for i in range(t, n - 1)])
            if (t, p) == TUNE.get("mine_after"):
                mine[0] = after(mine[0], *came)
            extra = ()
            if (t, p) == TUNE.get("pairs_before"):
                extra = (pairs[0],)
            if (t, p) == TUNE.get("outer_before"):
                extra = (new_outer,)
            if (t, p) == TUNE.get("mine_before"):
                extra = tuple(mine[1:])
            tie = TUNE.get(("tie", t, p), t - 1)
            others = () if tie is None else tuple(held[tie][w])
            cost = TUNE.get(("x", t, p), 0) * 10**9
            source = cotangent if TUNE.get("chain", 0) else key_cotangent
            others = (*others, *extra)
            if others or cost:
                source = after(source, *others, flops=cost)
                cotangent = source
            if t == 1 and TUNE.get("gate") is not None:
                loads = [firsts[p]]
            else:
                loads = [term(columns_of(owner, p), source) for owner in owners]
            if len(loads) == 1:
                load = loads[0] if t == 1 else loads[0] + one_of(sums[p])
                up_load = down_load = load.astype(jnp.float16)
            else:
                up_load = (loads[0] + sums[p][0].astype(jnp.float32)).astype(jnp.float16)
                down_load = (loads[1] + sums[p][1].astype(jnp.float32)).astype(jnp.float16)
            sums[p] = exchange(up_load, down_load, links)

    mine = jnp.stack(mine)
    theirs = swap(mine, 1)
    new_local = merge(local_slab, mine, theirs, place)

    owners, valid, steps = [me], [me >= 0], [weights]
    for t in range(n - 1):
        if held[t][0][0] is held[t][0][1]:
            owners.append(jnp.where(me - t - 1 >= 0, me - t - 1, me + t + 1))
            valid.append((me - t - 1 >= 0) | (me + t + 1 <= n - 1))
            steps.append([held[t][p][0] for p in each])
        else:
            owners += [me - t - 1, me + t + 1]
            valid += [me - t - 1 >= 0, me + t + 1 <= n - 1]
            steps += [[held[t][p][0] for p in each], [held[t][p][1] for p in each]]
    owners = jnp.clip(jnp.stack(owners), 0, n - 1).astype(jnp.int32)
    others = (new_local,) if TUNE.get("merge_first", 1) else ()
    projected = project(owners, jnp.stack(valid).astype(jnp.int32), tokens, steps, rows, *others)

    source = after(key_cotangent, projected)
    own = [term(columns_of(me, p), source) for p in every]
    gradient = jnp.concatenate([own[p] + one_of(sums[p]) for p in every], 0) / scale
    new_first = BETA_ONE * first_moment + (1.0 - BETA_ONE) * gradient
    new_second = BETA_TWO * second_moment + (1.0 - BETA_TWO) * gradient * gradient
    weight_f = key_weight.astype(jnp.float32)
    update = (
        new_first / FIRST_FIX / (jnp.sqrt(new_second / SECOND_FIX) + EPSILON)
        + DECAY_RATE * weight_f
    )
    new_weight = (weight_f - INNER_RATE * update).astype(jnp.bfloat16)
    return (projected, new_weight, new_first, new_second, new_outer, new_momentum, new_local)


def solution(mesh):
    split = P(("replica", "fsdp"), None)
    outer = P("fsdp", "replica")
    return jax.shard_map(
        shards,
        mesh=mesh,
        in_specs=(split, split, split, split, split, split, outer, outer),
        out_specs=(split, split, split, split, outer, outer, split),
        check_vma=False,
    )
```

time: 179 us -> 125 us (0.70)
  waiting for transfers between devices: 52.4 us -> 32.2 us
  Pallas kernels: 29.4 us -> 12.1 us
  other arithmetic: 21.1 us -> 5.1 us
  between operations: 14.5 us -> 1.22 us
  matrix products: 0 us -> 7.01 us
  starting transfers between devices: 53.4 us -> 57.6 us
    ppermute x3 -> x4, waiting for transfers between devices: 22 us -> 3.42 us  [exchange(): come = lax.ppermute(load, 'fsdp', up + down)]
    pallas_call x5, Pallas kernels: 29.4 us -> 12.1 us  [the longest x1 6.16 us: project(): call(kernel, vmem=TUNE.get('vk', 60), flops=TUNE.get('project', 6) * 10 *...]
    ppermute x6 -> x8, waiting for transfers between devices: 29 us -> 18.5 us  [exchange(): lax.ppermute(down_load, 'fsdp', down)]
    convert_element_type x8 -> x0, other arithmetic: 10.5 us -> none  [the longest x4 7.4 us: shards(): up_load = down_load = load.astype(jnp.float16)]
    ppermute x0 -> x8, starting transfers between devices: none -> 8.57 us  [swap(): return lax.ppermute(array, 'replica', [(i, i ^ k) for i in range(replicas)])]
    dot_general x0 -> x10, matrix products: none -> 7.01 us  [term(): lax.dot_general(columns, cotangent, (((0,), (0,)), ((), ())), preferred_e...]
    ppermute x0 -> x8, waiting for transfers between devices: none -> 4.59 us  [swap(): return lax.ppermute(array, 'replica', [(i, i ^ k) for i in range(replicas)])]
    ppermute x6 -> x8, waiting for transfers between devices: 1.35 us -> 5.75 us  [exchange(): lax.ppermute(up_load, 'fsdp', up)]
  transfers between devices with their start and end apart: 17 -> 28, of which waited for: 5 -> 10; matrix products, arithmetic and copies ran while one was open for 9% -> 7% of each run, Pallas kernels for 10% -> 10%
where the time goes in v3:
time: 125 us; the launch traced here: 124 us
  starting transfers between devices  57.6 us (46%)
  waiting for transfers between devices  32.2 us (26%)
  Pallas kernels  12.1 us (10%)
  local copies, waits for them, and re-layouts  8.5 us (7%)
  matrix products  7.01 us (6%)
  other arithmetic  5.1 us (4%)
    ppermute x8, starting transfers between devices, exchange(): lax.ppermute(up_load, 'fsdp', up)  31.3 us
    ppermute x8, waiting for transfers between devices, exchange(): lax.ppermute(down_load, 'fsdp', down)  18.5 us
    ppermute x8, starting transfers between devices, exchange(): lax.ppermute(down_load, 'fsdp', down)  9.24 us
    ppermute x8, starting transfers between devices, swap(): return lax.ppermute(array, 'replica', [(i, i ^ k) for i in range(replicas)])  8.57 us
    ppermute x4, starting transfers between devices, exchange(): come = lax.ppermute(load, 'fsdp', up + down)  8.46 us
    dot_general x10, matrix products, term(): lax.dot_general(columns, cotangent, (((0,), (0,)), ((), ())), preferred_e...  7.01 us
    pallas_call x1, Pallas kernels, project(): call(kernel, vmem=TUNE.get('vk', 60), flops=TUNE.get('project', 6) * 10 *...  6.16 us
    unnamed x24, local copies, waits for them, and re-layouts  6.08 us
  transfers between devices with their start and end apart: 28, of which 10 were waited for; matrix products, arithmetic and copies ran while one was open for 7% of the time, Pallas kernels for 10%

profile of v3, /device:TPU:0, one launch (start us, length us, event | category | flops | bytes accessed | tf_op | source)
XLA Modules:
  0.0 123.9 jit_solution(49237459993619362)
XLA Ops:
  0.6 1.2 copy.26.refs_0_
  1.8 2.2 %fusion.39 = (bf16[512,512]{1,0:T(8,128)(2,1)}, bf16[512,512]{1,0:T(8,128)(2,1)}) fusion(bf16[1024,512]{1,0:T(8,128)(2,1)} %param.10), kind=kLoop, calls=%fused_computation.58 | loop fusion | bytes 2097152 | tf_op jit(solution)/shard_map/slice | solution.py:280
  4.0 5.7 %collective-permute-start = (bf16[512,512]{1,0:T(8,128)(2,1)}, bf16[512,512]{1,0:T(8,128)(2,1)}, u32[]{:S(2)}, u32[]{:S(2)}) collective-permute-start(bf16[512,512]{1,0:T(8,128)(2,1)} %get-tuple-element.27.refs_0_), channel_id=1, source_target_pairs={{0,1},{1,2},{2,3},{4,5},{5,6},{6,7},{8,9},{9,10},{10,11},{12,13},{... | collective-permute-start | bytes 1572872 | tf_op jit(solution)/shard_map/ppermute | solution.py:270
  9.8 1.3 %collective-permute-start.2 = (bf16[512,512]{1,0:T(8,128)(2,1)}, bf16[512,512]{1,0:T(8,128)(2,1)}, u32[]{:S(2)}, u32[]{:S(2)}) collective-permute-start(bf16[512,512]{1,0:T(8,128)(2,1)} %get-tuple-element.27.refs_0_), channel_id=1, source_target_pairs={{3,2},{2,1},{1,0},{7,6},{6,5},{5,4},{11,10},{10,9},{9,8},{15,14},{... | collective-permute-start | bytes 1572872 | tf_op jit(solution)/shard_map/ppermute | solution.py:270
  11.1 1.5 %shard_map.135 = (bf16[4,192,512]{2,1,0:T(8,128)(2,1)S(1)}, bf16[4,192,512]{2,1,0:T(8,128)(2,1)}) custom-call(s32[1]{0:T(128)} %bitcast.12.place_ref, bf16[192,4096]{1,0:T(8,128)(2,1)S(1)} %copy-done), custom_call_target="tpu_custom_call" | custom-call | tf_op jit(solution)/shard_map/pallas_call | solution.py:145
  12.6 5.3 %collective-permute-start.1 = (bf16[512,512]{1,0:T(8,128)(2,1)}, bf16[512,512]{1,0:T(8,128)(2,1)}, u32[]{:S(2)}, u32[]{:S(2)}) collective-permute-start(bf16[512,512]{1,0:T(8,128)(2,1)} %get-tuple-element.26.refs_1_), channel_id=1, source_target_pairs={{0,1},{1,2},{2,3},{4,5},{5,6},{6,7},{8,9},{9,10},{10,11},{12,13},{... | collective-permute-start | bytes 1572872 | tf_op jit(solution)/shard_map/ppermute | solution.py:270
  18.0 1.3 %collective-permute-start.3 = (bf16[512,512]{1,0:T(8,128)(2,1)}, bf16[512,512]{1,0:T(8,128)(2,1)}, u32[]{:S(2)}, u32[]{:S(2)}) collective-permute-start(bf16[512,512]{1,0:T(8,128)(2,1)} %get-tuple-element.26.refs_1_), channel_id=1, source_target_pairs={{3,2},{2,1},{1,0},{7,6},{6,5},{5,4},{11,10},{10,9},{9,8},{15,14},{... | collective-permute-start | bytes 1572872 | tf_op jit(solution)/shard_map/ppermute | solution.py:270
  19.3 2.3 %collective-permute-done.refs_2_ = bf16[512,512]{1,0:T(8,128)(2,1)} collective-permute-done((bf16[512,512]{1,0:T(8,128)(2,1)}, bf16[512,512]{1,0:T(8,128)(2,1)}, u32[]{:S(2)}, u32[]{:S(2)}) %collective-permute-start) | collective-permute-done | bytes 524320 | tf_op jit(solution)/shard_map/ppermute | solution.py:270
  22.3 4.5 %collective-permute-done.2.refs_4_ = bf16[512,512]{1,0:T(8,128)(2,1)} collective-permute-done((bf16[512,512]{1,0:T(8,128)(2,1)}, bf16[512,512]{1,0:T(8,128)(2,1)}, u32[]{:S(2)}, u32[]{:S(2)}) %collective-permute-start.2) | collective-permute-done | bytes 524320 | tf_op jit(solution)/shard_map/ppermute | solution.py:270
  26.8 1.3 %collective-permute-start.6 = (bf16[512,512]{1,0:T(8,128)(2,1)}, bf16[512,512]{1,0:T(8,128)(2,1)}, u32[]{:S(2)}, u32[]{:S(2)}) collective-permute-start(bf16[512,512]{1,0:T(8,128)(2,1)} %collective-permute-done.2.refs_4_), channel_id=1, source_target_pairs={{2,1},{1,0},{6,5},{5,4},{10,9},{9,8},{14,13},{13,12},{18,17},{17,1... | collective-permute-start | bytes 1572872 | tf_op jit(solution)/shard_map/ppermute | solution.py:270
  28.3 0.8 copy.21.refs_0_
  29.1 1.5 %fusion.17 = f16[512,512]{1,0:T(8,128)(2,1)S(1)} fusion(bf16[512,512]{1,0:T(8,128)(2,1)S(1)} %copy.26.refs_0_, bf16[512,4096]{1,0:T(8,128)(2,1)} %tokens_ref.1, s32[]{:T(128)S(6)} %select_n.61), kind=kOutput, calls=%fused_computation.33 | convolution fusion | flops 268959744 | bytes 1572868 | tf_op jit(solution)/shard_map/dot_general | solution.py:293
  30.6 1.6 %fusion.18 = f16[512,512]{1,0:T(8,128)(2,1)S(1)} fusion(bf16[512,512]{1,0:T(8,128)(2,1)S(1)} %copy.26.refs_0_, bf16[512,4096]{1,0:T(8,128)(2,1)} %tokens_ref.1, s32[]{:T(128)S(6)} %select_n.66), kind=kOutput, calls=%fused_computation.34 | convolution fusion | flops 268959744 | bytes 1572868 | tf_op jit(solution)/shard_map/dot_general | solution.py:293
  32.2 4.6 %collective-permute-start.18 = (f16[512,512]{1,0:T(8,128)(2,1)S(1)}, f16[512,512]{1,0:T(8,128)(2,1)S(1)}, u32[]{:S(2)}, u32[]{:S(2)}) collective-permute-start(f16[512,512]{1,0:T(8,128)(2,1)S(1)} %fusion.17), channel_id=1, source_target_pairs={{0,1},{3,2},{4,5},{7,6},{8,9},{11,10},{12,13},{15,14},{16,17},{19,... | collective-permute-start | bytes 1572872 | tf_op jit(solution)/shard_map/ppermute | solution.py:268
  36.8 1.3 %shard_map.136 = (f32[192,512]{1,0:T(8,128)S(1)}, f32[192,512]{1,0:T(8,128)S(1)}, f32[192,512]{1,0:T(8,128)S(1)}, f32[192,512]{1,0:T(8,128)S(1)}) custom-call(s32[1]{0:T(128)} %bitcast.12.place_ref, bf16[4,192,512]{2,1,0:T(8,128)(2,1)S(1)} %get-tuple-element.15.keep_ref, bf16[4,192,512]{2,1,0:T(8,128)(2,1)} %collective-permute-done.10.came_ref), custom_call_target="tpu_custom_call" | custom-call | tf_op jit(solution)/shard_map/pallas_call | solution.py:172
  38.1 1.3 %collective-permute-start.23 = (f16[512,512]{1,0:T(8,128)(2,1)S(1)}, f16[512,512]{1,0:T(8,128)(2,1)S(1)}, u32[]{:S(2)}, u32[]{:S(2)}) collective-permute-start(f16[512,512]{1,0:T(8,128)(2,1)S(1)} %fusion.18), channel_id=1, source_target_pairs={{0,1},{3,2},{4,5},{7,6},{8,9},{11,10},{12,13},{15,14},{16,17},{19,... | collective-permute-start | bytes 1572872 | tf_op jit(solution)/shard_map/ppermute | solution.py:268
  39.4 0.7 collective-permute-start.5
  40.1 1.3 %collective-permute-start.7 = (bf16[512,512]{1,0:T(8,128)(2,1)}, bf16[512,512]{1,0:T(8,128)(2,1)S(1)}, u32[]{:S(2)}, u32[]{:S(2)}) collective-permute-start(bf16[512,512]{1,0:T(8,128)(2,1)} %collective-permute-done.3.refs_5_), channel_id=1, source_target_pairs={{2,1},{1,0},{6,5},{5,4},{10,9},{9,8},{14,13},{13,12},{18,17},{17,1... | collective-permute-start | bytes 1572872 | tf_op jit(solution)/shard_map/ppermute | solution.py:270
  41.4 7.6 %collective-permute-done.6.refs_8_.refs_2_ = bf16[512,512]{1,0:T(8,128)(2,1)} collective-permute-done((bf16[512,512]{1,0:T(8,128)(2,1)}, bf16[512,512]{1,0:T(8,128)(2,1)}, u32[]{:S(2)}, u32[]{:S(2)}) %collective-permute-start.6) | collective-permute-done | bytes 524320 | tf_op jit(solution)/shard_map/ppermute | solution.py:270
  49.1 1.5 %collective-permute-start.11 = (f32[192,512]{1,0:T(8,128)S(1)}, f32[192,512]{1,0:T(8,128)S(1)}, u32[]{:S(2)}, u32[]{:S(2)}) collective-permute-start(f32[192,512]{1,0:T(8,128)S(1)} %get-tuple-element.18), channel_id=1, source_target_pairs={{0,8},{4,12},{8,0},{12,4},{16,24},{20,28},{24,16},{28,20},{1,9},{5... | collective-permute-start | bytes 1179656 | tf_op jit(solution)/shard_map/ppermute | solution.py:302
  50.6 1.1 broadcast_select_fusion.1
  51.7 1.6 %collective-permute-start.12 = (f32[192,512]{1,0:T(8,128)S(1)}, f32[192,512]{1,0:T(8,128)S(1)}, u32[]{:S(2)}, u32[]{:S(2)}) collective-permute-start(f32[192,512]{1,0:T(8,128)S(1)} %get-tuple-element.19), channel_id=1, source_target_pairs={{0,16},{4,20},{8,24},{12,28},{16,0},{20,4},{24,8},{28,12},{1,17},{... | collective-permute-start | bytes 1179656 | tf_op jit(solution)/shard_map/ppermute | solution.py:302
  53.8 0.8 collective-permute-start.13
  54.6 4.4 %collective-permute-done.7.refs_9_.refs_2_ = bf16[512,512]{1,0:T(8,128)(2,1)S(1)} collective-permute-done((bf16[512,512]{1,0:T(8,128)(2,1)}, bf16[512,512]{1,0:T(8,128)(2,1)S(1)}, u32[]{:S(2)}, u32[]{:S(2)}) %collective-permute-start.7) | collective-permute-done | bytes 524320 | tf_op jit(solution)/shard_map/ppermute | solution.py:270
  58.9 1.3 %collective-permute-start.8 = (bf16[512,512]{1,0:T(8,128)(2,1)S(1)}, bf16[512,512]{1,0:T(8,128)(2,1)S(1)}, u32[]{:S(2)}, u32[]{:S(2)}) collective-permute-start(bf16[512,512]{1,0:T(8,128)(2,1)S(1)} %broadcast_select_fusion.1), channel_id=1, source_target_pairs={{2,3},{1,0},{6,7},{5,4},{10,11},{9,8},{14,15},{13,12},{18,19},{17,... | collective-permute-start | bytes 1572872 | tf_op jit(solution)/shard_map/ppermute | solution.py:268
  60.3 0.8 collective-permute-start.21
  61.7 5.2 %collective-permute-start.19 = (f16[512,512]{1,0:T(8,128)(2,1)S(1)}, f16[512,512]{1,0:T(8,128)(2,1)S(1)}, u32[]{:S(2)}, u32[]{:S(2)}) collective-permute-start(f16[512,512]{1,0:T(8,128)(2,1)S(1)} %fusion.12), channel_id=1, source_target_pairs={{0,1},{1,2},{4,5},{5,6},{8,9},{9,10},{12,13},{13,14},{16,17},{17,1... | collective-permute-start | bytes 1572872 | tf_op jit(solution)/shard_map/ppermute | solution.py:270
  66.9 1.4 %collective-permute-done.12.refs_2_ = f32[192,512]{1,0:T(8,128)S(1)} collective-permute-done((f32[192,512]{1,0:T(8,128)S(1)}, f32[192,512]{1,0:T(8,128)S(1)}, u32[]{:S(2)}, u32[]{:S(2)}) %collective-permute-start.12) | collective-permute-done | bytes 393248 | tf_op jit(solution)/shard_map/ppermute | solution.py:302
  68.3 1.3 %collective-permute-start.9 = (bf16[512,512]{1,0:T(8,128)(2,1)S(1)}, bf16[512,512]{1,0:T(8,128)(2,1)S(1)}, u32[]{:S(2)}, u32[]{:S(2)}) collective-permute-start(bf16[512,512]{1,0:T(8,128)(2,1)S(1)} %broadcast_select_fusion), channel_id=1, source_target_pairs={{2,3},{1,0},{6,7},{5,4},{10,11},{9,8},{14,15},{13,12},{18,19},{17,... | collective-permute-start | bytes 1572872 | tf_op jit(solution)/shard_map/ppermute | solution.py:268
  69.7 1.0 shard_map.137
  70.7 1.6 %collective-permute-start.16 = (f32[192,512]{1,0:T(8,128)}, f32[192,512]{1,0:T(8,128)S(1)}, u32[]{:S(2)}, u32[]{:S(2)}) collective-permute-start(f32[192,512]{1,0:T(8,128)} %get-tuple-element.12), channel_id=1, source_target_pairs={{0,24},{4,28},{8,16},{12,20},{16,8},{20,12},{24,0},{28,4},{1,25},{... | collective-permute-start | bytes 1179656 | tf_op jit(solution)/shard_map/ppermute | solution.py:302
  72.3 3.4 %collective-permute-done.8.refs_10_.refs_1_.refs_2_ = bf16[512,512]{1,0:T(8,128)(2,1)S(1)} collective-permute-done((bf16[512,512]{1,0:T(8,128)(2,1)S(1)}, bf16[512,512]{1,0:T(8,128)(2,1)S(1)}, u32[]{:S(2)}, u32[]{:S(2)}) %collective-permute-start.8) | collective-permute-done | bytes 524320 | tf_op jit(solution)/shard_map/ppermute | solution.py:268
  75.7 1.5 %collective-permute-start.15 = (f32[192,512]{1,0:T(8,128)}, f32[192,512]{1,0:T(8,128)S(1)}, u32[]{:S(2)}, u32[]{:S(2)}) collective-permute-start(f32[192,512]{1,0:T(8,128)} %get-tuple-element.12), channel_id=1, source_target_pairs={{0,16},{4,20},{8,24},{12,28},{16,0},{20,4},{24,8},{28,12},{1,17},{... | collective-permute-start | bytes 1179656 | tf_op jit(solution)/shard_map/ppermute | solution.py:302
  77.2 1.5 %collective-permute-start.14 = (f32[192,512]{1,0:T(8,128)S(1)}, f32[192,512]{1,0:T(8,128)S(1)}, u32[]{:S(2)}, u32[]{:S(2)}) collective-permute-start(f32[192,512]{1,0:T(8,128)S(1)} %copy-done.10), channel_id=1, source_target_pairs={{0,8},{4,12},{8,0},{12,4},{16,24},{20,28},{24,16},{28,20},{1,9},{5... | collective-permute-start | bytes 1179656 | tf_op jit(solution)/shard_map/ppermute | solution.py:302
  80.4 3.1 %collective-permute-done.16 = f32[192,512]{1,0:T(8,128)S(1)} collective-permute-done((f32[192,512]{1,0:T(8,128)}, f32[192,512]{1,0:T(8,128)S(1)}, u32[]{:S(2)}, u32[]{:S(2)}) %collective-permute-start.16) | collective-permute-done | bytes 393248 | tf_op jit(solution)/shard_map/ppermute | solution.py:302
  83.6 4.7 %collective-permute-start.24 = (f16[512,512]{1,0:T(8,128)(2,1)S(1)}, f16[512,512]{1,0:T(8,128)(2,1)S(1)}, u32[]{:S(2)}, u32[]{:S(2)}) collective-permute-start(f16[512,512]{1,0:T(8,128)(2,1)S(1)} %fusion.15), channel_id=1, source_target_pairs={{0,1},{1,2},{4,5},{5,6},{8,9},{9,10},{12,13},{13,14},{16,17},{17,1... | collective-permute-start | bytes 1572872 | tf_op jit(solution)/shard_map/ppermute | solution.py:270
  88.3 1.3 %collective-permute-start.22 = (f16[512,512]{1,0:T(8,128)(2,1)S(1)}, f16[512,512]{1,0:T(8,128)(2,1)S(1)}, u32[]{:S(2)}, u32[]{:S(2)}) collective-permute-start(f16[512,512]{1,0:T(8,128)(2,1)S(1)} %fusion.13), channel_id=1, source_target_pairs={{3,2},{2,1},{1,0},{7,6},{6,5},{5,4},{11,10},{10,9},{9,8},{15,14},{... | collective-permute-start | bytes 1572872 | tf_op jit(solution)/shard_map/ppermute | solution.py:270
  89.6 4.6 %collective-permute-start.20 = (f16[512,512]{1,0:T(8,128)(2,1)S(1)}, f16[512,512]{1,0:T(8,128)(2,1)S(1)}, u32[]{:S(2)}, u32[]{:S(2)}) collective-permute-start(f16[512,512]{1,0:T(8,128)(2,1)S(1)} %fusion.11), channel_id=1, source_target_pairs={{0,1},{1,2},{2,3},{4,5},{5,6},{6,7},{8,9},{9,10},{10,11},{12,13},{... | collective-permute-start | bytes 1572872 | tf_op jit(solution)/shard_map/ppermute | solution.py:270
  94.9 1.3 %collective-permute-start.27 = (f16[512,512]{1,0:T(8,128)(2,1)S(1)}, f16[512,512]{1,0:T(8,128)(2,1)S(1)}, u32[]{:S(2)}, u32[]{:S(2)}) collective-permute-start(f16[512,512]{1,0:T(8,128)(2,1)S(1)} %fusion.16), channel_id=1, source_target_pairs={{3,2},{2,1},{1,0},{7,6},{6,5},{5,4},{11,10},{10,9},{9,8},{15,14},{... | collective-permute-start | bytes 1572872 | tf_op jit(solution)/shard_map/ppermute | solution.py:270
  97.2 4.4 %collective-permute-start.25 = (f16[512,512]{1,0:T(8,128)(2,1)S(1)}, f16[512,512]{1,0:T(8,128)(2,1)S(1)}, u32[]{:S(2)}, u32[]{:S(2)}) collective-permute-start(f16[512,512]{1,0:T(8,128)(2,1)S(1)} %fusion.14), channel_id=1, source_target_pairs={{0,1},{1,2},{2,3},{4,5},{5,6},{6,7},{8,9},{9,10},{10,11},{12,13},{... | collective-permute-start | bytes 1572872 | tf_op jit(solution)/shard_map/ppermute | solution.py:270
  101.6 2.1 %shard_map.138.refs_12_ = bf16[192,4096]{1,0:T(8,128)(2,1)} custom-call(s32[1]{0:T(128)} %bitcast.12.place_ref, bf16[192,4096]{1,0:T(8,128)(2,1)S(1)} %copy-done, f32[4,192,512]{2,1,0:T(8,128)S(1)} %pad_maximum_fusion.1.mine_ref, f32[4,192,512]{2,1,0:T(8,128)S(1)} %collective-permute-done.17.theirs_ref), custom_call_target="tpu_custom_call" | custom-call | flops 3000000000 | tf_op jit(solution)/shard_map/pallas_call | solution.py:224
  103.8 1.4 %copy-done.6 = bf16[192,4096]{1,0:T(8,128)(2,1)S(1)} copy-done((bf16[192,4096]{1,0:T(8,128)(2,1)S(1)}, bf16[192,4096]{1,0:T(8,128)(2,1)}, u32[]{:S(2)}) %copy-start.6) | copy-done | bytes 1572888
  105.2 6.2 %shard_map.139.refs_1_ = bf16[512,512]{1,0:T(8,128)(2,1)} custom-call(s32[6]{0:T(128)S(1)} %broadcast_clamp_fusion.owners_ref, s32[6]{0:T(128)S(1)} %convert_element_type.63.valid_ref, bf16[512,4096]{1,0:T(8,128)(2,1)S(1)} %copy-done.5, bf16[512,512]{1,0:T(8,128)(2,1)} %get-tuple-element.27.refs_0_, bf16[512,512]{1,0:T(8,128)(2,1)} %get-tuple-element.26.refs_1_, ...), custom_call_target="tpu_custom_call" | custom-call | flops 6000000000 | tf_op jit(solution)/shard_map/pallas_call | solution.py:102
  111.4 1.0 copy-done.1
  112.4 2.0 %collective-permute-done.27 = f16[512,512]{1,0:T(8,128)(2,1)S(1)} collective-permute-done((f16[512,512]{1,0:T(8,128)(2,1)S(1)}, f16[512,512]{1,0:T(8,128)(2,1)S(1)}, u32[]{:S(2)}, u32[]{:S(2)}) %collective-permute-start.27) | collective-permute-done | bytes 524320 | tf_op jit(solution)/shard_map/ppermute | solution.py:270
  114.4 3.0 %collective-permute-done.25 = f16[512,512]{1,0:T(8,128)(2,1)S(1)} collective-permute-done((f16[512,512]{1,0:T(8,128)(2,1)S(1)}, f16[512,512]{1,0:T(8,128)(2,1)S(1)}, u32[]{:S(2)}, u32[]{:S(2)}) %collective-permute-start.25) | collective-permute-done | bytes 524320 | tf_op jit(solution)/shard_map/ppermute | solution.py:270
  119.4 0.7 copy-done.8
  120.1 3.8 %fusion.2 = (bf16[1024,512]{1,0:T(8,128)(2,1)}, f32[1024,512]{1,0:T(8,128)}, f32[1024,512]{1,0:T(8,128)}) fusion(bf16[1024,512]{1,0:T(8,128)(2,1)S(1)} %copy-done.7, f32[512,512]{1,0:T(8,128)S(1)} %fusion.6, f32[512,512]{1,0:T(8,128)S(1)} %fusion.10, f32[1024,512]{1,0:T(8,128)S(1)} %copy-done.8, f32[1024,512]{1,0:T(8,128)S(1)} %copy-done.9), kind=kLoop, calls=%fused_computation.4 | loop fusion | flops 9961472 | bytes 12582912 | tf_op jit(solution)/shard_map/convert_element_type | solution.py:385
  (61 shorter events, 7.3 us)
Async XLA Ops:
  0.6 10.4 %copy-start = (bf16[192,4096]{1,0:T(8,128)(2,1)S(1)}, bf16[192,4096]{1,0:T(8,128)(2,1)}, u32[]{:S(2)}) copy-start(bf16[192,4096]{1,0:T(8,128)(2,1)} %slab_ref.3) | copy-start | bytes 4718596
  4.0 17.6 %collective-permute-start = (bf16[512,512]{1,0:T(8,128)(2,1)}, bf16[512,512]{1,0:T(8,128)(2,1)}, u32[]{:S(2)}, u32[]{:S(2)}) collective-permute-start(bf16[512,512]{1,0:T(8,128)(2,1)} %get-tuple-element.27.refs_0_), channel_id=1, source_target_pairs={{0,1},{1,2},{2,3},{4,5},{5,6},{6,7},{8,9},{9,10},{10,11},{12,13},{... | collective-permute-start | bytes 1572872 | tf_op jit(solution)/shard_map/ppermute | solution.py:270
  9.8 17.0 %collective-permute-start.2 = (bf16[512,512]{1,0:T(8,128)(2,1)}, bf16[512,512]{1,0:T(8,128)(2,1)}, u32[]{:S(2)}, u32[]{:S(2)}) collective-permute-start(bf16[512,512]{1,0:T(8,128)(2,1)} %get-tuple-element.27.refs_0_), channel_id=1, source_target_pairs={{3,2},{2,1},{1,0},{7,6},{6,5},{5,4},{11,10},{10,9},{9,8},{15,14},{... | collective-permute-start | bytes 1572872 | tf_op jit(solution)/shard_map/ppermute | solution.py:270
  12.6 19.6 %collective-permute-start.10 = (bf16[4,192,512]{2,1,0:T(8,128)(2,1)}, bf16[4,192,512]{2,1,0:T(8,128)(2,1)}, u32[]{:S(2)}, u32[]{:S(2)}) collective-permute-start(bf16[4,192,512]{2,1,0:T(8,128)(2,1)} %get-tuple-element.16), channel_id=1, source_target_pairs={{0,4},{4,0},{8,12},{12,8},{16,20},{20,16},{24,28},{28,24},{1,5},{5... | collective-permute-start | bytes 2359304 | tf_op jit(solution)/shard_map/ppermute | solution.py:302
  12.6 25.5 %collective-permute-start.1 = (bf16[512,512]{1,0:T(8,128)(2,1)}, bf16[512,512]{1,0:T(8,128)(2,1)}, u32[]{:S(2)}, u32[]{:S(2)}) collective-permute-start(bf16[512,512]{1,0:T(8,128)(2,1)} %get-tuple-element.26.refs_1_), channel_id=1, source_target_pairs={{0,1},{1,2},{2,3},{4,5},{5,6},{6,7},{8,9},{9,10},{10,11},{12,13},{... | collective-permute-start | bytes 1572872 | tf_op jit(solution)/shard_map/ppermute | solution.py:270
  18.0 21.5 %collective-permute-start.3 = (bf16[512,512]{1,0:T(8,128)(2,1)}, bf16[512,512]{1,0:T(8,128)(2,1)}, u32[]{:S(2)}, u32[]{:S(2)}) collective-permute-start(bf16[512,512]{1,0:T(8,128)(2,1)} %get-tuple-element.26.refs_1_), channel_id=1, source_target_pairs={{3,2},{2,1},{1,0},{7,6},{6,5},{5,4},{11,10},{10,9},{9,8},{15,14},{... | collective-permute-start | bytes 1572872 | tf_op jit(solution)/shard_map/ppermute | solution.py:270
  21.6 18.5 %collective-permute-start.4 = (bf16[512,512]{1,0:T(8,128)(2,1)}, bf16[512,512]{1,0:T(8,128)(2,1)S(1)}, u32[]{:S(2)}, u32[]{:S(2)}) collective-permute-start(bf16[512,512]{1,0:T(8,128)(2,1)} %collective-permute-done.refs_2_), channel_id=1, source_target_pairs={{1,2},{2,3},{5,6},{6,7},{9,10},{10,11},{13,14},{14,15},{17,18},{18... | collective-permute-start | bytes 1572872 | tf_op jit(solution)/shard_map/ppermute | solution.py:270
  26.8 22.2 %collective-permute-start.6 = (bf16[512,512]{1,0:T(8,128)(2,1)}, bf16[512,512]{1,0:T(8,128)(2,1)}, u32[]{:S(2)}, u32[]{:S(2)}) collective-permute-start(bf16[512,512]{1,0:T(8,128)(2,1)} %collective-permute-done.2.refs_4_), channel_id=1, source_target_pairs={{2,1},{1,0},{6,5},{5,4},{10,9},{9,8},{14,13},{13,12},{18,17},{17,1... | collective-permute-start | bytes 1572872 | tf_op jit(solution)/shard_map/ppermute | solution.py:270
  30.6 20.0 %copy-start.2 = (bf16[512,512]{1,0:T(8,128)(2,1)S(1)}, bf16[512,512]{1,0:T(8,128)(2,1)}, u32[]{:S(2)}) copy-start(bf16[512,512]{1,0:T(8,128)(2,1)} %copy.21.refs_0_) | copy-start | bytes 1572868
  32.2 19.5 %collective-permute-start.18 = (f16[512,512]{1,0:T(8,128)(2,1)S(1)}, f16[512,512]{1,0:T(8,128)(2,1)S(1)}, u32[]{:S(2)}, u32[]{:S(2)}) collective-permute-start(f16[512,512]{1,0:T(8,128)(2,1)S(1)} %fusion.17), channel_id=1, source_target_pairs={{0,1},{3,2},{4,5},{7,6},{8,9},{11,10},{12,13},{15,14},{16,17},{19,... | collective-permute-start | bytes 1572872 | tf_op jit(solution)/shard_map/ppermute | solution.py:268
  38.1 22.3 %collective-permute-start.23 = (f16[512,512]{1,0:T(8,128)(2,1)S(1)}, f16[512,512]{1,0:T(8,128)(2,1)S(1)}, u32[]{:S(2)}, u32[]{:S(2)}) collective-permute-start(f16[512,512]{1,0:T(8,128)(2,1)S(1)} %fusion.18), channel_id=1, source_target_pairs={{0,1},{3,2},{4,5},{7,6},{8,9},{11,10},{12,13},{15,14},{16,17},{19,... | collective-permute-start | bytes 1572872 | tf_op jit(solution)/shard_map/ppermute | solution.py:268
  39.4 14.3 %collective-permute-start.5 = (bf16[512,512]{1,0:T(8,128)(2,1)}, bf16[512,512]{1,0:T(8,128)(2,1)S(1)}, u32[]{:S(2)}, u32[]{:S(2)}) collective-permute-start(bf16[512,512]{1,0:T(8,128)(2,1)} %collective-permute-done.1.refs_3_), channel_id=1, source_target_pairs={{1,2},{2,3},{5,6},{6,7},{9,10},{10,11},{13,14},{14,15},{17,18},{18... | collective-permute-start | bytes 1572872 | tf_op jit(solution)/shard_map/ppermute | solution.py:270
  40.1 18.8 %collective-permute-start.7 = (bf16[512,512]{1,0:T(8,128)(2,1)}, bf16[512,512]{1,0:T(8,128)(2,1)S(1)}, u32[]{:S(2)}, u32[]{:S(2)}) collective-permute-start(bf16[512,512]{1,0:T(8,128)(2,1)} %collective-permute-done.3.refs_5_), channel_id=1, source_target_pairs={{2,1},{1,0},{6,5},{5,4},{10,9},{9,8},{14,13},{13,12},{18,17},{17,1... | collective-permute-start | bytes 1572872 | tf_op jit(solution)/shard_map/ppermute | solution.py:270
  49.1 4.2 %copy-start.5 = (bf16[512,4096]{1,0:T(8,128)(2,1)S(1)}, bf16[512,4096]{1,0:T(8,128)(2,1)}, u32[]{:S(2)}) copy-start(bf16[512,4096]{1,0:T(8,128)(2,1)} %tokens_ref.1) | copy-start | bytes 12582916
  49.1 12.6 %collective-permute-start.11 = (f32[192,512]{1,0:T(8,128)S(1)}, f32[192,512]{1,0:T(8,128)S(1)}, u32[]{:S(2)}, u32[]{:S(2)}) collective-permute-start(f32[192,512]{1,0:T(8,128)S(1)} %get-tuple-element.18), channel_id=1, source_target_pairs={{0,8},{4,12},{8,0},{12,4},{16,24},{20,28},{24,16},{28,20},{1,9},{5... | collective-permute-start | bytes 1179656 | tf_op jit(solution)/shard_map/ppermute | solution.py:302
  51.7 16.7 %collective-permute-start.12 = (f32[192,512]{1,0:T(8,128)S(1)}, f32[192,512]{1,0:T(8,128)S(1)}, u32[]{:S(2)}, u32[]{:S(2)}) collective-permute-start(f32[192,512]{1,0:T(8,128)S(1)} %get-tuple-element.19), channel_id=1, source_target_pairs={{0,16},{4,20},{8,24},{12,28},{16,0},{20,4},{24,8},{28,12},{1,17},{... | collective-permute-start | bytes 1179656 | tf_op jit(solution)/shard_map/ppermute | solution.py:302
  53.8 15.9 %collective-permute-start.13 = (f32[192,512]{1,0:T(8,128)S(1)}, f32[192,512]{1,0:T(8,128)S(1)}, u32[]{:S(2)}, u32[]{:S(2)}) collective-permute-start(f32[192,512]{1,0:T(8,128)S(1)} %get-tuple-element.20), channel_id=1, source_target_pairs={{0,24},{4,28},{8,16},{12,20},{16,8},{20,12},{24,0},{28,4},{1,25},{... | collective-permute-start | bytes 1179656 | tf_op jit(solution)/shard_map/ppermute | solution.py:302
  58.9 16.7 %collective-permute-start.8 = (bf16[512,512]{1,0:T(8,128)(2,1)S(1)}, bf16[512,512]{1,0:T(8,128)(2,1)S(1)}, u32[]{:S(2)}, u32[]{:S(2)}) collective-permute-start(bf16[512,512]{1,0:T(8,128)(2,1)S(1)} %broadcast_select_fusion.1), channel_id=1, source_target_pairs={{2,3},{1,0},{6,7},{5,4},{10,11},{9,8},{14,15},{13,12},{18,19},{17,... | collective-permute-start | bytes 1572872 | tf_op jit(solution)/shard_map/ppermute | solution.py:268
  60.2 9.4 %copy-start.3 = (f32[192,512]{1,0:T(8,128)S(1)}, f32[192,512]{1,0:T(8,128)}, u32[]{:S(2)}) copy-start(f32[192,512]{1,0:T(8,128)} %params_ref.1) | copy-start | bytes 1179652
  60.3 9.4 %copy-start.4 = (f32[192,512]{1,0:T(8,128)S(1)}, f32[192,512]{1,0:T(8,128)}, u32[]{:S(2)}) copy-start(f32[192,512]{1,0:T(8,128)} %momentum_ref.1) | copy-start | bytes 1179652
  60.3 16.9 %collective-permute-start.21 = (f16[512,512]{1,0:T(8,128)(2,1)S(1)}, f16[512,512]{1,0:T(8,128)(2,1)S(1)}, u32[]{:S(2)}, u32[]{:S(2)}) collective-permute-start(f16[512,512]{1,0:T(8,128)(2,1)S(1)} %fusion.12), channel_id=1, source_target_pairs={{3,2},{2,1},{7,6},{6,5},{11,10},{10,9},{15,14},{14,13},{19,18},{18... | collective-permute-start | bytes 1572872 | tf_op jit(solution)/shard_map/ppermute | solution.py:270
  61.7 17.5 %collective-permute-start.19 = (f16[512,512]{1,0:T(8,128)(2,1)S(1)}, f16[512,512]{1,0:T(8,128)(2,1)S(1)}, u32[]{:S(2)}, u32[]{:S(2)}) collective-permute-start(f16[512,512]{1,0:T(8,128)(2,1)S(1)} %fusion.12), channel_id=1, source_target_pairs={{0,1},{1,2},{4,5},{5,6},{8,9},{9,10},{12,13},{13,14},{16,17},{17,1... | collective-permute-start | bytes 1572872 | tf_op jit(solution)/shard_map/ppermute | solution.py:270
  68.3 26.0 %collective-permute-start.9 = (bf16[512,512]{1,0:T(8,128)(2,1)S(1)}, bf16[512,512]{1,0:T(8,128)(2,1)S(1)}, u32[]{:S(2)}, u32[]{:S(2)}) collective-permute-start(bf16[512,512]{1,0:T(8,128)(2,1)S(1)} %broadcast_select_fusion), channel_id=1, source_target_pairs={{2,3},{1,0},{6,7},{5,4},{10,11},{9,8},{14,15},{13,12},{18,19},{17,... | collective-permute-start | bytes 1572872 | tf_op jit(solution)/shard_map/ppermute | solution.py:268
  70.7 6.5 %copy-start.10 = (f32[192,512]{1,0:T(8,128)S(1)}, f32[192,512]{1,0:T(8,128)}, u32[]{:S(2)}) copy-start(f32[192,512]{1,0:T(8,128)} %get-tuple-element.12) | copy-start | bytes 1179652
  70.7 12.9 %collective-permute-start.16 = (f32[192,512]{1,0:T(8,128)}, f32[192,512]{1,0:T(8,128)S(1)}, u32[]{:S(2)}, u32[]{:S(2)}) collective-permute-start(f32[192,512]{1,0:T(8,128)} %get-tuple-element.12), channel_id=1, source_target_pairs={{0,24},{4,28},{8,16},{12,20},{16,8},{20,12},{24,0},{28,4},{1,25},{... | collective-permute-start | bytes 1179656 | tf_op jit(solution)/shard_map/ppermute | solution.py:302
  75.7 12.6 %collective-permute-start.15 = (f32[192,512]{1,0:T(8,128)}, f32[192,512]{1,0:T(8,128)S(1)}, u32[]{:S(2)}, u32[]{:S(2)}) collective-permute-start(f32[192,512]{1,0:T(8,128)} %get-tuple-element.12), channel_id=1, source_target_pairs={{0,16},{4,20},{8,24},{12,28},{16,0},{20,4},{24,8},{28,12},{1,17},{... | collective-permute-start | bytes 1179656 | tf_op jit(solution)/shard_map/ppermute | solution.py:302
  77.2 12.4 %collective-permute-start.14 = (f32[192,512]{1,0:T(8,128)S(1)}, f32[192,512]{1,0:T(8,128)S(1)}, u32[]{:S(2)}, u32[]{:S(2)}) collective-permute-start(f32[192,512]{1,0:T(8,128)S(1)} %copy-done.10), channel_id=1, source_target_pairs={{0,8},{4,12},{8,0},{12,4},{16,24},{20,28},{24,16},{28,20},{1,9},{5... | collective-permute-start | bytes 1179656 | tf_op jit(solution)/shard_map/ppermute | solution.py:302
  79.2 15.2 %collective-permute-start.26 = (f16[512,512]{1,0:T(8,128)(2,1)S(1)}, f16[512,512]{1,0:T(8,128)(2,1)S(1)}, u32[]{:S(2)}, u32[]{:S(2)}) collective-permute-start(f16[512,512]{1,0:T(8,128)(2,1)S(1)} %fusion.15), channel_id=1, source_target_pairs={{3,2},{2,1},{7,6},{6,5},{11,10},{10,9},{15,14},{14,13},{19,18},{18... | collective-permute-start | bytes 1572872 | tf_op jit(solution)/shard_map/ppermute | solution.py:270
  83.6 13.1 %collective-permute-start.24 = (f16[512,512]{1,0:T(8,128)(2,1)S(1)}, f16[512,512]{1,0:T(8,128)(2,1)S(1)}, u32[]{:S(2)}, u32[]{:S(2)}) collective-permute-start(f16[512,512]{1,0:T(8,128)(2,1)S(1)} %fusion.15), channel_id=1, source_target_pairs={{0,1},{1,2},{4,5},{5,6},{8,9},{9,10},{12,13},{13,14},{16,17},{17,1... | collective-permute-start | bytes 1572872 | tf_op jit(solution)/shard_map/ppermute | solution.py:270
  88.3 29.6 %collective-permute-start.22 = (f16[512,512]{1,0:T(8,128)(2,1)S(1)}, f16[512,512]{1,0:T(8,128)(2,1)S(1)}, u32[]{:S(2)}, u32[]{:S(2)}) collective-permute-start(f16[512,512]{1,0:T(8,128)(2,1)S(1)} %fusion.13), channel_id=1, source_target_pairs={{3,2},{2,1},{1,0},{7,6},{6,5},{5,4},{11,10},{10,9},{9,8},{15,14},{... | collective-permute-start | bytes 1572872 | tf_op jit(solution)/shard_map/ppermute | solution.py:270
  89.6 28.3 %collective-permute-start.20 = (f16[512,512]{1,0:T(8,128)(2,1)S(1)}, f16[512,512]{1,0:T(8,128)(2,1)S(1)}, u32[]{:S(2)}, u32[]{:S(2)}) collective-permute-start(f16[512,512]{1,0:T(8,128)(2,1)S(1)} %fusion.11), channel_id=1, source_target_pairs={{0,1},{1,2},{2,3},{4,5},{5,6},{6,7},{8,9},{9,10},{10,11},{12,13},{... | collective-permute-start | bytes 1572872 | tf_op jit(solution)/shard_map/ppermute | solution.py:270
  94.3 7.3 %collective-permute-start.17 = (f32[4,192,512]{2,1,0:T(8,128)S(1)}, f32[4,192,512]{2,1,0:T(8,128)S(1)}, u32[]{:S(2)}, u32[]{:S(2)}) collective-permute-start(f32[4,192,512]{2,1,0:T(8,128)S(1)} %pad_maximum_fusion.1.mine_ref), channel_id=1, source_target_pairs={{0,4},{4,0},{8,12},{12,8},{16,20},{20,16},{24,28},{28,24},{1,5},{5... | collective-permute-start | bytes 4718600 | tf_op jit(solution)/shard_map/ppermute | solution.py:302
  94.9 19.4 %collective-permute-start.27 = (f16[512,512]{1,0:T(8,128)(2,1)S(1)}, f16[512,512]{1,0:T(8,128)(2,1)S(1)}, u32[]{:S(2)}, u32[]{:S(2)}) collective-permute-start(f16[512,512]{1,0:T(8,128)(2,1)S(1)} %fusion.16), channel_id=1, source_target_pairs={{3,2},{2,1},{1,0},{7,6},{6,5},{5,4},{11,10},{10,9},{9,8},{15,14},{... | collective-permute-start | bytes 1572872 | tf_op jit(solution)/shard_map/ppermute | solution.py:270
  97.2 20.2 %collective-permute-start.25 = (f16[512,512]{1,0:T(8,128)(2,1)S(1)}, f16[512,512]{1,0:T(8,128)(2,1)S(1)}, u32[]{:S(2)}, u32[]{:S(2)}) collective-permute-start(f16[512,512]{1,0:T(8,128)(2,1)S(1)} %fusion.14), channel_id=1, source_target_pairs={{0,1},{1,2},{2,3},{4,5},{5,6},{6,7},{8,9},{9,10},{10,11},{12,13},{... | collective-permute-start | bytes 1572872 | tf_op jit(solution)/shard_map/ppermute | solution.py:270
  103.8 1.4 %copy-start.6 = (bf16[192,4096]{1,0:T(8,128)(2,1)S(1)}, bf16[192,4096]{1,0:T(8,128)(2,1)}, u32[]{:S(2)}) copy-start(bf16[192,4096]{1,0:T(8,128)(2,1)} %shard_map.138.refs_12_) | copy-start | bytes 4718596
  111.4 1.0 copy-start.1
  117.4 1.6 %copy-start.9 = (f32[1024,512]{1,0:T(8,128)S(1)}, f32[1024,512]{1,0:T(8,128)}, u32[]{:S(2)}) copy-start(f32[1024,512]{1,0:T(8,128)} %param.12) | copy-start | bytes 6291460
  117.9 1.5 %copy-start.7 = (bf16[1024,512]{1,0:T(8,128)(2,1)S(1)}, bf16[1024,512]{1,0:T(8,128)(2,1)}, u32[]{:S(2)}) copy-start(bf16[1024,512]{1,0:T(8,128)(2,1)} %param.10) | copy-start | bytes 3145732
  117.9 2.2 %copy-start.8 = (f32[1024,512]{1,0:T(8,128)S(1)}, f32[1024,512]{1,0:T(8,128)}, u32[]{:S(2)}) copy-start(f32[1024,512]{1,0:T(8,128)} %param.11) | copy-start | bytes 6291460

commit v4 on v3

--- a/solution.py
+++ b/solution.py
@@ -17,10 +17,7 @@
 OUTER_RATE = 0.7
 OUTER_MOMENTUM = 0.9
 MERGE_WEIGHT = 0.5
-TUNE = {'rp': 2, 'gp': 2, 'vk': 16, 'vm': 12, 'vo': 12, 'columns': 0, 'chain': 1, 'gate': None, ('tie', 1, 0): None, ('tie', 1, 1): None, ('tie', 3, 0): 2, ('tie', 3, 1): 2, ('x', 2, 0): 14, ('x', 2, 1): 14, ('x', 3, 0): 14, ('x', 3, 1): 14}
-PIECES = TUNE.get("rp", 2)
-WEIGHT_PIECES = TUNE.get('gp', 2)
-VM = TUNE.get('vmem', 60)
+PIECES = 2
 ANY = pl.BlockSpec(memory_space=pl.ANY)
 MIB = 1 << 20
 
@@ -36,11 +33,11 @@
     return jax.ShapeDtypeStruct(array.shape, dtype or array.dtype)
 
 
-def call(kernel, vmem=VM, flops=0, moved=0, **settings):
+def call(kernel, vmem, flops=0, **settings):
     return pl.pallas_call(
         kernel,
         compiler_params=pltpu.CompilerParams(vmem_limit_bytes=vmem * MIB),
-        cost_estimate=pl.CostEstimate(flops=flops, bytes_accessed=moved, transcendentals=0),
+        cost_estimate=pl.CostEstimate(flops=flops, bytes_accessed=0, transcendentals=0),
         **settings,
     )
 
@@ -58,6 +55,22 @@
         out_specs=ANY,
         input_output_aliases={0: 0},
     )(value, *others)
+
+
+def copy_rows(array, strips, k, *others):
+    strip = array.shape[0] // strips
+
+    def kernel(in_ref, *refs):
+        refs[-1][...] = in_ref[...]
+
+    return call(
+        kernel,
+        vmem=8,
+        out_shape=jax.ShapeDtypeStruct((strip, array.shape[1]), array.dtype),
+        grid=(1,),
+        in_specs=[pl.BlockSpec((strip, array.shape[1]), lambda i: (k, 0))] + [ANY] * len(others),
+        out_specs=pl.BlockSpec((strip, array.shape[1]), lambda i: (0, 0)),
+    )(array, *others)
 
 
 def project(owners, valid, tokens, weights, rows, *others):
@@ -101,8 +114,8 @@
 
     return call(
         kernel,
-        vmem=TUNE.get('vk', 60),
-        flops=TUNE.get("project", 6) * 10**9,
+        vmem=16,
+        flops=6 * 10**9,
         out_shape=jax.ShapeDtypeStruct((tokens.shape[0], width), jnp.bfloat16),
         grid_spec=pltpu.PrefetchScalarGridSpec(
             num_scalar_prefetch=2,
@@ -144,8 +157,7 @@
     out = jax.ShapeDtypeStruct((half, slab_rows, column_count), slab.dtype)
     return call(
         kernel,
-        vmem=TUNE.get("vo", 12),
-        flops=int(TUNE.get("columns", 0) * 10**9),
+        vmem=12,
         out_shape=[out, out],
         grid_spec=pltpu.PrefetchScalarGridSpec(
             num_scalar_prefetch=1,
@@ -223,8 +235,8 @@
     outer = pl.BlockSpec((half, step, column_count), lambda i, place: (0, i, 0))
     return call(
         kernel,
-        vmem=TUNE.get("vm", 12),
-        flops=int(TUNE.get("merge", 3) * 10**9),
+        vmem=12,
+        flops=3 * 10**9,
         out_shape=shape_of(slab),
         grid_spec=pltpu.PrefetchScalarGridSpec(
             num_scalar_prefetch=1, grid=(blocks,), in_specs=[block, outer, outer], out_specs=block
@@ -275,13 +287,10 @@
     def both(come):
         return come[0].astype(jnp.float32) + come[1].astype(jnp.float32)
 
-    weight_strip = rows // WEIGHT_PIECES
-    each = range(WEIGHT_PIECES)
-    weights = [key_weight[p * weight_strip : (p + 1) * weight_strip] for p in each]
-    held = [[None] * WEIGHT_PIECES for _ in range(n)]
+    weights = [copy_rows(key_weight, PIECES, p) for p in every]
+    held = [[None] * PIECES for _ in range(n)]
     sums = [None] * PIECES
-
-    for p in each:
+    for p in every:
         held[0][p] = exchange(weights[p], weights[p], [(i, i + 1) for i in range(n - 1)])
     place = lax.axis_index("replica")
 
@@ -294,58 +303,30 @@
             columns, cotangent, (((0,), (0,)), ((), ())), preferred_element_type=jnp.float32
         )
 
-    if TUNE.get("gate") is not None:
-        first_owner = jnp.where(me < 1, n + me - 1, 0 - (n - 1 - me))
-        firsts = [after(term(columns_of(first_owner, q), key_cotangent)) for q in every]
-
     def swap(array, k):
         return lax.ppermute(array, "replica", [(i, i ^ k) for i in range(replicas)])
 
-    late = tuple(firsts) if TUNE.get("late", 0) else ()
-    keep, send = split_blocks(local_slab, place, replicas, *late)
+    keep, send = split_blocks(local_slab, place, replicas)
     pairs = pair_sums(keep, swap(send, 1), place)
     parts = [pairs[0]] + [swap(pairs[j], 2 * j) for j in range(1, replicas // 2)]
-    if TUNE.get("outer_tie") is not None:
-        parts[0] = after(parts[0], *held[TUNE["outer_tie"]][0])
     new_outer, new_momentum = outer_update(parts, outer_params, outer_momentum, replicas)
     mine = [new_outer] + [swap(new_outer, 2 * j) for j in range(1, replicas // 2)]
 
-    cotangent = key_cotangent
+    cotangent = copy_rows(key_cotangent, 1, 0, held[0][0][0])
     for t in range(1, n):
         links = [(i, i + 1) for i in range(t)]
         up, down = n + me - t, t - 1 - (n - 1 - me)
         owners = [jnp.where(me < t, up, down)] if 2 * t <= n else [up, down]
         for p in every:
-            w = p * WEIGHT_PIECES // PIECES
-            if t == 1 and p == 0 and TUNE.get("gate") is not None:
-                for v in each:
-                    first = after(held[0][v][0], *firsts, flops=TUNE["gate"] * 10**9)
-                    second = first if held[0][v][1] is held[0][v][0] else after(held[0][v][1], *firsts)
-                    held[0][v] = (first, second)
-            came = held[t - 1][w]
-            if t < n - 1 and held[t][w] is None:
-                held[t][w] = exchange(*came, [(i, i + 1) for i in range(t, n - 1)])
-            if (t, p) == TUNE.get("mine_after"):
-                mine[0] = after(mine[0], *came)
-            extra = ()
-            if (t, p) == TUNE.get("pairs_before"):
-                extra = (pairs[0],)
-            if (t, p) == TUNE.get("outer_before"):
-                extra = (new_outer,)
-            if (t, p) == TUNE.get("mine_before"):
-                extra = tuple(mine[1:])
-            tie = TUNE.get(("tie", t, p), t - 1)
-            others = () if tie is None else tuple(held[tie][w])
-            cost = TUNE.get(("x", t, p), 0) * 10**9
-            source = cotangent if TUNE.get("chain", 0) else key_cotangent
-            others = (*others, *extra)
-            if others or cost:
-                source = after(source, *others, flops=cost)
-                cotangent = source
-            if t == 1 and TUNE.get("gate") is not None:
-                loads = [firsts[p]]
-            else:
-                loads = [term(columns_of(owner, p), source) for owner in owners]
+            came = held[t - 1][p]
+            if t < n - 1:
+                held[t][p] = exchange(*came, [(i, i + 1) for i in range(t, n - 1)])
+            source = key_cotangent
+            if t > 1:
+                source = cotangent = after(cotangent, *held[t - 1][p], flops=14 * 10**9)
+            if t == n - 1 and p == 0:
+                mine = [mine[0]] + [after(block, source) for block in mine[1:]]
+            loads = [term(columns_of(owner, p), source) for owner in owners]
             if len(loads) == 1:
                 load = loads[0] if t == 1 else loads[0] + one_of(sums[p])
                 up_load = down_load = load.astype(jnp.float16)
@@ -363,16 +344,16 @@
         if held[t][0][0] is held[t][0][1]:
             owners.append(jnp.where(me - t - 1 >= 0, me - t - 1, me + t + 1))
             valid.append((me - t - 1 >= 0) | (me + t + 1 <= n - 1))
-            steps.append([held[t][p][0] for p in each])
+            steps.append([held[t][p][0] for p in every])
         else:
             owners += [me - t - 1, me + t + 1]
             valid += [me - t - 1 >= 0, me + t + 1 <= n - 1]
-            steps += [[held[t][p][0] for p in each], [held[t][p][1] for p in each]]
+            steps += [[held[t][p][0] for p in every], [held[t][p][1] for p in every]]
     owners = jnp.clip(jnp.stack(owners), 0, n - 1).astype(jnp.int32)
-    others = (new_local,) if TUNE.get("merge_first", 1) else ()
-    projected = project(owners, jnp.stack(valid).astype(jnp.int32), tokens, steps, rows, *others)
-
-    source = after(key_cotangent, projected)
+    valid = jnp.stack(valid).astype(jnp.int32)
+    projected = project(owners, valid, tokens, steps, rows, new_local)
+
+    source = after(cotangent, projected)
     own = [term(columns_of(me, p), source) for p in every]
     gradient = jnp.concatenate([own[p] + one_of(sums[p]) for p in every], 0) / scale
     new_first = BETA_ONE * first_moment + (1.0 - BETA_ONE) * gradient

time: 125 us -> 124 us (level)
  starting transfers between devices: 57.6 us -> 59.5 us
  local copies, waits for them, and re-layouts: 8.5 us -> 6.62 us
  waiting for transfers between devices: 32.2 us -> 30.6 us
    ppermute x8, waiting for transfers between devices: 5.75 us -> 1.89 us  [exchange(): lax.ppermute(up_load, 'fsdp', up)]
    slice x1 -> x0, local copies, waits for them, and re-layouts: 2.23 us -> none  [shards(): key_weight[p * weight_strip:(p + 1) * weight_strip]]
    pallas_call x3 -> x6, Pallas kernels: 9.84 us -> 11.5 us  [the longest x1 6.17 us: project(): call(kernel, vmem=16, flops=6 * 10 ** 9, out_shape=jax.ShapeDtypeStruct((...]
    ppermute x8, waiting for transfers between devices: 18.5 us -> 20.1 us  [exchange(): lax.ppermute(down_load, 'fsdp', down)]
    ppermute x8, waiting for transfers between devices: 4.59 us -> 6.14 us  [swap(): return lax.ppermute(array, 'replica', [(i, i ^ k) for i in range(replicas)])]
    ppermute x8, starting transfers between devices: 31.3 us -> 32.6 us  [exchange(): lax.ppermute(up_load, 'fsdp', up)]
    unnamed x24 -> x26, local copies, waits for them, and re-layouts: 6.08 us -> 6.43 us
where the time goes in v4:
time: 124 us; the launch traced here: 123 us
  starting transfers between devices  59.5 us (48%)
  waiting for transfers between devices  30.6 us (25%)
  Pallas kernels  12.7 us (10%)
  matrix products  6.99 us (6%)
  local copies, waits for them, and re-layouts  6.62 us (5%)
  other arithmetic  5.11 us (4%)
  between operations  1.24 us (1%)
    ppermute x8, starting transfers between devices, exchange(): lax.ppermute(up_load, 'fsdp', up)  32.6 us
    ppermute x8, waiting for transfers between devices, exchange(): lax.ppermute(down_load, 'fsdp', down)  20.1 us
    ppermute x8, starting transfers between devices, exchange(): lax.ppermute(down_load, 'fsdp', down)  9.22 us
    ppermute x4, starting transfers between devices, exchange(): come = lax.ppermute(load, 'fsdp', up + down)  9.12 us
    ppermute x8, starting transfers between devices, swap(): return lax.ppermute(array, 'replica', [(i, i ^ k) for i in range(replicas)])  8.56 us
    dot_general x10, matrix products, term(): lax.dot_general(columns, cotangent, (((0,), (0,)), ((), ())), preferred_e...  6.99 us
    unnamed x26, local copies, waits for them, and re-layouts  6.43 us
    pallas_call x1, Pallas kernels, project(): call(kernel, vmem=16, flops=6 * 10 ** 9, out_shape=jax.ShapeDtypeStruct((...  6.17 us
  transfers between devices with their start and end apart: 28, of which 10 were waited for; matrix products, arithmetic and copies ran while one was open for 7% of the time, Pallas kernels for 10%

profile of v4, /device:TPU:0, one launch (start us, length us, event | category | flops | bytes accessed | tf_op | source)
XLA Modules:
  0.0 122.8 jit_solution(9217626255154714619)
XLA Ops:
  0.6 1.2 copy-done
  1.9 0.8 shard_map.135.refs_0_
  2.7 5.7 %collective-permute-start = (bf16[512,512]{1,0:T(8,128)(2,1)}, bf16[512,512]{1,0:T(8,128)(2,1)}, u32[]{:S(2)}, u32[]{:S(2)}) collective-permute-start(bf16[512,512]{1,0:T(8,128)(2,1)} %shard_map.135.refs_0_), channel_id=1, source_target_pairs={{0,1},{1,2},{2,3},{4,5},{5,6},{6,7},{8,9},{9,10},{10,11},{12,13},{... | collective-permute-start | bytes 1572872 | tf_op jit(solution)/shard_map/ppermute | solution.py:282
  8.4 1.3 %collective-permute-start.2 = (bf16[512,512]{1,0:T(8,128)(2,1)}, bf16[512,512]{1,0:T(8,128)(2,1)}, u32[]{:S(2)}, u32[]{:S(2)}) collective-permute-start(bf16[512,512]{1,0:T(8,128)(2,1)} %shard_map.135.refs_0_), channel_id=1, source_target_pairs={{3,2},{2,1},{1,0},{7,6},{6,5},{5,4},{11,10},{10,9},{9,8},{15,14},{... | collective-permute-start | bytes 1572872 | tf_op jit(solution)/shard_map/ppermute | solution.py:282
  9.7 1.4 %copy-done.2 = bf16[192,4096]{1,0:T(8,128)(2,1)S(1)} copy-done((bf16[192,4096]{1,0:T(8,128)(2,1)S(1)}, bf16[192,4096]{1,0:T(8,128)(2,1)}, u32[]{:S(2)}) %copy-start.2) | copy-done | bytes 1572888
  11.1 1.5 %shard_map.137 = (bf16[4,192,512]{2,1,0:T(8,128)(2,1)S(1)}, bf16[4,192,512]{2,1,0:T(8,128)(2,1)}) custom-call(s32[1]{0:T(128)} %bitcast.12.place_ref, bf16[192,4096]{1,0:T(8,128)(2,1)S(1)} %copy-done.2), custom_call_target="tpu_custom_call" | custom-call | tf_op jit(solution)/shard_map/pallas_call | solution.py:158
  12.6 0.8 shard_map.136.refs_1_
  13.4 5.4 %collective-permute-start.1 = (bf16[512,512]{1,0:T(8,128)(2,1)}, bf16[512,512]{1,0:T(8,128)(2,1)}, u32[]{:S(2)}, u32[]{:S(2)}) collective-permute-start(bf16[512,512]{1,0:T(8,128)(2,1)} %shard_map.136.refs_1_), channel_id=1, source_target_pairs={{0,1},{1,2},{2,3},{4,5},{5,6},{6,7},{8,9},{9,10},{10,11},{12,13},{... | collective-permute-start | bytes 1572872 | tf_op jit(solution)/shard_map/ppermute | solution.py:282
  18.8 1.3 %collective-permute-start.3 = (bf16[512,512]{1,0:T(8,128)(2,1)}, bf16[512,512]{1,0:T(8,128)(2,1)}, u32[]{:S(2)}, u32[]{:S(2)}) collective-permute-start(bf16[512,512]{1,0:T(8,128)(2,1)} %shard_map.136.refs_1_), channel_id=1, source_target_pairs={{3,2},{2,1},{1,0},{7,6},{6,5},{5,4},{11,10},{10,9},{9,8},{15,14},{... | collective-permute-start | bytes 1572872 | tf_op jit(solution)/shard_map/ppermute | solution.py:282
  20.2 1.5 %collective-permute-start.4 = (bf16[512,512]{1,0:T(8,128)(2,1)}, bf16[512,512]{1,0:T(8,128)(2,1)}, u32[]{:S(2)}, u32[]{:S(2)}) collective-permute-start(bf16[512,512]{1,0:T(8,128)(2,1)} %collective-permute-done.refs_0_.refs_2_), channel_id=1, source_target_pairs={{1,2},{2,3},{5,6},{6,7},{9,10},{10,11},{13,14},{14,15},{17,18},{18... | collective-permute-start | bytes 1572872 | tf_op jit(solution)/shard_map/ppermute | solution.py:282
  21.7 2.4 %collective-permute-done.2.refs_4_ = bf16[512,512]{1,0:T(8,128)(2,1)} collective-permute-done((bf16[512,512]{1,0:T(8,128)(2,1)}, bf16[512,512]{1,0:T(8,128)(2,1)}, u32[]{:S(2)}, u32[]{:S(2)}) %collective-permute-start.2) | collective-permute-done | bytes 524320 | tf_op jit(solution)/shard_map/ppermute | solution.py:282
  24.1 1.3 %collective-permute-start.6 = (bf16[512,512]{1,0:T(8,128)(2,1)}, bf16[512,512]{1,0:T(8,128)(2,1)}, u32[]{:S(2)}, u32[]{:S(2)}) collective-permute-start(bf16[512,512]{1,0:T(8,128)(2,1)} %collective-permute-done.2.refs_4_), channel_id=1, source_target_pairs={{2,1},{1,0},{6,5},{5,4},{10,9},{9,8},{14,13},{13,12},{18,17},{17,1... | collective-permute-start | bytes 1572872 | tf_op jit(solution)/shard_map/ppermute | solution.py:282
  25.6 1.5 %fusion.17 = f16[512,512]{1,0:T(8,128)(2,1)S(1)} fusion(bf16[512,512]{1,0:T(8,128)(2,1)S(1)} %copy-done.4, bf16[512,4096]{1,0:T(8,128)(2,1)} %tokens_ref.1, s32[]{:T(128)S(6)} %select_n.61), kind=kOutput, calls=%fused_computation.33 | convolution fusion | flops 268959744 | bytes 1572868 | tf_op jit(solution)/shard_map/dot_general | solution.py:302
  27.1 1.5 %fusion.18 = f16[512,512]{1,0:T(8,128)(2,1)S(1)} fusion(bf16[512,512]{1,0:T(8,128)(2,1)S(1)} %copy-done.4, bf16[512,4096]{1,0:T(8,128)(2,1)} %tokens_ref.1, s32[]{:T(128)S(6)} %select_n.66), kind=kOutput, calls=%fused_computation.34 | convolution fusion | flops 268959744 | bytes 1572868 | tf_op jit(solution)/shard_map/dot_general | solution.py:302
  28.7 5.2 %collective-permute-start.18 = (f16[512,512]{1,0:T(8,128)(2,1)S(1)}, f16[512,512]{1,0:T(8,128)(2,1)S(1)}, u32[]{:S(2)}, u32[]{:S(2)}) collective-permute-start(f16[512,512]{1,0:T(8,128)(2,1)S(1)} %fusion.17), channel_id=1, source_target_pairs={{0,1},{3,2},{4,5},{7,6},{8,9},{11,10},{12,13},{15,14},{16,17},{19,... | collective-permute-start | bytes 1572872 | tf_op jit(solution)/shard_map/ppermute | solution.py:280
  34.1 1.3 %collective-permute-start.23 = (f16[512,512]{1,0:T(8,128)(2,1)S(1)}, f16[512,512]{1,0:T(8,128)(2,1)S(1)}, u32[]{:S(2)}, u32[]{:S(2)}) collective-permute-start(f16[512,512]{1,0:T(8,128)(2,1)S(1)} %fusion.18), channel_id=1, source_target_pairs={{0,1},{3,2},{4,5},{7,6},{8,9},{11,10},{12,13},{15,14},{16,17},{19,... | collective-permute-start | bytes 1572872 | tf_op jit(solution)/shard_map/ppermute | solution.py:280
  36.5 1.3 %collective-permute-start.7 = (bf16[512,512]{1,0:T(8,128)(2,1)}, bf16[512,512]{1,0:T(8,128)(2,1)S(1)}, u32[]{:S(2)}, u32[]{:S(2)}) collective-permute-start(bf16[512,512]{1,0:T(8,128)(2,1)} %collective-permute-done.3.refs_5_), channel_id=1, source_target_pairs={{2,1},{1,0},{6,5},{5,4},{10,9},{9,8},{14,13},{13,12},{18,17},{17,1... | collective-permute-start | bytes 1572872 | tf_op jit(solution)/shard_map/ppermute | solution.py:282
  37.8 9.2 %collective-permute-done.6.refs_2_.refs_8_ = bf16[512,512]{1,0:T(8,128)(2,1)} collective-permute-done((bf16[512,512]{1,0:T(8,128)(2,1)}, bf16[512,512]{1,0:T(8,128)(2,1)}, u32[]{:S(2)}, u32[]{:S(2)}) %collective-permute-start.6) | collective-permute-done | bytes 524320 | tf_op jit(solution)/shard_map/ppermute | solution.py:282
  47.0 1.5 %collective-permute-start.11 = (f32[192,512]{1,0:T(8,128)S(1)}, f32[192,512]{1,0:T(8,128)S(1)}, u32[]{:S(2)}, u32[]{:S(2)}) collective-permute-start(f32[192,512]{1,0:T(8,128)S(1)} %get-tuple-element.18), channel_id=1, source_target_pairs={{0,8},{4,12},{8,0},{12,4},{16,24},{20,28},{24,16},{28,20},{1,9},{5... | collective-permute-start | bytes 1179656 | tf_op jit(solution)/shard_map/ppermute | solution.py:307
  48.5 1.1 broadcast_select_fusion.1
  49.6 1.6 %collective-permute-start.12 = (f32[192,512]{1,0:T(8,128)S(1)}, f32[192,512]{1,0:T(8,128)S(1)}, u32[]{:S(2)}, u32[]{:S(2)}) collective-permute-start(f32[192,512]{1,0:T(8,128)S(1)} %get-tuple-element.19), channel_id=1, source_target_pairs={{0,16},{4,20},{8,24},{12,28},{16,0},{20,4},{24,8},{28,12},{1,17},{... | collective-permute-start | bytes 1179656 | tf_op jit(solution)/shard_map/ppermute | solution.py:307
  51.7 0.8 collective-permute-start.13
  52.5 5.1 %collective-permute-done.7.refs_2_.refs_9_ = bf16[512,512]{1,0:T(8,128)(2,1)S(1)} collective-permute-done((bf16[512,512]{1,0:T(8,128)(2,1)}, bf16[512,512]{1,0:T(8,128)(2,1)S(1)}, u32[]{:S(2)}, u32[]{:S(2)}) %collective-permute-start.7) | collective-permute-done | bytes 524320 | tf_op jit(solution)/shard_map/ppermute | solution.py:282
  57.6 1.3 %collective-permute-start.8 = (bf16[512,512]{1,0:T(8,128)(2,1)S(1)}, bf16[512,512]{1,0:T(8,128)(2,1)S(1)}, u32[]{:S(2)}, u32[]{:S(2)}) collective-permute-start(bf16[512,512]{1,0:T(8,128)(2,1)S(1)} %broadcast_select_fusion.1), channel_id=1, source_target_pairs={{2,3},{1,0},{6,7},{5,4},{10,11},{9,8},{14,15},{13,12},{18,19},{17,... | collective-permute-start | bytes 1572872 | tf_op jit(solution)/shard_map/ppermute | solution.py:280
  59.0 0.8 collective-permute-start.21
  60.3 5.2 %collective-permute-start.19 = (f16[512,512]{1,0:T(8,128)(2,1)S(1)}, f16[512,512]{1,0:T(8,128)(2,1)S(1)}, u32[]{:S(2)}, u32[]{:S(2)}) collective-permute-start(f16[512,512]{1,0:T(8,128)(2,1)S(1)} %fusion.12), channel_id=1, source_target_pairs={{0,1},{1,2},{4,5},{5,6},{8,9},{9,10},{12,13},{13,14},{16,17},{17,1... | collective-permute-start | bytes 1572872 | tf_op jit(solution)/shard_map/ppermute | solution.py:282
  65.6 2.4 %collective-permute-done.12.refs_2_ = f32[192,512]{1,0:T(8,128)S(1)} collective-permute-done((f32[192,512]{1,0:T(8,128)S(1)}, f32[192,512]{1,0:T(8,128)S(1)}, u32[]{:S(2)}, u32[]{:S(2)}) %collective-permute-start.12) | collective-permute-done | bytes 393248 | tf_op jit(solution)/shard_map/ppermute | solution.py:307
  67.9 1.3 %collective-permute-start.9 = (bf16[512,512]{1,0:T(8,128)(2,1)S(1)}, bf16[512,512]{1,0:T(8,128)(2,1)S(1)}, u32[]{:S(2)}, u32[]{:S(2)}) collective-permute-start(bf16[512,512]{1,0:T(8,128)(2,1)S(1)} %broadcast_select_fusion), channel_id=1, source_target_pairs={{2,3},{1,0},{6,7},{5,4},{10,11},{9,8},{14,15},{13,12},{18,19},{17,... | collective-permute-start | bytes 1572872 | tf_op jit(solution)/shard_map/ppermute | solution.py:280
  69.3 1.0 shard_map.139
  70.3 1.6 %collective-permute-start.16 = (f32[192,512]{1,0:T(8,128)}, f32[192,512]{1,0:T(8,128)S(1)}, u32[]{:S(2)}, u32[]{:S(2)}) collective-permute-start(f32[192,512]{1,0:T(8,128)} %get-tuple-element.12), channel_id=1, source_target_pairs={{0,24},{4,28},{8,16},{12,20},{16,8},{20,12},{24,0},{28,4},{1,25},{... | collective-permute-start | bytes 1179656 | tf_op jit(solution)/shard_map/ppermute | solution.py:307
  71.9 2.5 %collective-permute-done.8.refs_1_.refs_2_.refs_10_ = bf16[512,512]{1,0:T(8,128)(2,1)S(1)} collective-permute-done((bf16[512,512]{1,0:T(8,128)(2,1)S(1)}, bf16[512,512]{1,0:T(8,128)(2,1)S(1)}, u32[]{:S(2)}, u32[]{:S(2)}) %collective-permute-start.8) | collective-permute-done | bytes 524320 | tf_op jit(solution)/shard_map/ppermute | solution.py:280
  74.3 0.9 collective-permute-start.15
  75.2 2.2 %collective-permute-start.14 = (f32[192,512]{1,0:T(8,128)S(1)}, f32[192,512]{1,0:T(8,128)S(1)}, u32[]{:S(2)}, u32[]{:S(2)}) collective-permute-start(f32[192,512]{1,0:T(8,128)S(1)} %copy-done.12), channel_id=1, source_target_pairs={{0,8},{4,12},{8,0},{12,4},{16,24},{20,28},{24,16},{28,20},{1,9},{5... | collective-permute-start | bytes 1179656 | tf_op jit(solution)/shard_map/ppermute | solution.py:307
  77.9 0.7 collective-permute-start.26
  79.1 3.4 %collective-permute-done.16.refs_0_ = f32[192,512]{1,0:T(8,128)S(1)} collective-permute-done((f32[192,512]{1,0:T(8,128)}, f32[192,512]{1,0:T(8,128)S(1)}, u32[]{:S(2)}, u32[]{:S(2)}) %collective-permute-start.16) | collective-permute-done | bytes 393248 | tf_op jit(solution)/shard_map/ppermute | solution.py:307
  82.5 5.0 %collective-permute-start.24 = (f16[512,512]{1,0:T(8,128)(2,1)S(1)}, f16[512,512]{1,0:T(8,128)(2,1)S(1)}, u32[]{:S(2)}, u32[]{:S(2)}) collective-permute-start(f16[512,512]{1,0:T(8,128)(2,1)S(1)} %fusion.15), channel_id=1, source_target_pairs={{0,1},{1,2},{4,5},{5,6},{8,9},{9,10},{12,13},{13,14},{16,17},{17,1... | collective-permute-start | bytes 1572872 | tf_op jit(solution)/shard_map/ppermute | solution.py:282
  87.9 1.3 %collective-permute-start.22 = (f16[512,512]{1,0:T(8,128)(2,1)S(1)}, f16[512,512]{1,0:T(8,128)(2,1)S(1)}, u32[]{:S(2)}, u32[]{:S(2)}) collective-permute-start(f16[512,512]{1,0:T(8,128)(2,1)S(1)} %fusion.13), channel_id=1, source_target_pairs={{3,2},{2,1},{1,0},{7,6},{6,5},{5,4},{11,10},{10,9},{9,8},{15,14},{... | collective-permute-start | bytes 1572872 | tf_op jit(solution)/shard_map/ppermute | solution.py:282
  89.2 4.6 %collective-permute-start.20 = (f16[512,512]{1,0:T(8,128)(2,1)S(1)}, f16[512,512]{1,0:T(8,128)(2,1)S(1)}, u32[]{:S(2)}, u32[]{:S(2)}) collective-permute-start(f16[512,512]{1,0:T(8,128)(2,1)S(1)} %fusion.11), channel_id=1, source_target_pairs={{0,1},{1,2},{2,3},{4,5},{5,6},{6,7},{8,9},{9,10},{10,11},{12,13},{... | collective-permute-start | bytes 1572872 | tf_op jit(solution)/shard_map/ppermute | solution.py:282
  94.6 1.3 %collective-permute-start.27 = (f16[512,512]{1,0:T(8,128)(2,1)S(1)}, f16[512,512]{1,0:T(8,128)(2,1)S(1)}, u32[]{:S(2)}, u32[]{:S(2)}) collective-permute-start(f16[512,512]{1,0:T(8,128)(2,1)S(1)} %fusion.16), channel_id=1, source_target_pairs={{3,2},{2,1},{1,0},{7,6},{6,5},{5,4},{11,10},{10,9},{9,8},{15,14},{... | collective-permute-start | bytes 1572872 | tf_op jit(solution)/shard_map/ppermute | solution.py:282
  96.4 4.6 %collective-permute-start.25 = (f16[512,512]{1,0:T(8,128)(2,1)S(1)}, f16[512,512]{1,0:T(8,128)(2,1)S(1)}, u32[]{:S(2)}, u32[]{:S(2)}) collective-permute-start(f16[512,512]{1,0:T(8,128)(2,1)S(1)} %fusion.14), channel_id=1, source_target_pairs={{0,1},{1,2},{2,3},{4,5},{5,6},{6,7},{8,9},{9,10},{10,11},{12,13},{... | collective-permute-start | bytes 1572872 | tf_op jit(solution)/shard_map/ppermute | solution.py:282
  101.0 2.1 %shard_map.147.refs_12_ = bf16[192,4096]{1,0:T(8,128)(2,1)} custom-call(s32[1]{0:T(128)} %bitcast.12.place_ref, bf16[192,4096]{1,0:T(8,128)(2,1)S(1)} %copy-done.3, f32[4,192,512]{2,1,0:T(8,128)S(1)} %pad_maximum_fusion.1.mine_ref, f32[4,192,512]{2,1,0:T(8,128)S(1)} %collective-permute-done.17.theirs_ref), custom_call_target="tpu_custom_call" | custom-call | flops 3000000000 | tf_op jit(solution)/shard_map/pallas_call | solution.py:236
  103.1 1.4 %copy-done.9 = bf16[192,4096]{1,0:T(8,128)(2,1)S(1)} copy-done((bf16[192,4096]{1,0:T(8,128)(2,1)S(1)}, bf16[192,4096]{1,0:T(8,128)(2,1)}, u32[]{:S(2)}) %copy-start.9) | copy-done | bytes 1572888
  104.5 6.2 %shard_map.148.refs_1_ = bf16[512,512]{1,0:T(8,128)(2,1)} custom-call(s32[6]{0:T(128)S(1)} %broadcast_clamp_fusion.owners_ref, s32[6]{0:T(128)S(1)} %convert_element_type.63.valid_ref, bf16[512,4096]{1,0:T(8,128)(2,1)S(1)} %copy-done.8, bf16[512,512]{1,0:T(8,128)(2,1)} %shard_map.135.refs_0_, bf16[512,512]{1,0:T(8,128)(2,1)} %shard_map.136.refs_1_, ...), custom_call_target="tpu_custom_call" | custom-call | flops 6000000000 | tf_op jit(solution)/shard_map/pallas_call | solution.py:115
  110.7 1.0 copy-done.5
  111.8 3.0 %collective-permute-done.27 = f16[512,512]{1,0:T(8,128)(2,1)S(1)} collective-permute-done((f16[512,512]{1,0:T(8,128)(2,1)S(1)}, f16[512,512]{1,0:T(8,128)(2,1)S(1)}, u32[]{:S(2)}, u32[]{:S(2)}) %collective-permute-start.27) | collective-permute-done | bytes 524320 | tf_op jit(solution)/shard_map/ppermute | solution.py:282
  114.8 1.9 %collective-permute-done.25 = f16[512,512]{1,0:T(8,128)(2,1)S(1)} collective-permute-done((f16[512,512]{1,0:T(8,128)(2,1)S(1)}, f16[512,512]{1,0:T(8,128)(2,1)S(1)}, u32[]{:S(2)}, u32[]{:S(2)}) %collective-permute-start.25) | collective-permute-done | bytes 524320 | tf_op jit(solution)/shard_map/ppermute | solution.py:282
  118.2 0.8 copy-done.10
  119.0 3.8 %fusion.2 = (bf16[1024,512]{1,0:T(8,128)(2,1)}, f32[1024,512]{1,0:T(8,128)}, f32[1024,512]{1,0:T(8,128)}) fusion(bf16[1024,512]{1,0:T(8,128)(2,1)S(1)} %copy-done.1, f32[512,512]{1,0:T(8,128)S(1)} %fusion.6, f32[512,512]{1,0:T(8,128)S(1)} %fusion.10, f32[1024,512]{1,0:T(8,128)S(1)} %copy-done.10, f32[1024,512]{1,0:T(8,128)S(1)} %copy-done.11), kind=kLoop, calls=%fused_computation.4 | loop fusion | flops 9961472 | bytes 12582912 | tf_op jit(solution)/shard_map/convert_element_type | solution.py:366
  (68 shorter events, 6.7 us)
Async XLA Ops:
  0.6 1.2 copy-start
  1.9 10.8 %copy-start.1 = (bf16[1024,512]{1,0:T(8,128)(2,1)S(1)}, bf16[1024,512]{1,0:T(8,128)(2,1)}, u32[]{:S(2)}) copy-start(bf16[1024,512]{1,0:T(8,128)(2,1)} %in_ref.4) | copy-start | bytes 3145732
  1.9 23.7 %copy-start.4 = (bf16[512,512]{1,0:T(8,128)(2,1)S(1)}, bf16[512,512]{1,0:T(8,128)(2,1)}, u32[]{:S(2)}) copy-start(bf16[512,512]{1,0:T(8,128)(2,1)} %in_ref.5) | copy-start | bytes 1572868
  2.7 17.5 %collective-permute-start = (bf16[512,512]{1,0:T(8,128)(2,1)}, bf16[512,512]{1,0:T(8,128)(2,1)}, u32[]{:S(2)}, u32[]{:S(2)}) collective-permute-start(bf16[512,512]{1,0:T(8,128)(2,1)} %shard_map.135.refs_0_), channel_id=1, source_target_pairs={{0,1},{1,2},{2,3},{4,5},{5,6},{6,7},{8,9},{9,10},{10,11},{12,13},{... | collective-permute-start | bytes 1572872 | tf_op jit(solution)/shard_map/ppermute | solution.py:282
  8.4 15.7 %collective-permute-start.2 = (bf16[512,512]{1,0:T(8,128)(2,1)}, bf16[512,512]{1,0:T(8,128)(2,1)}, u32[]{:S(2)}, u32[]{:S(2)}) collective-permute-start(bf16[512,512]{1,0:T(8,128)(2,1)} %shard_map.135.refs_0_), channel_id=1, source_target_pairs={{3,2},{2,1},{1,0},{7,6},{6,5},{5,4},{11,10},{10,9},{9,8},{15,14},{... | collective-permute-start | bytes 1572872 | tf_op jit(solution)/shard_map/ppermute | solution.py:282
  9.7 1.4 %copy-start.2 = (bf16[192,4096]{1,0:T(8,128)(2,1)S(1)}, bf16[192,4096]{1,0:T(8,128)(2,1)}, u32[]{:S(2)}) copy-start(bf16[192,4096]{1,0:T(8,128)(2,1)} %slab_ref.3) | copy-start | bytes 4718596
  12.6 16.0 %collective-permute-start.10 = (bf16[4,192,512]{2,1,0:T(8,128)(2,1)}, bf16[4,192,512]{2,1,0:T(8,128)(2,1)S(1)}, u32[]{:S(2)}, u32[]{:S(2)}) collective-permute-start(bf16[4,192,512]{2,1,0:T(8,128)(2,1)} %get-tuple-element.16), channel_id=1, source_target_pairs={{0,4},{4,0},{8,12},{12,8},{16,20},{20,16},{24,28},{28,24},{1,5},{5... | collective-permute-start | bytes 2359304 | tf_op jit(solution)/shard_map/ppermute | solution.py:307
  13.4 20.6 %collective-permute-start.1 = (bf16[512,512]{1,0:T(8,128)(2,1)}, bf16[512,512]{1,0:T(8,128)(2,1)}, u32[]{:S(2)}, u32[]{:S(2)}) collective-permute-start(bf16[512,512]{1,0:T(8,128)(2,1)} %shard_map.136.refs_1_), channel_id=1, source_target_pairs={{0,1},{1,2},{2,3},{4,5},{5,6},{6,7},{8,9},{9,10},{10,11},{12,13},{... | collective-permute-start | bytes 1572872 | tf_op jit(solution)/shard_map/ppermute | solution.py:282
  18.8 17.0 %collective-permute-start.3 = (bf16[512,512]{1,0:T(8,128)(2,1)}, bf16[512,512]{1,0:T(8,128)(2,1)}, u32[]{:S(2)}, u32[]{:S(2)}) collective-permute-start(bf16[512,512]{1,0:T(8,128)(2,1)} %shard_map.136.refs_1_), channel_id=1, source_target_pairs={{3,2},{2,1},{1,0},{7,6},{6,5},{5,4},{11,10},{10,9},{9,8},{15,14},{... | collective-permute-start | bytes 1572872 | tf_op jit(solution)/shard_map/ppermute | solution.py:282
  20.2 16.3 %collective-permute-start.4 = (bf16[512,512]{1,0:T(8,128)(2,1)}, bf16[512,512]{1,0:T(8,128)(2,1)}, u32[]{:S(2)}, u32[]{:S(2)}) collective-permute-start(bf16[512,512]{1,0:T(8,128)(2,1)} %collective-permute-done.refs_0_.refs_2_), channel_id=1, source_target_pairs={{1,2},{2,3},{5,6},{6,7},{9,10},{10,11},{13,14},{14,15},{17,18},{18... | collective-permute-start | bytes 1572872 | tf_op jit(solution)/shard_map/ppermute | solution.py:282
  24.1 22.9 %collective-permute-start.6 = (bf16[512,512]{1,0:T(8,128)(2,1)}, bf16[512,512]{1,0:T(8,128)(2,1)}, u32[]{:S(2)}, u32[]{:S(2)}) collective-permute-start(bf16[512,512]{1,0:T(8,128)(2,1)} %collective-permute-done.2.refs_4_), channel_id=1, source_target_pairs={{2,1},{1,0},{6,5},{5,4},{10,9},{9,8},{14,13},{13,12},{18,17},{17,1... | collective-permute-start | bytes 1572872 | tf_op jit(solution)/shard_map/ppermute | solution.py:282
  28.7 20.9 %collective-permute-start.18 = (f16[512,512]{1,0:T(8,128)(2,1)S(1)}, f16[512,512]{1,0:T(8,128)(2,1)S(1)}, u32[]{:S(2)}, u32[]{:S(2)}) collective-permute-start(f16[512,512]{1,0:T(8,128)(2,1)S(1)} %fusion.17), channel_id=1, source_target_pairs={{0,1},{3,2},{4,5},{7,6},{8,9},{11,10},{12,13},{15,14},{16,17},{19,... | collective-permute-start | bytes 1572872 | tf_op jit(solution)/shard_map/ppermute | solution.py:280
  34.1 24.9 %collective-permute-start.23 = (f16[512,512]{1,0:T(8,128)(2,1)S(1)}, f16[512,512]{1,0:T(8,128)(2,1)S(1)}, u32[]{:S(2)}, u32[]{:S(2)}) collective-permute-start(f16[512,512]{1,0:T(8,128)(2,1)S(1)} %fusion.18), channel_id=1, source_target_pairs={{0,1},{3,2},{4,5},{7,6},{8,9},{11,10},{12,13},{15,14},{16,17},{19,... | collective-permute-start | bytes 1572872 | tf_op jit(solution)/shard_map/ppermute | solution.py:280
  35.8 15.9 %collective-permute-start.5 = (bf16[512,512]{1,0:T(8,128)(2,1)}, bf16[512,512]{1,0:T(8,128)(2,1)S(1)}, u32[]{:S(2)}, u32[]{:S(2)}) collective-permute-start(bf16[512,512]{1,0:T(8,128)(2,1)} %collective-permute-done.1.refs_3_), channel_id=1, source_target_pairs={{1,2},{2,3},{5,6},{6,7},{9,10},{10,11},{13,14},{14,15},{17,18},{18... | collective-permute-start | bytes 1572872 | tf_op jit(solution)/shard_map/ppermute | solution.py:282
  36.5 21.1 %collective-permute-start.7 = (bf16[512,512]{1,0:T(8,128)(2,1)}, bf16[512,512]{1,0:T(8,128)(2,1)S(1)}, u32[]{:S(2)}, u32[]{:S(2)}) collective-permute-start(bf16[512,512]{1,0:T(8,128)(2,1)} %collective-permute-done.3.refs_5_), channel_id=1, source_target_pairs={{2,1},{1,0},{6,5},{5,4},{10,9},{9,8},{14,13},{13,12},{18,17},{17,1... | collective-permute-start | bytes 1572872 | tf_op jit(solution)/shard_map/ppermute | solution.py:282
  47.0 4.2 %copy-start.8 = (bf16[512,4096]{1,0:T(8,128)(2,1)S(1)}, bf16[512,4096]{1,0:T(8,128)(2,1)}, u32[]{:S(2)}) copy-start(bf16[512,4096]{1,0:T(8,128)(2,1)} %tokens_ref.1) | copy-start | bytes 12582916
  47.0 13.3 %collective-permute-start.11 = (f32[192,512]{1,0:T(8,128)S(1)}, f32[192,512]{1,0:T(8,128)S(1)}, u32[]{:S(2)}, u32[]{:S(2)}) collective-permute-start(f32[192,512]{1,0:T(8,128)S(1)} %get-tuple-element.18), channel_id=1, source_target_pairs={{0,8},{4,12},{8,0},{12,4},{16,24},{20,28},{24,16},{28,20},{1,9},{5... | collective-permute-start | bytes 1179656 | tf_op jit(solution)/shard_map/ppermute | solution.py:307
  49.6 18.3 %collective-permute-start.12 = (f32[192,512]{1,0:T(8,128)S(1)}, f32[192,512]{1,0:T(8,128)S(1)}, u32[]{:S(2)}, u32[]{:S(2)}) collective-permute-start(f32[192,512]{1,0:T(8,128)S(1)} %get-tuple-element.19), channel_id=1, source_target_pairs={{0,16},{4,20},{8,24},{12,28},{16,0},{20,4},{24,8},{28,12},{1,17},{... | collective-permute-start | bytes 1179656 | tf_op jit(solution)/shard_map/ppermute | solution.py:307
  51.7 17.5 %collective-permute-start.13 = (f32[192,512]{1,0:T(8,128)S(1)}, f32[192,512]{1,0:T(8,128)S(1)}, u32[]{:S(2)}, u32[]{:S(2)}) collective-permute-start(f32[192,512]{1,0:T(8,128)S(1)} %get-tuple-element.20), channel_id=1, source_target_pairs={{0,24},{4,28},{8,16},{12,20},{16,8},{20,12},{24,0},{28,4},{1,25},{... | collective-permute-start | bytes 1179656 | tf_op jit(solution)/shard_map/ppermute | solution.py:307
  57.6 16.7 %collective-permute-start.8 = (bf16[512,512]{1,0:T(8,128)(2,1)S(1)}, bf16[512,512]{1,0:T(8,128)(2,1)S(1)}, u32[]{:S(2)}, u32[]{:S(2)}) collective-permute-start(bf16[512,512]{1,0:T(8,128)(2,1)S(1)} %broadcast_select_fusion.1), channel_id=1, source_target_pairs={{2,3},{1,0},{6,7},{5,4},{10,11},{9,8},{14,15},{13,12},{18,19},{17,... | collective-permute-start | bytes 1572872 | tf_op jit(solution)/shard_map/ppermute | solution.py:280
  58.9 10.3 %copy-start.6 = (f32[192,512]{1,0:T(8,128)S(1)}, f32[192,512]{1,0:T(8,128)}, u32[]{:S(2)}) copy-start(f32[192,512]{1,0:T(8,128)} %params_ref.1) | copy-start | bytes 1179652
  58.9 10.3 %copy-start.7 = (f32[192,512]{1,0:T(8,128)S(1)}, f32[192,512]{1,0:T(8,128)}, u32[]{:S(2)}) copy-start(f32[192,512]{1,0:T(8,128)} %momentum_ref.1) | copy-start | bytes 1179652
  59.0 16.2 %collective-permute-start.21 = (f16[512,512]{1,0:T(8,128)(2,1)S(1)}, f16[512,512]{1,0:T(8,128)(2,1)S(1)}, u32[]{:S(2)}, u32[]{:S(2)}) collective-permute-start(f16[512,512]{1,0:T(8,128)(2,1)S(1)} %fusion.12), channel_id=1, source_target_pairs={{3,2},{2,1},{7,6},{6,5},{11,10},{10,9},{15,14},{14,13},{19,18},{18... | collective-permute-start | bytes 1572872 | tf_op jit(solution)/shard_map/ppermute | solution.py:282
  60.3 17.5 %collective-permute-start.19 = (f16[512,512]{1,0:T(8,128)(2,1)S(1)}, f16[512,512]{1,0:T(8,128)(2,1)S(1)}, u32[]{:S(2)}, u32[]{:S(2)}) collective-permute-start(f16[512,512]{1,0:T(8,128)(2,1)S(1)} %fusion.12), channel_id=1, source_target_pairs={{0,1},{1,2},{4,5},{5,6},{8,9},{9,10},{12,13},{13,14},{16,17},{17,1... | collective-permute-start | bytes 1572872 | tf_op jit(solution)/shard_map/ppermute | solution.py:282
  67.9 26.0 %collective-permute-start.9 = (bf16[512,512]{1,0:T(8,128)(2,1)S(1)}, bf16[512,512]{1,0:T(8,128)(2,1)S(1)}, u32[]{:S(2)}, u32[]{:S(2)}) collective-permute-start(bf16[512,512]{1,0:T(8,128)(2,1)S(1)} %broadcast_select_fusion), channel_id=1, source_target_pairs={{2,3},{1,0},{6,7},{5,4},{10,11},{9,8},{14,15},{13,12},{18,19},{17,... | collective-permute-start | bytes 1572872 | tf_op jit(solution)/shard_map/ppermute | solution.py:280
  70.3 4.9 %copy-start.12 = (f32[192,512]{1,0:T(8,128)S(1)}, f32[192,512]{1,0:T(8,128)}, u32[]{:S(2)}) copy-start(f32[192,512]{1,0:T(8,128)} %get-tuple-element.12) | copy-start | bytes 1179652
  70.3 12.3 %collective-permute-start.16 = (f32[192,512]{1,0:T(8,128)}, f32[192,512]{1,0:T(8,128)S(1)}, u32[]{:S(2)}, u32[]{:S(2)}) collective-permute-start(f32[192,512]{1,0:T(8,128)} %get-tuple-element.12), channel_id=1, source_target_pairs={{0,24},{4,28},{8,16},{12,20},{16,8},{20,12},{24,0},{28,4},{1,25},{... | collective-permute-start | bytes 1179656 | tf_op jit(solution)/shard_map/ppermute | solution.py:307
  74.3 13.5 %collective-permute-start.15 = (f32[192,512]{1,0:T(8,128)}, f32[192,512]{1,0:T(8,128)S(1)}, u32[]{:S(2)}, u32[]{:S(2)}) collective-permute-start(f32[192,512]{1,0:T(8,128)} %get-tuple-element.12), channel_id=1, source_target_pairs={{0,16},{4,20},{8,24},{12,28},{16,0},{20,4},{24,8},{28,12},{1,17},{... | collective-permute-start | bytes 1179656 | tf_op jit(solution)/shard_map/ppermute | solution.py:307
  75.2 14.0 %collective-permute-start.14 = (f32[192,512]{1,0:T(8,128)S(1)}, f32[192,512]{1,0:T(8,128)S(1)}, u32[]{:S(2)}, u32[]{:S(2)}) collective-permute-start(f32[192,512]{1,0:T(8,128)S(1)} %copy-done.12), channel_id=1, source_target_pairs={{0,8},{4,12},{8,0},{12,4},{16,24},{20,28},{24,16},{28,20},{1,9},{5... | collective-permute-start | bytes 1179656 | tf_op jit(solution)/shard_map/ppermute | solution.py:307
  77.9 16.2 %collective-permute-start.26 = (f16[512,512]{1,0:T(8,128)(2,1)S(1)}, f16[512,512]{1,0:T(8,128)(2,1)S(1)}, u32[]{:S(2)}, u32[]{:S(2)}) collective-permute-start(f16[512,512]{1,0:T(8,128)(2,1)S(1)} %fusion.15), channel_id=1, source_target_pairs={{3,2},{2,1},{7,6},{6,5},{11,10},{10,9},{15,14},{14,13},{19,18},{18... | collective-permute-start | bytes 1572872 | tf_op jit(solution)/shard_map/ppermute | solution.py:282
  82.5 13.3 %collective-permute-start.24 = (f16[512,512]{1,0:T(8,128)(2,1)S(1)}, f16[512,512]{1,0:T(8,128)(2,1)S(1)}, u32[]{:S(2)}, u32[]{:S(2)}) collective-permute-start(f16[512,512]{1,0:T(8,128)(2,1)S(1)} %fusion.15), channel_id=1, source_target_pairs={{0,1},{1,2},{4,5},{5,6},{8,9},{9,10},{12,13},{13,14},{16,17},{17,1... | collective-permute-start | bytes 1572872 | tf_op jit(solution)/shard_map/ppermute | solution.py:282
  87.9 29.3 %collective-permute-start.22 = (f16[512,512]{1,0:T(8,128)(2,1)S(1)}, f16[512,512]{1,0:T(8,128)(2,1)S(1)}, u32[]{:S(2)}, u32[]{:S(2)}) collective-permute-start(f16[512,512]{1,0:T(8,128)(2,1)S(1)} %fusion.13), channel_id=1, source_target_pairs={{3,2},{2,1},{1,0},{7,6},{6,5},{5,4},{11,10},{10,9},{9,8},{15,14},{... | collective-permute-start | bytes 1572872 | tf_op jit(solution)/shard_map/ppermute | solution.py:282
  89.2 28.0 %collective-permute-start.20 = (f16[512,512]{1,0:T(8,128)(2,1)S(1)}, f16[512,512]{1,0:T(8,128)(2,1)S(1)}, u32[]{:S(2)}, u32[]{:S(2)}) collective-permute-start(f16[512,512]{1,0:T(8,128)(2,1)S(1)} %fusion.11), channel_id=1, source_target_pairs={{0,1},{1,2},{2,3},{4,5},{5,6},{6,7},{8,9},{9,10},{10,11},{12,13},{... | collective-permute-start | bytes 1572872 | tf_op jit(solution)/shard_map/ppermute | solution.py:282
  93.9 7.0 %collective-permute-start.17 = (f32[4,192,512]{2,1,0:T(8,128)S(1)}, f32[4,192,512]{2,1,0:T(8,128)S(1)}, u32[]{:S(2)}, u32[]{:S(2)}) collective-permute-start(f32[4,192,512]{2,1,0:T(8,128)S(1)} %pad_maximum_fusion.1.mine_ref), channel_id=1, source_target_pairs={{0,4},{4,0},{8,12},{12,8},{16,20},{20,16},{24,28},{28,24},{1,5},{5... | collective-permute-start | bytes 4718600 | tf_op jit(solution)/shard_map/ppermute | solution.py:307
  94.0 7.0 %copy-start.3 = (bf16[192,4096]{1,0:T(8,128)(2,1)S(1)}, bf16[192,4096]{1,0:T(8,128)(2,1)}, u32[]{:S(2)}) copy-start(bf16[192,4096]{1,0:T(8,128)(2,1)} %slab_ref.3) | copy-start | bytes 4718596
  94.6 20.2 %collective-permute-start.27 = (f16[512,512]{1,0:T(8,128)(2,1)S(1)}, f16[512,512]{1,0:T(8,128)(2,1)S(1)}, u32[]{:S(2)}, u32[]{:S(2)}) collective-permute-start(f16[512,512]{1,0:T(8,128)(2,1)S(1)} %fusion.16), channel_id=1, source_target_pairs={{3,2},{2,1},{1,0},{7,6},{6,5},{5,4},{11,10},{10,9},{9,8},{15,14},{... | collective-permute-start | bytes 1572872 | tf_op jit(solution)/shard_map/ppermute | solution.py:282
  96.4 20.3 %collective-permute-start.25 = (f16[512,512]{1,0:T(8,128)(2,1)S(1)}, f16[512,512]{1,0:T(8,128)(2,1)S(1)}, u32[]{:S(2)}, u32[]{:S(2)}) collective-permute-start(f16[512,512]{1,0:T(8,128)(2,1)S(1)} %fusion.14), channel_id=1, source_target_pairs={{0,1},{1,2},{2,3},{4,5},{5,6},{6,7},{8,9},{9,10},{10,11},{12,13},{... | collective-permute-start | bytes 1572872 | tf_op jit(solution)/shard_map/ppermute | solution.py:282
  103.1 1.4 %copy-start.9 = (bf16[192,4096]{1,0:T(8,128)(2,1)S(1)}, bf16[192,4096]{1,0:T(8,128)(2,1)}, u32[]{:S(2)}) copy-start(bf16[192,4096]{1,0:T(8,128)(2,1)} %shard_map.147.refs_12_) | copy-start | bytes 4718596
  110.7 1.0 copy-start.5
  116.7 1.6 %copy-start.11 = (f32[1024,512]{1,0:T(8,128)S(1)}, f32[1024,512]{1,0:T(8,128)}, u32[]{:S(2)}) copy-start(f32[1024,512]{1,0:T(8,128)} %param.12) | copy-start | bytes 6291460
  117.2 1.8 %copy-start.10 = (f32[1024,512]{1,0:T(8,128)S(1)}, f32[1024,512]{1,0:T(8,128)}, u32[]{:S(2)}) copy-start(f32[1024,512]{1,0:T(8,128)} %param.11) | copy-start | bytes 6291460

commit v5 on v4

--- a/solution.py
+++ b/solution.py
@@ -306,7 +306,7 @@
     def swap(array, k):
         return lax.ppermute(array, "replica", [(i, i ^ k) for i in range(replicas)])
 
-    keep, send = split_blocks(local_slab, place, replicas)
+    keep, send = split_blocks(local_slab, place, replicas, held[0][0][0])
     pairs = pair_sums(keep, swap(send, 1), place)
     parts = [pairs[0]] + [swap(pairs[j], 2 * j) for j in range(1, replicas // 2)]
     new_outer, new_momentum = outer_update(parts, outer_params, outer_momentum, replicas)

time: 124 us -> 136 us (1.097)
  waiting for transfers between devices: 30.6 us -> 39.6 us
  starting transfers between devices: 59.5 us -> 64.6 us
  Pallas kernels: 12.7 us -> 10.4 us
  matrix products: 6.99 us -> 8.82 us
    ppermute x4, waiting for transfers between devices: 2.48 us -> 8.47 us  [exchange(): come = lax.ppermute(load, 'fsdp', up + down)]
    ppermute x8, waiting for transfers between devices: 20.1 us -> 14.4 us  [exchange(): lax.ppermute(down_load, 'fsdp', down)]
    ppermute x8, waiting for transfers between devices: 6.14 us -> 11.5 us  [swap(): return lax.ppermute(array, 'replica', [(i, i ^ k) for i in range(replicas)])]
    ppermute x8, starting transfers between devices: 32.6 us -> 36.8 us  [exchange(): lax.ppermute(up_load, 'fsdp', up)]
    ppermute x8, waiting for transfers between devices: 1.89 us -> 5.21 us  [exchange(): lax.ppermute(up_load, 'fsdp', up)]
    dot_general x10, matrix products: 6.99 us -> 8.82 us  [term(): lax.dot_general(columns, cotangent, (((0,), (0,)), ((), ())), preferred_e...]
    unnamed x26 -> x24, local copies, waits for them, and re-layouts: 6.43 us -> 5.34 us
  transfers between devices with their start and end apart: 28 -> 28, of which waited for: 10 -> 9; matrix products, arithmetic and copies ran while one was open for 7% -> 7% of each run, Pallas kernels for 10% -> 8%
where the time goes in v5:
time: 136 us; the launch traced here: 135 us
  starting transfers between devices  64.6 us (47%)
  waiting for transfers between devices  39.6 us (29%)
  Pallas kernels  10.4 us (8%)
  matrix products  8.82 us (6%)
  local copies, waits for them, and re-layouts  5.53 us (4%)
  other arithmetic  5.12 us (4%)
    ppermute x8, starting transfers between devices, exchange(): lax.ppermute(up_load, 'fsdp', up)  36.8 us
    ppermute x8, waiting for transfers between devices, exchange(): lax.ppermute(down_load, 'fsdp', down)  14.4 us
    ppermute x8, waiting for transfers between devices, swap(): return lax.ppermute(array, 'replica', [(i, i ^ k) for i in range(replicas)])  11.5 us
    ppermute x4, starting transfers between devices, exchange(): come = lax.ppermute(load, 'fsdp', up + down)  9.55 us
    ppermute x8, starting transfers between devices, swap(): return lax.ppermute(array, 'replica', [(i, i ^ k) for i in range(replicas)])  9.15 us
    ppermute x8, starting transfers between devices, exchange(): lax.ppermute(down_load, 'fsdp', down)  9.11 us
    dot_general x10, matrix products, term(): lax.dot_general(columns, cotangent, (((0,), (0,)), ((), ())), preferred_e...  8.82 us
    ppermute x4, waiting for transfers between devices, exchange(): come = lax.ppermute(load, 'fsdp', up + down)  8.47 us
  transfers between devices with their start and end apart: 28, of which 9 were waited for; matrix products, arithmetic and copies ran while one was open for 7% of the time, Pallas kernels for 8%

profile of v5, /device:TPU:0, one launch (start us, length us, event | category | flops | bytes accessed | tf_op | source)
XLA Modules:
  0.0 135.2 jit_solution(5508605355662573669)
XLA Ops:
  0.6 1.2 copy-done
  1.9 5.1 %collective-permute-start = (bf16[512,512]{1,0:T(8,128)(2,1)S(1)}, bf16[512,512]{1,0:T(8,128)(2,1)S(1)}, u32[]{:S(2)}, u32[]{:S(2)}) collective-permute-start(bf16[512,512]{1,0:T(8,128)(2,1)S(1)} %shard_map.135.refs_0_), channel_id=1, source_target_pairs={{0,1},{1,2},{2,3},{4,5},{5,6},{6,7},{8,9},{9,10},{10,11},{12,13},{... | collective-permute-start | bytes 1572872 | tf_op jit(solution)/shard_map/ppermute | solution.py:282
  7.0 1.3 collective-permute-start.2
  8.3 0.8 shard_map.136.refs_1_
  9.1 5.3 %collective-permute-start.1 = (bf16[512,512]{1,0:T(8,128)(2,1)}, bf16[512,512]{1,0:T(8,128)(2,1)}, u32[]{:S(2)}, u32[]{:S(2)}) collective-permute-start(bf16[512,512]{1,0:T(8,128)(2,1)} %shard_map.136.refs_1_), channel_id=1, source_target_pairs={{0,1},{1,2},{2,3},{4,5},{5,6},{6,7},{8,9},{9,10},{10,11},{12,13},{... | collective-permute-start | bytes 1572872 | tf_op jit(solution)/shard_map/ppermute | solution.py:282
  14.5 1.3 collective-permute-start.3
  15.8 3.5 %collective-permute-done.refs_0_.refs_2_ = bf16[512,512]{1,0:T(8,128)(2,1)S(1)} collective-permute-done((bf16[512,512]{1,0:T(8,128)(2,1)S(1)}, bf16[512,512]{1,0:T(8,128)(2,1)S(1)}, u32[]{:S(2)}, u32[]{:S(2)}) %collective-permute-start) | collective-permute-done | bytes 524320 | tf_op jit(solution)/shard_map/ppermute | solution.py:282
  19.3 1.5 %collective-permute-start.4 = (bf16[512,512]{1,0:T(8,128)(2,1)S(1)}, bf16[512,512]{1,0:T(8,128)(2,1)}, u32[]{:S(2)}, u32[]{:S(2)}) collective-permute-start(bf16[512,512]{1,0:T(8,128)(2,1)S(1)} %collective-permute-done.refs_0_.refs_2_), channel_id=1, source_target_pairs={{1,2},{2,3},{5,6},{6,7},{9,10},{10,11},{13,14},{14,15},{17,18},{18... | collective-permute-start | bytes 1572872 | tf_op jit(solution)/shard_map/ppermute | solution.py:282
  20.7 3.1 %collective-permute-done.2.refs_4_ = bf16[512,512]{1,0:T(8,128)(2,1)} collective-permute-done((bf16[512,512]{1,0:T(8,128)(2,1)S(1)}, bf16[512,512]{1,0:T(8,128)(2,1)}, u32[]{:S(2)}, u32[]{:S(2)}) %collective-permute-start.2) | collective-permute-done | bytes 524320 | tf_op jit(solution)/shard_map/ppermute | solution.py:282
  23.8 1.3 collective-permute-start.6
  25.1 2.3 %fusion.17 = f16[512,512]{1,0:T(8,128)(2,1)} fusion(bf16[512,512]{1,0:T(8,128)(2,1)S(1)} %copy-done.3, bf16[512,4096]{1,0:T(8,128)(2,1)} %tokens_ref.1, s32[]{:T(128)S(6)} %select_n.61), kind=kOutput, calls=%fused_computation.33 | convolution fusion | flops 268959744 | bytes 1572868 | tf_op jit(solution)/shard_map/dot_general | solution.py:302
  27.5 5.7 %collective-permute-start.18 = (f16[512,512]{1,0:T(8,128)(2,1)}, f16[512,512]{1,0:T(8,128)(2,1)}, u32[]{:S(2)}, u32[]{:S(2)}) collective-permute-start(f16[512,512]{1,0:T(8,128)(2,1)} %fusion.17), channel_id=1, source_target_pairs={{0,1},{3,2},{4,5},{7,6},{8,9},{11,10},{12,13},{15,14},{16,17},{19,... | collective-permute-start | bytes 1572872 | tf_op jit(solution)/shard_map/ppermute | solution.py:280
  33.3 1.5 %fusion.18 = f16[512,512]{1,0:T(8,128)(2,1)S(1)} fusion(bf16[512,512]{1,0:T(8,128)(2,1)S(1)} %copy-done.3, bf16[512,4096]{1,0:T(8,128)(2,1)} %tokens_ref.1, s32[]{:T(128)S(6)} %select_n.66), kind=kOutput, calls=%fused_computation.34 | convolution fusion | flops 268959744 | bytes 1572868 | tf_op jit(solution)/shard_map/dot_general | solution.py:302
  35.2 1.3 collective-permute-start.23
  36.7 0.8 collective-permute-start.5
  37.5 7.3 %collective-permute-done.6.refs_2_.refs_8_ = bf16[512,512]{1,0:T(8,128)(2,1)} collective-permute-done((bf16[512,512]{1,0:T(8,128)(2,1)}, bf16[512,512]{1,0:T(8,128)(2,1)}, u32[]{:S(2)}, u32[]{:S(2)}) %collective-permute-start.6) | collective-permute-done | bytes 524320 | tf_op jit(solution)/shard_map/ppermute | solution.py:282
  44.9 1.3 collective-permute-start.7
  46.2 1.6 %fusion.12 = f16[512,512]{1,0:T(8,128)(2,1)S(1)} fusion(bf16[512,512]{1,0:T(8,128)(2,1)S(1)} %shard_map.141.refs_0_, f16[512,512]{1,0:T(8,128)(2,1)} %collective-permute-done.18, bf16[512,4096]{1,0:T(8,128)(2,1)S(1)} %copy-done.7, s32[]{:T(128)S(6)} %select_n.59), kind=kOutput, calls=%fused_computation.28 | convolution fusion | flops 269484032 | bytes 2097156 | tf_op jit(solution)/shard_map/dot_general | solution.py:302
  47.7 0.7 collective-permute-start.21
  48.4 1.1 broadcast_select_fusion.1
  49.6 9.6 %collective-permute-start.19 = (f16[512,512]{1,0:T(8,128)(2,1)S(1)}, f16[512,512]{1,0:T(8,128)(2,1)S(1)}, u32[]{:S(2)}, u32[]{:S(2)}) collective-permute-start(f16[512,512]{1,0:T(8,128)(2,1)S(1)} %fusion.12), channel_id=1, source_target_pairs={{0,1},{1,2},{4,5},{5,6},{8,9},{9,10},{12,13},{13,14},{16,17},{17,1... | collective-permute-start | bytes 1572872 | tf_op jit(solution)/shard_map/ppermute | solution.py:282
  59.6 1.3 collective-permute-start.8
  61.7 1.6 %collective-permute-start.11 = (f32[192,512]{1,0:T(8,128)S(1)}, f32[192,512]{1,0:T(8,128)S(1)}, u32[]{:S(2)}, u32[]{:S(2)}) collective-permute-start(f32[192,512]{1,0:T(8,128)S(1)} %get-tuple-element.18), channel_id=1, source_target_pairs={{0,8},{4,12},{8,0},{12,4},{16,24},{20,28},{24,16},{28,20},{1,9},{5... | collective-permute-start | bytes 1179656 | tf_op jit(solution)/shard_map/ppermute | solution.py:307
  63.2 1.5 %collective-permute-start.12 = (f32[192,512]{1,0:T(8,128)S(1)}, f32[192,512]{1,0:T(8,128)S(1)}, u32[]{:S(2)}, u32[]{:S(2)}) collective-permute-start(f32[192,512]{1,0:T(8,128)S(1)} %get-tuple-element.19), channel_id=1, source_target_pairs={{0,16},{4,20},{8,24},{12,28},{16,0},{20,4},{24,8},{28,12},{1,17},{... | collective-permute-start | bytes 1179656 | tf_op jit(solution)/shard_map/ppermute | solution.py:307
  64.7 8.5 %collective-permute-done.8.refs_1_.refs_2_.refs_10_ = bf16[512,512]{1,0:T(8,128)(2,1)S(1)} collective-permute-done((bf16[512,512]{1,0:T(8,128)(2,1)S(1)}, bf16[512,512]{1,0:T(8,128)(2,1)S(1)}, u32[]{:S(2)}, u32[]{:S(2)}) %collective-permute-start.8) | collective-permute-done | bytes 524320 | tf_op jit(solution)/shard_map/ppermute | solution.py:280
  73.2 2.4 %collective-permute-start.13 = (f32[192,512]{1,0:T(8,128)S(1)}, f32[192,512]{1,0:T(8,128)S(1)}, u32[]{:S(2)}, u32[]{:S(2)}) collective-permute-start(f32[192,512]{1,0:T(8,128)S(1)} %get-tuple-element.20), channel_id=1, source_target_pairs={{0,24},{4,28},{8,16},{12,20},{16,8},{20,12},{24,0},{28,4},{1,25},{... | collective-permute-start | bytes 1179656 | tf_op jit(solution)/shard_map/ppermute | solution.py:307
  75.7 1.3 collective-permute-start.9
  77.0 5.8 %collective-permute-done.13.refs_3_ = f32[192,512]{1,0:T(8,128)S(1)} collective-permute-done((f32[192,512]{1,0:T(8,128)S(1)}, f32[192,512]{1,0:T(8,128)S(1)}, u32[]{:S(2)}, u32[]{:S(2)}) %collective-permute-start.13) | collective-permute-done | bytes 393248 | tf_op jit(solution)/shard_map/ppermute | solution.py:307
  82.8 1.0 shard_map.139
  83.8 2.5 %collective-permute-start.16 = (f32[192,512]{1,0:T(8,128)}, f32[192,512]{1,0:T(8,128)S(1)}, u32[]{:S(2)}, u32[]{:S(2)}) collective-permute-start(f32[192,512]{1,0:T(8,128)} %get-tuple-element.12), channel_id=1, source_target_pairs={{0,24},{4,28},{8,16},{12,20},{16,8},{20,12},{24,0},{28,4},{1,25},{... | collective-permute-start | bytes 1179656 | tf_op jit(solution)/shard_map/ppermute | solution.py:307
  86.3 0.5 collective-permute-start.15
  87.8 0.7 collective-permute-start.26
  88.5 0.5 fusion.11
  89.0 5.7 %collective-permute-done.16.refs_0_ = f32[192,512]{1,0:T(8,128)S(1)} collective-permute-done((f32[192,512]{1,0:T(8,128)}, f32[192,512]{1,0:T(8,128)S(1)}, u32[]{:S(2)}, u32[]{:S(2)}) %collective-permute-start.16) | collective-permute-done | bytes 393248 | tf_op jit(solution)/shard_map/ppermute | solution.py:307
  94.7 5.0 %collective-permute-start.24 = (f16[512,512]{1,0:T(8,128)(2,1)S(1)}, f16[512,512]{1,0:T(8,128)(2,1)S(1)}, u32[]{:S(2)}, u32[]{:S(2)}) collective-permute-start(f16[512,512]{1,0:T(8,128)(2,1)S(1)} %fusion.15), channel_id=1, source_target_pairs={{0,1},{1,2},{4,5},{5,6},{8,9},{9,10},{12,13},{13,14},{16,17},{17,1... | collective-permute-start | bytes 1572872 | tf_op jit(solution)/shard_map/ppermute | solution.py:282
  99.7 1.3 collective-permute-start.22
  101.0 4.9 %collective-permute-start.20 = (f16[512,512]{1,0:T(8,128)(2,1)S(1)}, f16[512,512]{1,0:T(8,128)(2,1)S(1)}, u32[]{:S(2)}, u32[]{:S(2)}) collective-permute-start(f16[512,512]{1,0:T(8,128)(2,1)S(1)} %fusion.11), channel_id=1, source_target_pairs={{0,1},{1,2},{2,3},{4,5},{5,6},{6,7},{8,9},{9,10},{10,11},{12,13},{... | collective-permute-start | bytes 1572872 | tf_op jit(solution)/shard_map/ppermute | solution.py:282
  106.6 1.3 collective-permute-start.27
  108.5 4.6 %collective-permute-start.25 = (f16[512,512]{1,0:T(8,128)(2,1)S(1)}, f16[512,512]{1,0:T(8,128)(2,1)S(1)}, u32[]{:S(2)}, u32[]{:S(2)}) collective-permute-start(f16[512,512]{1,0:T(8,128)(2,1)S(1)} %fusion.14), channel_id=1, source_target_pairs={{0,1},{1,2},{2,3},{4,5},{5,6},{6,7},{8,9},{9,10},{10,11},{12,13},{... | collective-permute-start | bytes 1572872 | tf_op jit(solution)/shard_map/ppermute | solution.py:282
  113.1 2.1 %shard_map.147.refs_12_ = bf16[192,4096]{1,0:T(8,128)(2,1)} custom-call(s32[1]{0:T(128)} %bitcast.12.place_ref, bf16[192,4096]{1,0:T(8,128)(2,1)S(1)} %copy-done.2, f32[4,192,512]{2,1,0:T(8,128)S(1)} %pad_maximum_fusion.1.mine_ref, f32[4,192,512]{2,1,0:T(8,128)S(1)} %collective-permute-done.17.theirs_ref), custom_call_target="tpu_custom_call" | custom-call | flops 3000000000 | tf_op jit(solution)/shard_map/pallas_call | solution.py:236
  115.2 1.4 %copy-done.8 = bf16[192,4096]{1,0:T(8,128)(2,1)S(1)} copy-done((bf16[192,4096]{1,0:T(8,128)(2,1)S(1)}, bf16[192,4096]{1,0:T(8,128)(2,1)}, u32[]{:S(2)}) %copy-start.8) | copy-done | bytes 1572888
  116.6 5.9 %shard_map.148.refs_1_ = bf16[512,512]{1,0:T(8,128)(2,1)} custom-call(s32[6]{0:T(128)S(1)} %broadcast_clamp_fusion.owners_ref, s32[6]{0:T(128)S(1)} %convert_element_type.63.valid_ref, bf16[512,4096]{1,0:T(8,128)(2,1)S(1)} %copy-done.7, bf16[512,512]{1,0:T(8,128)(2,1)S(1)} %shard_map.135.refs_0_, bf16[512,512]{1,0:T(8,128)(2,1)} %shard_map.136.refs_1_, ...), custom_call_target="tpu_custom_call" | custom-call | flops 6000000000 | tf_op jit(solution)/shard_map/pallas_call | solution.py:115
  122.5 1.0 copy-done.4
  123.5 3.6 %collective-permute-done.27 = f16[512,512]{1,0:T(8,128)(2,1)S(1)} collective-permute-done((f16[512,512]{1,0:T(8,128)(2,1)S(1)}, f16[512,512]{1,0:T(8,128)(2,1)S(1)}, u32[]{:S(2)}, u32[]{:S(2)}) %collective-permute-start.27) | collective-permute-done | bytes 524320 | tf_op jit(solution)/shard_map/ppermute | solution.py:282
  127.1 1.7 %collective-permute-done.25 = f16[512,512]{1,0:T(8,128)(2,1)S(1)} collective-permute-done((f16[512,512]{1,0:T(8,128)(2,1)S(1)}, f16[512,512]{1,0:T(8,128)(2,1)S(1)}, u32[]{:S(2)}, u32[]{:S(2)}) %collective-permute-start.25) | collective-permute-done | bytes 524320 | tf_op jit(solution)/shard_map/ppermute | solution.py:282
  129.8 0.6 copy-done.10
  130.7 0.7 copy-done.9
  131.4 3.8 %fusion.2 = (bf16[1024,512]{1,0:T(8,128)(2,1)}, f32[1024,512]{1,0:T(8,128)}, f32[1024,512]{1,0:T(8,128)}) fusion(bf16[1024,512]{1,0:T(8,128)(2,1)S(1)} %copy-done.1, f32[512,512]{1,0:T(8,128)S(1)} %fusion.6, f32[512,512]{1,0:T(8,128)S(1)} %fusion.10, f32[1024,512]{1,0:T(8,128)S(1)} %copy-done.9, f32[1024,512]{1,0:T(8,128)S(1)} %copy-done.10), kind=kLoop, calls=%fused_computation.4 | loop fusion | flops 9961472 | bytes 12582912 | tf_op jit(solution)/shard_map/convert_element_type | solution.py:366
  (66 shorter events, 5.4 us)
Async XLA Ops:
  0.6 1.2 copy-start
  1.9 23.3 %copy-start.3 = (bf16[512,512]{1,0:T(8,128)(2,1)S(1)}, bf16[512,512]{1,0:T(8,128)(2,1)}, u32[]{:S(2)}) copy-start(bf16[512,512]{1,0:T(8,128)(2,1)} %in_ref.5) | copy-start | bytes 1572868
  1.9 17.4 %collective-permute-start = (bf16[512,512]{1,0:T(8,128)(2,1)S(1)}, bf16[512,512]{1,0:T(8,128)(2,1)S(1)}, u32[]{:S(2)}, u32[]{:S(2)}) collective-permute-start(bf16[512,512]{1,0:T(8,128)(2,1)S(1)} %shard_map.135.refs_0_), channel_id=1, source_target_pairs={{0,1},{1,2},{2,3},{4,5},{5,6},{6,7},{8,9},{9,10},{10,11},{12,13},{... | collective-permute-start | bytes 1572872 | tf_op jit(solution)/shard_map/ppermute | solution.py:282
  7.0 16.8 %collective-permute-start.2 = (bf16[512,512]{1,0:T(8,128)(2,1)S(1)}, bf16[512,512]{1,0:T(8,128)(2,1)}, u32[]{:S(2)}, u32[]{:S(2)}) collective-permute-start(bf16[512,512]{1,0:T(8,128)(2,1)S(1)} %shard_map.135.refs_0_), channel_id=1, source_target_pairs={{3,2},{2,1},{1,0},{7,6},{6,5},{5,4},{11,10},{10,9},{9,8},{15,14},{... | collective-permute-start | bytes 1572872 | tf_op jit(solution)/shard_map/ppermute | solution.py:282
  9.1 26.1 %collective-permute-start.1 = (bf16[512,512]{1,0:T(8,128)(2,1)}, bf16[512,512]{1,0:T(8,128)(2,1)}, u32[]{:S(2)}, u32[]{:S(2)}) collective-permute-start(bf16[512,512]{1,0:T(8,128)(2,1)} %shard_map.136.refs_1_), channel_id=1, source_target_pairs={{0,1},{1,2},{2,3},{4,5},{5,6},{6,7},{8,9},{9,10},{10,11},{12,13},{... | collective-permute-start | bytes 1572872 | tf_op jit(solution)/shard_map/ppermute | solution.py:282
  14.5 22.1 %collective-permute-start.3 = (bf16[512,512]{1,0:T(8,128)(2,1)}, bf16[512,512]{1,0:T(8,128)(2,1)}, u32[]{:S(2)}, u32[]{:S(2)}) collective-permute-start(bf16[512,512]{1,0:T(8,128)(2,1)} %shard_map.136.refs_1_), channel_id=1, source_target_pairs={{3,2},{2,1},{1,0},{7,6},{6,5},{5,4},{11,10},{10,9},{9,8},{15,14},{... | collective-permute-start | bytes 1572872 | tf_op jit(solution)/shard_map/ppermute | solution.py:282
  19.3 17.4 %collective-permute-start.4 = (bf16[512,512]{1,0:T(8,128)(2,1)S(1)}, bf16[512,512]{1,0:T(8,128)(2,1)}, u32[]{:S(2)}, u32[]{:S(2)}) collective-permute-start(bf16[512,512]{1,0:T(8,128)(2,1)S(1)} %collective-permute-done.refs_0_.refs_2_), channel_id=1, source_target_pairs={{1,2},{2,3},{5,6},{6,7},{9,10},{10,11},{13,14},{14,15},{17,18},{18... | collective-permute-start | bytes 1572872 | tf_op jit(solution)/shard_map/ppermute | solution.py:282
  23.8 21.0 %collective-permute-start.6 = (bf16[512,512]{1,0:T(8,128)(2,1)}, bf16[512,512]{1,0:T(8,128)(2,1)}, u32[]{:S(2)}, u32[]{:S(2)}) collective-permute-start(bf16[512,512]{1,0:T(8,128)(2,1)} %collective-permute-done.2.refs_4_), channel_id=1, source_target_pairs={{2,1},{1,0},{6,5},{5,4},{10,9},{9,8},{14,13},{13,12},{18,17},{17,1... | collective-permute-start | bytes 1572872 | tf_op jit(solution)/shard_map/ppermute | solution.py:282
  27.5 7.4 %copy-start.2 = (bf16[192,4096]{1,0:T(8,128)(2,1)S(1)}, bf16[192,4096]{1,0:T(8,128)(2,1)}, u32[]{:S(2)}) copy-start(bf16[192,4096]{1,0:T(8,128)(2,1)} %slab_ref.3) | copy-start | bytes 4718596
  27.5 18.7 %collective-permute-start.18 = (f16[512,512]{1,0:T(8,128)(2,1)}, f16[512,512]{1,0:T(8,128)(2,1)}, u32[]{:S(2)}, u32[]{:S(2)}) collective-permute-start(f16[512,512]{1,0:T(8,128)(2,1)} %fusion.17), channel_id=1, source_target_pairs={{0,1},{3,2},{4,5},{7,6},{8,9},{11,10},{12,13},{15,14},{16,17},{19,... | collective-permute-start | bytes 1572872 | tf_op jit(solution)/shard_map/ppermute | solution.py:280
  35.2 25.7 %collective-permute-start.23 = (f16[512,512]{1,0:T(8,128)(2,1)S(1)}, f16[512,512]{1,0:T(8,128)(2,1)S(1)}, u32[]{:S(2)}, u32[]{:S(2)}) collective-permute-start(f16[512,512]{1,0:T(8,128)(2,1)S(1)} %fusion.18), channel_id=1, source_target_pairs={{0,1},{3,2},{4,5},{7,6},{8,9},{11,10},{12,13},{15,14},{16,17},{19,... | collective-permute-start | bytes 1572872 | tf_op jit(solution)/shard_map/ppermute | solution.py:280
  36.6 9.6 %copy-start.7 = (bf16[512,4096]{1,0:T(8,128)(2,1)S(1)}, bf16[512,4096]{1,0:T(8,128)(2,1)}, u32[]{:S(2)}) copy-start(bf16[512,4096]{1,0:T(8,128)(2,1)} %tokens_ref.1) | copy-start | bytes 12582916
  36.6 24.9 %collective-permute-start.10 = (bf16[4,192,512]{2,1,0:T(8,128)(2,1)S(1)}, bf16[4,192,512]{2,1,0:T(8,128)(2,1)S(1)}, u32[]{:S(2)}, u32[]{:S(2)}) collective-permute-start(bf16[4,192,512]{2,1,0:T(8,128)(2,1)S(1)} %get-tuple-element.16), channel_id=1, source_target_pairs={{0,4},{4,0},{8,12},{12,8},{16,20},{20,16},{24,28},{28,24},{1,5},{5... | collective-permute-start | bytes 2359304 | tf_op jit(solution)/shard_map/ppermute | solution.py:307
  36.7 12.9 %collective-permute-start.5 = (bf16[512,512]{1,0:T(8,128)(2,1)}, bf16[512,512]{1,0:T(8,128)(2,1)S(1)}, u32[]{:S(2)}, u32[]{:S(2)}) collective-permute-start(bf16[512,512]{1,0:T(8,128)(2,1)} %collective-permute-done.1.refs_3_), channel_id=1, source_target_pairs={{1,2},{2,3},{5,6},{6,7},{9,10},{10,11},{13,14},{14,15},{17,18},{18... | collective-permute-start | bytes 1572872 | tf_op jit(solution)/shard_map/ppermute | solution.py:282
  44.9 14.7 %collective-permute-start.7 = (bf16[512,512]{1,0:T(8,128)(2,1)}, bf16[512,512]{1,0:T(8,128)(2,1)S(1)}, u32[]{:S(2)}, u32[]{:S(2)}) collective-permute-start(bf16[512,512]{1,0:T(8,128)(2,1)} %collective-permute-done.3.refs_5_), channel_id=1, source_target_pairs={{2,1},{1,0},{6,5},{5,4},{10,9},{9,8},{14,13},{13,12},{18,17},{17,1... | collective-permute-start | bytes 1572872 | tf_op jit(solution)/shard_map/ppermute | solution.py:282
  47.7 39.0 %collective-permute-start.21 = (f16[512,512]{1,0:T(8,128)(2,1)S(1)}, f16[512,512]{1,0:T(8,128)(2,1)S(1)}, u32[]{:S(2)}, u32[]{:S(2)}) collective-permute-start(f16[512,512]{1,0:T(8,128)(2,1)S(1)} %fusion.12), channel_id=1, source_target_pairs={{3,2},{2,1},{7,6},{6,5},{11,10},{10,9},{15,14},{14,13},{19,18},{18... | collective-permute-start | bytes 1572872 | tf_op jit(solution)/shard_map/ppermute | solution.py:282
  49.6 38.2 %collective-permute-start.19 = (f16[512,512]{1,0:T(8,128)(2,1)S(1)}, f16[512,512]{1,0:T(8,128)(2,1)S(1)}, u32[]{:S(2)}, u32[]{:S(2)}) collective-permute-start(f16[512,512]{1,0:T(8,128)(2,1)S(1)} %fusion.12), channel_id=1, source_target_pairs={{0,1},{1,2},{4,5},{5,6},{8,9},{9,10},{12,13},{13,14},{16,17},{17,1... | collective-permute-start | bytes 1572872 | tf_op jit(solution)/shard_map/ppermute | solution.py:282
  59.6 13.6 %collective-permute-start.8 = (bf16[512,512]{1,0:T(8,128)(2,1)S(1)}, bf16[512,512]{1,0:T(8,128)(2,1)S(1)}, u32[]{:S(2)}, u32[]{:S(2)}) collective-permute-start(bf16[512,512]{1,0:T(8,128)(2,1)S(1)} %broadcast_select_fusion.1), channel_id=1, source_target_pairs={{2,3},{1,0},{6,7},{5,4},{10,11},{9,8},{14,15},{13,12},{18,19},{17,... | collective-permute-start | bytes 1572872 | tf_op jit(solution)/shard_map/ppermute | solution.py:280
  61.7 14.0 %collective-permute-start.11 = (f32[192,512]{1,0:T(8,128)S(1)}, f32[192,512]{1,0:T(8,128)S(1)}, u32[]{:S(2)}, u32[]{:S(2)}) collective-permute-start(f32[192,512]{1,0:T(8,128)S(1)} %get-tuple-element.18), channel_id=1, source_target_pairs={{0,8},{4,12},{8,0},{12,4},{16,24},{20,28},{24,16},{28,20},{1,9},{5... | collective-permute-start | bytes 1179656 | tf_op jit(solution)/shard_map/ppermute | solution.py:307
  63.2 13.7 %collective-permute-start.12 = (f32[192,512]{1,0:T(8,128)S(1)}, f32[192,512]{1,0:T(8,128)S(1)}, u32[]{:S(2)}, u32[]{:S(2)}) collective-permute-start(f32[192,512]{1,0:T(8,128)S(1)} %get-tuple-element.19), channel_id=1, source_target_pairs={{0,16},{4,20},{8,24},{12,28},{16,0},{20,4},{24,8},{28,12},{1,17},{... | collective-permute-start | bytes 1179656 | tf_op jit(solution)/shard_map/ppermute | solution.py:307
  73.2 9.6 %copy-start.5 = (f32[192,512]{1,0:T(8,128)S(1)}, f32[192,512]{1,0:T(8,128)}, u32[]{:S(2)}) copy-start(f32[192,512]{1,0:T(8,128)} %params_ref.1) | copy-start | bytes 1179652
  73.2 9.6 %copy-start.6 = (f32[192,512]{1,0:T(8,128)S(1)}, f32[192,512]{1,0:T(8,128)}, u32[]{:S(2)}) copy-start(f32[192,512]{1,0:T(8,128)} %momentum_ref.1) | copy-start | bytes 1179652
  73.2 9.6 %collective-permute-start.13 = (f32[192,512]{1,0:T(8,128)S(1)}, f32[192,512]{1,0:T(8,128)S(1)}, u32[]{:S(2)}, u32[]{:S(2)}) collective-permute-start(f32[192,512]{1,0:T(8,128)S(1)} %get-tuple-element.20), channel_id=1, source_target_pairs={{0,24},{4,28},{8,16},{12,20},{16,8},{20,12},{24,0},{28,4},{1,25},{... | collective-permute-start | bytes 1179656 | tf_op jit(solution)/shard_map/ppermute | solution.py:307
  75.7 30.4 %collective-permute-start.9 = (bf16[512,512]{1,0:T(8,128)(2,1)S(1)}, bf16[512,512]{1,0:T(8,128)(2,1)S(1)}, u32[]{:S(2)}, u32[]{:S(2)}) collective-permute-start(bf16[512,512]{1,0:T(8,128)(2,1)S(1)} %broadcast_select_fusion), channel_id=1, source_target_pairs={{2,3},{1,0},{6,7},{5,4},{10,11},{9,8},{14,15},{13,12},{18,19},{17,... | collective-permute-start | bytes 1572872 | tf_op jit(solution)/shard_map/ppermute | solution.py:280
  83.8 10.9 %collective-permute-start.16 = (f32[192,512]{1,0:T(8,128)}, f32[192,512]{1,0:T(8,128)S(1)}, u32[]{:S(2)}, u32[]{:S(2)}) collective-permute-start(f32[192,512]{1,0:T(8,128)} %get-tuple-element.12), channel_id=1, source_target_pairs={{0,24},{4,28},{8,16},{12,20},{16,8},{20,12},{24,0},{28,4},{1,25},{... | collective-permute-start | bytes 1179656 | tf_op jit(solution)/shard_map/ppermute | solution.py:307
  86.3 13.4 %collective-permute-start.15 = (f32[192,512]{1,0:T(8,128)}, f32[192,512]{1,0:T(8,128)S(1)}, u32[]{:S(2)}, u32[]{:S(2)}) collective-permute-start(f32[192,512]{1,0:T(8,128)} %get-tuple-element.12), channel_id=1, source_target_pairs={{0,16},{4,20},{8,24},{12,28},{16,0},{20,4},{24,8},{28,12},{1,17},{... | collective-permute-start | bytes 1179656 | tf_op jit(solution)/shard_map/ppermute | solution.py:307
  86.8 14.2 %collective-permute-start.14 = (f32[192,512]{1,0:T(8,128)}, f32[192,512]{1,0:T(8,128)S(1)}, u32[]{:S(2)}, u32[]{:S(2)}) collective-permute-start(f32[192,512]{1,0:T(8,128)} %get-tuple-element.12), channel_id=1, source_target_pairs={{0,8},{4,12},{8,0},{12,4},{16,24},{20,28},{24,16},{28,20},{1,9},{5... | collective-permute-start | bytes 1179656 | tf_op jit(solution)/shard_map/ppermute | solution.py:307
  87.8 18.3 %collective-permute-start.26 = (f16[512,512]{1,0:T(8,128)(2,1)S(1)}, f16[512,512]{1,0:T(8,128)(2,1)S(1)}, u32[]{:S(2)}, u32[]{:S(2)}) collective-permute-start(f16[512,512]{1,0:T(8,128)(2,1)S(1)} %fusion.15), channel_id=1, source_target_pairs={{3,2},{2,1},{7,6},{6,5},{11,10},{10,9},{15,14},{14,13},{19,18},{18... | collective-permute-start | bytes 1572872 | tf_op jit(solution)/shard_map/ppermute | solution.py:282
  89.0 16.9 %copy-start.11 = (f32[192,512]{1,0:T(8,128)S(1)}, f32[192,512]{1,0:T(8,128)}, u32[]{:S(2)}) copy-start(f32[192,512]{1,0:T(8,128)} %get-tuple-element.12) | copy-start | bytes 1179652
  94.7 13.3 %collective-permute-start.24 = (f16[512,512]{1,0:T(8,128)(2,1)S(1)}, f16[512,512]{1,0:T(8,128)(2,1)S(1)}, u32[]{:S(2)}, u32[]{:S(2)}) collective-permute-start(f16[512,512]{1,0:T(8,128)(2,1)S(1)} %fusion.15), channel_id=1, source_target_pairs={{0,1},{1,2},{4,5},{5,6},{8,9},{9,10},{12,13},{13,14},{16,17},{17,1... | collective-permute-start | bytes 1572872 | tf_op jit(solution)/shard_map/ppermute | solution.py:282
  99.7 29.6 %collective-permute-start.22 = (f16[512,512]{1,0:T(8,128)(2,1)S(1)}, f16[512,512]{1,0:T(8,128)(2,1)S(1)}, u32[]{:S(2)}, u32[]{:S(2)}) collective-permute-start(f16[512,512]{1,0:T(8,128)(2,1)S(1)} %fusion.13), channel_id=1, source_target_pairs={{3,2},{2,1},{1,0},{7,6},{6,5},{5,4},{11,10},{10,9},{9,8},{15,14},{... | collective-permute-start | bytes 1572872 | tf_op jit(solution)/shard_map/ppermute | solution.py:282
  101.0 28.3 %collective-permute-start.20 = (f16[512,512]{1,0:T(8,128)(2,1)S(1)}, f16[512,512]{1,0:T(8,128)(2,1)S(1)}, u32[]{:S(2)}, u32[]{:S(2)}) collective-permute-start(f16[512,512]{1,0:T(8,128)(2,1)S(1)} %fusion.11), channel_id=1, source_target_pairs={{0,1},{1,2},{2,3},{4,5},{5,6},{6,7},{8,9},{9,10},{10,11},{12,13},{... | collective-permute-start | bytes 1572872 | tf_op jit(solution)/shard_map/ppermute | solution.py:282
  106.0 7.0 %collective-permute-start.17 = (f32[4,192,512]{2,1,0:T(8,128)S(1)}, f32[4,192,512]{2,1,0:T(8,128)S(1)}, u32[]{:S(2)}, u32[]{:S(2)}) collective-permute-start(f32[4,192,512]{2,1,0:T(8,128)S(1)} %pad_maximum_fusion.1.mine_ref), channel_id=1, source_target_pairs={{0,4},{4,0},{8,12},{12,8},{16,20},{20,16},{24,28},{28,24},{1,5},{5... | collective-permute-start | bytes 4718600 | tf_op jit(solution)/shard_map/ppermute | solution.py:307
  106.6 20.5 %collective-permute-start.27 = (f16[512,512]{1,0:T(8,128)(2,1)S(1)}, f16[512,512]{1,0:T(8,128)(2,1)S(1)}, u32[]{:S(2)}, u32[]{:S(2)}) collective-permute-start(f16[512,512]{1,0:T(8,128)(2,1)S(1)} %fusion.16), channel_id=1, source_target_pairs={{3,2},{2,1},{1,0},{7,6},{6,5},{5,4},{11,10},{10,9},{9,8},{15,14},{... | collective-permute-start | bytes 1572872 | tf_op jit(solution)/shard_map/ppermute | solution.py:282
  108.5 20.3 %collective-permute-start.25 = (f16[512,512]{1,0:T(8,128)(2,1)S(1)}, f16[512,512]{1,0:T(8,128)(2,1)S(1)}, u32[]{:S(2)}, u32[]{:S(2)}) collective-permute-start(f16[512,512]{1,0:T(8,128)(2,1)S(1)} %fusion.14), channel_id=1, source_target_pairs={{0,1},{1,2},{2,3},{4,5},{5,6},{6,7},{8,9},{9,10},{10,11},{12,13},{... | collective-permute-start | bytes 1572872 | tf_op jit(solution)/shard_map/ppermute | solution.py:282
  115.2 1.4 %copy-start.8 = (bf16[192,4096]{1,0:T(8,128)(2,1)S(1)}, bf16[192,4096]{1,0:T(8,128)(2,1)}, u32[]{:S(2)}) copy-start(bf16[192,4096]{1,0:T(8,128)(2,1)} %shard_map.147.refs_12_) | copy-start | bytes 4718596
  122.5 1.0 copy-start.4
  128.8 1.6 %copy-start.10 = (f32[1024,512]{1,0:T(8,128)S(1)}, f32[1024,512]{1,0:T(8,128)}, u32[]{:S(2)}) copy-start(f32[1024,512]{1,0:T(8,128)} %param.12) | copy-start | bytes 6291460
  129.3 1.5 %copy-start.1 = (bf16[1024,512]{1,0:T(8,128)(2,1)S(1)}, bf16[1024,512]{1,0:T(8,128)(2,1)}, u32[]{:S(2)}) copy-start(bf16[1024,512]{1,0:T(8,128)(2,1)} %in_ref.4) | copy-start | bytes 3145732
  129.3 2.2 %copy-start.9 = (f32[1024,512]{1,0:T(8,128)S(1)}, f32[1024,512]{1,0:T(8,128)}, u32[]{:S(2)}) copy-start(f32[1024,512]{1,0:T(8,128)} %param.11) | copy-start | bytes 6291460
